TPU v7x, 512 devices: a whole 4x8x8 slice. The times are simulated.
512 devices in a mesh: dom: 64 (over z, x, core), feat: 8 (over y).
Axes of the slice: x: 4, y: 8, z: 8, core: 2. Of those that a mesh axis runs over, the one named last changes fastest.
Arguments:
- first_layer: bfloat16 [32768, 1024], P('dom', 'feat'), may hold values from -6 to 6
- w_first: bfloat16 [1024, 1024], P('feat', 'dom'), may hold values from -0.1875 to 0.1875
- w_second: bfloat16 [1024, 1024], P('feat', 'dom'), may hold values from -0.1875 to 0.1875
- tile_values: bfloat16 [256, 10, 128, 128], P('dom'), may hold values from -0.15625 to 0.15625
- tile_sources: int32 [64, 4, 10], P('dom'), may hold values from 0 to 35, as said below
- halo_sources: int32 [64, 32], P('dom'), may hold values from 0 to 63, as said below
- send_rows: int32 [64, 64, 128], P('dom'), may hold values from 0 to 512, as said below
- block_counts: int32 [64, 64], P('dom'), may hold values from 0 to 1, as said below
- stale_halo: bfloat16 [262144, 1024], P('dom', 'feat'), may hold values from 0 to 2
Outputs:
- layer_out: bfloat16 [32768, 1024], P('dom', 'feat')
- fresh_halo: bfloat16 [262144, 1024], P('dom', 'feat')
Inputs may be any that keep to these rules, and one draw needn't show every extreme that they name: `tile_sources`: tile 0 of row block i has source i (a local block), tile 1 a local block, the others halo blocks: 4 + j stands for halo block j; every halo block is read by some tile of its partition. `halo_sources`: row p lists 32 distinct partitions other than p, in increasing order. block_counts[q, p] is 1 exactly where q is listed in row p of halo_sources, else 0. `send_rows`: within one block the live rows come first and are distinct rows of the sending partition; the value 512 marks a padding slot.
All inputs are finite; a program needn't handle non-finite values.
Results may differ from a plain program's by a relative error of at most 0.014.
Values may be sent and summed in bfloat16 or wider, within the bound.
No kernel may reach another device: no remote copies, remote signals or barrier semaphores. Data moves between devices by JAX's collectives and lax.ppermute only.
A program may use at most 64 MiB of HBM per device.

v0:
```python
import math

import jax
import jax.numpy as jnp
from jax import lax
from jax.sharding import PartitionSpec as P

alpha_mix = 0.1
beta_first = math.log(1.5)
beta_second = math.log(1.25)


def outgoing(hidden, send_rows, block_counts):
    peers = send_rows.shape[1]
    width = hidden.shape[1]
    padded = jnp.concatenate([hidden, jnp.zeros((1, width), hidden.dtype)], axis=0)
    picked = jnp.take(padded, send_rows[0].reshape(-1), axis=0).reshape(peers, -1, width)
    keep_mask = (block_counts[0] > 0)[:, None, None]
    return jnp.where(keep_mask, picked, jnp.zeros_like(picked))


def compact(arrived, halo_sources):
    width = arrived.shape[2]
    return jnp.take(arrived, halo_sources[0], axis=0).reshape(-1, width)


def aggregate(local_rows, halo_rows, tile_values, tile_sources):
    blocks_here, tile_count, block_rows, _ = tile_values.shape
    width = local_rows.shape[1]
    all_blocks = jnp.concatenate([local_rows, halo_rows], axis=0).reshape(-1, block_rows, width)
    chosen = jnp.take(all_blocks, tile_sources[0].reshape(-1), axis=0)
    chosen = chosen.reshape(blocks_here, tile_count, block_rows, width)
    summed = jnp.einsum("ikrc,ikcd->ird", tile_values, chosen, preferred_element_type=jnp.float32)
    return summed.reshape(-1, width)


def transform(rounded, weight):
    full_rows = lax.all_gather(weight, "dom", axis=1, tiled=True)
    term_sum = jnp.dot(rounded, full_rows, preferred_element_type=jnp.float32)
    term_sum = term_sum.astype(jnp.bfloat16).astype(jnp.float32)
    return lax.psum_scatter(
        term_sum.astype(jnp.bfloat16), "feat", scatter_dimension=1, tiled=True
    ).astype(jnp.float32)


def layer(local_rows, halo_rows, first_rows, tile_values, tile_sources, weight, beta_value):
    aggregated = aggregate(local_rows, halo_rows, tile_values, tile_sources)
    mixture = (1.0 - alpha_mix) * aggregated + alpha_mix * first_rows.astype(jnp.float32)
    rounded = mixture.astype(jnp.bfloat16)
    turned = transform(rounded, weight)
    return jax.nn.relu((1.0 - beta_value) * mixture + beta_value * turned).astype(jnp.bfloat16)


def shards(
    first_layer,
    w_first,
    w_second,
    tile_values,
    tile_sources,
    halo_sources,
    send_rows,
    block_counts,
    stale_halo,
):
    leaving = outgoing(first_layer, send_rows, block_counts)
    arrived = lax.all_to_all(leaving, "dom", split_axis=0, concat_axis=0, tiled=True)
    halo_rows = compact(arrived, halo_sources)
    hidden_one = layer(
        first_layer, halo_rows, first_layer, tile_values, tile_sources, w_first, beta_first
    )
    sending = outgoing(hidden_one, send_rows, block_counts)
    received = lax.all_to_all(sending, "dom", split_axis=0, concat_axis=0, tiled=True)
    fresh_halo = compact(received, halo_sources)
    layer_out = layer(
        hidden_one, stale_halo, first_layer, tile_values, tile_sources, w_second, beta_second
    )
    return (layer_out, fresh_halo)


def solution(mesh):
    placed = (
        P("dom", "feat"),
        P("feat", "dom"),
        P("feat", "dom"),
        P("dom", None, None, None),
        P("dom", None, None),
        P("dom", None),
        P("dom", None, None),
        P("dom", None),
        P("dom", "feat"),
    )
    return jax.shard_map(
        shards,
        mesh=mesh,
        in_specs=placed,
        out_specs=(P("dom", "feat"), P("dom", "feat")),
        check_vma=False,
    )
```

profile of v0, /device:TPU:7, one launch (start us, length us, event | category | flops | bytes accessed | tf_op | source)
XLA Modules:
  0.0 379.0 jit_solution(5757164173672653659)
XLA Ops:
  7.2 1.5 fusion.4
  11.0 27.9 %gather_fusion = bf16[8192,128]{1,0:T(8,128)(2,1)S(1)} fusion(bf16[513,128]{1,0:T(8,128)(2,1)S(1)} %concatenate.12, s32[8192]{0:T(1024)} %fusion.4), kind=kCustom, calls=%fused_computation.clone | custom fusion | bytes 4227072 | tf_op jit(solution)/shard_map/jit(_take)/gather | solution.py:17
  39.0 4.3 %broadcast_select_fusion.3 = bf16[8192,128]{1,0:T(8,128)(2,1)S(1)} fusion(bf16[8192,128]{1,0:T(8,128)(2,1)S(1)} %gather_fusion, pred[8192]{0:T(1024)(128)(4,1)S(1)} %compare_and_fusion), kind=kLoop, calls=%fused_computation.9 | loop fusion | flops 1048576 | bytes 4202496 | tf_op jit(solution)/shard_map/jit(_take)/select_n | solution.py:17
  43.2 1.5 broadcast_select_fusion.1
  44.8 14.3 %all-to-all-start = ((bf16[64,128,128]{2,1,0:T(8,128)(2,1)}), bf16[64,128,128]{2,1,0:T(8,128)(2,1)S(1)}, u32[]{:S(2)}, u32[]{:S(2)}) async-start(bf16[64,128,128]{2,1,0:T(8,128)(2,1)} %broadcast_select_fusion.1), calls=%async_computation | async-start | bytes 4194304 | tf_op jit(solution)/shard_map/all_to_all | solution.py:66
  59.2 86.5 %all_gather.6 = bf16[128,1024]{0,1:T(8,128)(2,1)} all-gather(bf16[128,16]{0,1:T(8,128)(2,1)S(1)} %copy-done.7), channel_id=1, replica_groups=mesh['dom'=64,'feat'=8] {'dom'}, dimensions={1}, use_global_device_ids=true | all-gather | bytes 266240 | tf_op jit(solution)/shard_map/all_gather | solution.py:38
  145.8 1.7 gather_fusion.1
  147.5 1.4 broadcast_select_fusion.7
  149.0 1.9 gather_fusion.2
  150.9 1.5 broadcast_select_fusion.4
  153.8 1.3 copy.13
  155.2 35.9 %reduce-scatter.7.cloned.1.call-done = bf16[128,512]{1,0:T(8,128)(2,1)} async-done(((bf16[1024,512]{1,0:T(8,128)(2,1)}), bf16[128,512]{1,0:T(8,128)(2,1)}) %reduce-scatter.7.cloned.1.call-update) | async-done | bytes 131088
  192.9 27.9 %gather_fusion.4 = bf16[8192,128]{1,0:T(8,128)(2,1)S(1)} fusion(bf16[513,128]{1,0:T(8,128)(2,1)S(1)} %concatenate.15, s32[8192]{0:T(1024)} %fusion.4), kind=kCustom, calls=%fused_computation.3.clone | custom fusion | bytes 4227072 | tf_op jit(solution)/shard_map/jit(_take)/gather | solution.py:17
  220.8 4.3 %broadcast_select_fusion.2 = bf16[8192,128]{1,0:T(8,128)(2,1)S(1)} fusion(bf16[8192,128]{1,0:T(8,128)(2,1)S(1)} %gather_fusion.4, pred[8192]{0:T(1024)(128)(4,1)S(1)} %compare_and_fusion), kind=kLoop, calls=%fused_computation.8 | loop fusion | flops 1048576 | bytes 4202496 | tf_op jit(solution)/shard_map/jit(_take)/select_n | solution.py:17
  225.1 1.5 broadcast_select_fusion
  226.7 16.0 %all-to-all-start.1 = ((bf16[64,128,128]{2,1,0:T(8,128)(2,1)}), bf16[64,128,128]{2,1,0:T(8,128)(2,1)}, u32[]{:S(2)}, u32[]{:S(2)}) async-start(bf16[64,128,128]{2,1,0:T(8,128)(2,1)} %broadcast_select_fusion), calls=%async_computation.1 | async-start | bytes 4194304 | tf_op jit(solution)/shard_map/all_to_all | solution.py:72
  242.7 83.2 %all_gather.7 = bf16[128,1024]{0,1:T(8,128)(2,1)S(1)} all-gather(bf16[128,16]{0,1:T(8,128)(2,1)S(1)} %copy-done.8), channel_id=1, replica_groups=mesh['dom'=64,'feat'=8] {'dom'}, dimensions={1}, use_global_device_ids=true | all-gather | bytes 266240 | tf_op jit(solution)/shard_map/all_gather | solution.py:38
  325.9 1.3 pad_maximum_fusion.1
  327.2 2.0 gather_fusion.3
  329.3 1.5 broadcast_select_fusion.5
  332.2 1.3 copy.15
  333.5 33.4 %reduce-scatter.9.cloned.1.call-done = bf16[128,512]{1,0:T(8,128)(2,1)} async-done(((bf16[1024,512]{1,0:T(8,128)(2,1)}), bf16[128,512]{1,0:T(8,128)(2,1)}) %reduce-scatter.9.cloned.1.call-update) | async-done | bytes 131088
  368.6 2.3 gather_fusion.5
  371.0 1.1 broadcast_select_fusion.6
  (62 shorter events, 9.0 us)
Async XLA Ops:
  7.2 145.3 %copy-start = (bf16[4,10,128,128]{3,2,1,0:T(8,128)(2,1)S(1)}, bf16[4,10,128,128]{3,2,1,0:T(8,128)(2,1)}, u32[]{:S(2)}) copy-start(bf16[4,10,128,128]{3,2,1,0:T(8,128)(2,1)} %param.18) | copy-start | bytes 3932164
  10.1 33.1 %copy-start.11 = (pred[64]{0:T(512)(128)(4,1)}, pred[64]{0:T(512)(128)(4,1)S(1)}, u32[]{:S(2)}) copy-start(pred[64]{0:T(512)(128)(4,1)S(1)} %compare_bitcast_fusion) | copy-start | bytes 196
  44.8 14.3 %copy-start.13 = (s32[1,4,10]{2,1,0:T(4,128)S(1)}, s32[1,4,10]{2,1,0:T(4,128)}, u32[]{:S(2)}) copy-start(s32[1,4,10]{2,1,0:T(4,128)} %param.19) | copy-start | bytes 484
  44.8 14.4 %copy-start.7 = (bf16[128,16]{0,1:T(8,128)(2,1)S(1)}, bf16[128,16]{0,1:T(8,128)(2,1)}, u32[]{:S(2)}) copy-start(bf16[128,16]{0,1:T(8,128)(2,1)} %param.16) | copy-start | bytes 12292
  44.8 100.9 %copy-start.16 = (s32[1,32]{1,0:T(1,128)S(1)}, s32[1,32]{1,0:T(1,128)}, u32[]{:S(2)}) copy-start(s32[1,32]{1,0:T(1,128)} %param.20) | copy-start | bytes 388
  44.8 101.0 %all-to-all-start = ((bf16[64,128,128]{2,1,0:T(8,128)(2,1)}), bf16[64,128,128]{2,1,0:T(8,128)(2,1)S(1)}, u32[]{:S(2)}, u32[]{:S(2)}) async-start(bf16[64,128,128]{2,1,0:T(8,128)(2,1)} %broadcast_select_fusion.1), calls=%async_computation | async-start | bytes 4194304 | tf_op jit(solution)/shard_map/all_to_all | solution.py:66
  59.1 132.0 %reduce-scatter.7.cloned.1.call-start = ((), (), s32[]{:S(2)}) async-start(), calls=%async_computation.4 | async-start | bytes 1179648
  145.8 3.3 copy-start.6
  145.8 3.1 copy-start.9
  145.8 5.1 %copy-start.14 = (pred[40]{0:T(512)(128)(4,1)}, pred[40]{0:T(512)(128)(4,1)S(1)}, u32[]{:S(2)}) copy-start(pred[40]{0:T(512)(128)(4,1)S(1)} %compare_and_fusion.1) | copy-start | bytes 124
  147.5 1.4 copy-start.1
  152.4 1.0 copy-start.5
  192.2 0.7 copy-start.3
  220.8 4.3 %copy-start.12 = (pred[64]{0:T(512)(128)(4,1)S(1)}, pred[64]{0:T(512)(128)(4,1)}, u32[]{:S(2)}) copy-start(pred[64]{0:T(512)(128)(4,1)} %copy-done.11) | copy-start | bytes 196
  226.7 16.0 %copy-start.8 = (bf16[128,16]{0,1:T(8,128)(2,1)S(1)}, bf16[128,16]{0,1:T(8,128)(2,1)}, u32[]{:S(2)}) copy-start(bf16[128,16]{0,1:T(8,128)(2,1)} %param.17) | copy-start | bytes 12292
  226.7 99.3 %copy-start.4 = (bf16[512,128]{1,0:T(8,128)(2,1)S(1)}, bf16[512,128]{1,0:T(8,128)(2,1)}, u32[]{:S(2)}) copy-start(bf16[512,128]{1,0:T(8,128)(2,1)} %copy-done.3) | copy-start | bytes 393220
  226.7 142.0 %all-to-all-start.1 = ((bf16[64,128,128]{2,1,0:T(8,128)(2,1)}), bf16[64,128,128]{2,1,0:T(8,128)(2,1)}, u32[]{:S(2)}, u32[]{:S(2)}) async-start(bf16[64,128,128]{2,1,0:T(8,128)(2,1)} %broadcast_select_fusion), calls=%async_computation.1 | async-start | bytes 4194304 | tf_op jit(solution)/shard_map/all_to_all | solution.py:72
  242.6 124.2 %reduce-scatter.9.cloned.1.call-start = ((), (), s32[]{:S(2)}) async-start(), calls=%async_computation.5 | async-start | bytes 1179648
  327.2 2.0 copy-start.15
  330.8 0.9 copy-start.2
  367.9 3.1 copy-start.10
Sparse Core Ops, SparseCore 0:
  155.3 35.7 reduce-scatter.6
  333.6 33.1 reduce-scatter.8
where the time goes:
time: 385 us; the launch traced here: 379 us
  blocking collectives  170 us (44%)
  local copies, waits for them, and re-layouts  70.9 us (18%)
  waiting for transfers between devices  69.3 us (18%)
  starting transfers between devices  30.3 us (8%)
  other arithmetic  22.4 us (6%)
  between operations  14.4 us (4%)
    all_gather x2, blocking collectives, transform(): full_rows = lax.all_gather(weight, 'dom', axis=1, tiled=True)  170 us
    unnamed x4, waiting for transfers between devices  69.3 us
    gather x2, local copies, waits for them, and re-layouts, outgoing(): jnp.take(padded, send_rows[0].reshape(-1), axis=0).reshape(peers, -1, width)  55.9 us
    all_to_all x1, starting transfers between devices, shards(): lax.all_to_all(sending, 'dom', split_axis=0, concat_axis=0, tiled=True)  16 us
    all_to_all x1, starting transfers between devices, shards(): lax.all_to_all(leaving, 'dom', split_axis=0, concat_axis=0, tiled=True)  14.3 us
    select_n x2, other arithmetic, outgoing(): jnp.take(padded, send_rows[0].reshape(-1), axis=0).reshape(peers, -1, width)  8.54 us
  transfers between devices with their start and end apart: 4, of which 2 were waited for; matrix products, arithmetic and copies ran while one was open for 2% of the time, Pallas kernels for 0%

commit v1 on v0

v1 whole, which is shorter than its diff:
```python
import math

import jax
import jax.numpy as jnp
from jax import lax
from jax.experimental import pallas as pl
from jax.experimental.pallas import tpu as pltpu
from jax.sharding import PartitionSpec as P

alpha_mix = 0.1
beta_first = math.log(1.5)
beta_second = math.log(1.25)
VMEM_BYTES = 40 * 1024 * 1024
GROUP = 8
bf16 = jnp.bfloat16
f32 = jnp.float32


def params():
    return pltpu.CompilerParams(vmem_limit_bytes=VMEM_BYTES)


def cost(flops, moved):
    return pl.CostEstimate(flops=flops, bytes_accessed=moved, transcendentals=0)


def dot_nt(left, right):
    return lax.dot_general(left, right, (((1,), (1,)), ((), ())), preferred_element_type=f32)


def fold_rows(rows):
    half = rows.shape[0] // 2
    return jnp.concatenate([rows[:half], rows[half:]], axis=1)


def pick_blocks(folded, index_ref, out_ref):
    half = folded.shape[0]
    width = folded.shape[1] // 2
    slots = index_ref.shape[1]
    index = index_ref[0]
    low = index % half
    part = index // half
    lanes = lax.broadcasted_iota(jnp.int32, (slots, half), 1)
    for t in range(index.shape[1]):
        hot = jnp.where(lanes == low[:, t : t + 1], 1.0, 0.0).astype(bf16)
        both = jnp.dot(hot, folded, preferred_element_type=f32)
        side = jnp.broadcast_to(part[:, t : t + 1], (slots, width))
        rows = jnp.where(side == 0, both[:, :width], jnp.where(side == 1, both[:, width:], 0.0))
        out_ref[t] = rows.astype(out_ref.dtype)


def pack_kernel(rows_ref, index_ref, out_ref):
    pick_blocks(fold_rows(rows_ref[...]), index_ref, out_ref)


def pack(rows, index):
    groups, slots, per = index.shape
    count, width = rows.shape
    return pl.pallas_call(
        pack_kernel,
        grid=(groups,),
        in_specs=[
            pl.BlockSpec((count, width), lambda g: (0, 0)),
            pl.BlockSpec((1, slots, per), lambda g: (g, 0, 0)),
        ],
        out_specs=pl.BlockSpec((per, slots, width), lambda g: (g, 0, 0)),
        out_shape=jax.ShapeDtypeStruct((groups * per, slots, width), bf16),
        compiler_params=params(),
        cost_estimate=cost(2 * groups * per * slots * count * width, 3 * 1024 * 1024),
        name="pack",
    )(rows, index)


def layer_kernel(local_tiles, local_ref, first_ref, halo_ref, tiles_ref, weight_ref, sources_ref, peers_ref, part_ref, mixed_ref):
    blocks, tiles = tiles_ref.shape[0], tiles_ref.shape[1]
    size = tiles_ref.shape[2]
    for i in range(blocks):
        total = None
        for k in range(0, tiles, 2):
            pair = []
            for kk in (k, k + 1):
                source = sources_ref[i, kk]
                if kk < local_tiles:
                    start = pl.multiple_of(source * size, size)
                    pair.append(local_ref[pl.ds(start, size), :])
                else:
                    pair.append(halo_ref[peers_ref[source - blocks]])
            left = jnp.concatenate([tiles_ref[i, k], tiles_ref[i, k + 1]], axis=1)
            term = jnp.dot(left, jnp.concatenate(pair, axis=0), preferred_element_type=f32)
            total = term if total is None else total + term
        rows = pl.ds(i * size, size)
        mixed = (1.0 - alpha_mix) * total + alpha_mix * first_ref[rows, :].astype(f32)
        mixed_ref[rows, :] = mixed
    rounded = mixed_ref[...].astype(bf16)
    width = part_ref.shape[2]
    for g in range(part_ref.shape[0]):
        part_ref[g] = dot_nt(rounded, weight_ref[g * width : (g + 1) * width, :]).astype(bf16)


def layer_parts(local_rows, first_rows, halo, tiles, weight, sources, peers, feats, name):
    count, width = local_rows.shape
    vmem = pl.BlockSpec(memory_space=pltpu.VMEM)
    smem = pl.BlockSpec(memory_space=pltpu.SMEM)

    def kernel(*refs):
        layer_kernel(2, *refs)

    return pl.pallas_call(
        kernel,
        in_specs=[vmem] * 5 + [smem] * 2,
        out_specs=[vmem] * 2,
        out_shape=[
            jax.ShapeDtypeStruct((feats, count, width), bf16),
            jax.ShapeDtypeStruct((count, width), f32),
        ],
        compiler_params=params(),
        cost_estimate=cost(300 * 1000 * 1000, 6 * 1024 * 1024),
        name=name,
    )(local_rows, first_rows, halo, tiles, weight, sources, peers)


def finished(beta, part_ref, mixed_ref):
    turned = part_ref[0].astype(f32)
    for g in range(1, part_ref.shape[0]):
        turned = turned + part_ref[g].astype(f32)
    return jax.nn.relu((1.0 - beta) * mixed_ref[...] + beta * turned).astype(bf16)


def hidden_pack_kernel(part_ref, mixed_ref, index_ref, out_ref, hidden_ref, folded_ref):
    @pl.when(pl.program_id(0) == 0)
    def _():
        hidden = finished(beta_first, part_ref, mixed_ref)
        hidden_ref[...] = hidden
        folded_ref[...] = fold_rows(hidden)

    pick_blocks(folded_ref[...], index_ref, out_ref)


def hidden_pack(parts, mixed, index):
    groups, slots, per = index.shape
    feats, count, width = parts.shape
    return pl.pallas_call(
        hidden_pack_kernel,
        grid=(groups,),
        in_specs=[
            pl.BlockSpec((feats, count, width), lambda g: (0, 0, 0)),
            pl.BlockSpec((count, width), lambda g: (0, 0)),
            pl.BlockSpec((1, slots, per), lambda g: (g, 0, 0)),
        ],
        out_specs=[
            pl.BlockSpec((per, slots, width), lambda g: (g, 0, 0)),
            pl.BlockSpec((count, width), lambda g: (0, 0)),
        ],
        out_shape=[
            jax.ShapeDtypeStruct((groups * per, slots, width), bf16),
            jax.ShapeDtypeStruct((count, width), bf16),
        ],
        scratch_shapes=[pltpu.VMEM((count // 2, 2 * width), bf16)],
        compiler_params=params(),
        cost_estimate=cost(2 * groups * per * slots * count * width, 4 * 1024 * 1024),
        name="hidden_pack",
    )(parts, mixed, index)


def final_kernel(part_ref, mixed_ref, out_ref):
    out_ref[...] = finished(beta_second, part_ref, mixed_ref)


def final_rows(parts, mixed):
    vmem = pl.BlockSpec(memory_space=pltpu.VMEM)
    return pl.pallas_call(
        final_kernel,
        in_specs=[vmem] * 2,
        out_specs=vmem,
        out_shape=jax.ShapeDtypeStruct(mixed.shape, bf16),
        compiler_params=params(),
        cost_estimate=cost(1000 * 1000, 2 * 1024 * 1024),
        name="final_rows",
    )(parts, mixed)


def compact_kernel(peers_ref, arrived_ref, out_ref, sems):
    copies = [
        pltpu.make_async_copy(arrived_ref.at[peers_ref[j]], out_ref.at[j], sems.at[j])
        for j in range(out_ref.shape[0])
    ]
    for copy in copies:
        copy.start()
    for copy in copies:
        copy.wait()


def compact(arrived, peers):
    shape = (peers.shape[0],) + arrived.shape[1:]
    out = pl.pallas_call(
        compact_kernel,
        in_specs=[pl.BlockSpec(memory_space=pltpu.SMEM), pl.BlockSpec(memory_space=pl.ANY)],
        out_specs=pl.BlockSpec(memory_space=pl.ANY),
        out_shape=jax.ShapeDtypeStruct(shape, arrived.dtype),
        scratch_shapes=[pltpu.SemaphoreType.DMA((shape[0],))],
        cost_estimate=cost(0, 2 * 1024 * 1024),
        name="compact",
    )(peers, arrived)
    return out.reshape(-1, arrived.shape[2])


def spread(weight, peers):
    turned = weight.T
    sent = jnp.broadcast_to(turned[None], (peers,) + turned.shape)
    got = lax.all_to_all(sent, "dom", split_axis=0, concat_axis=0, tiled=True)
    return got.reshape(-1, turned.shape[1])


def swap(blocks, axis):
    return lax.all_to_all(blocks, axis, split_axis=0, concat_axis=0, tiled=True)


def shards(
    first_layer,
    w_first,
    w_second,
    tile_values,
    tile_sources,
    halo_sources,
    send_rows,
    block_counts,
    stale_halo,
):
    count, width = first_layer.shape
    peers, slots = send_rows.shape[1:]
    feats = lax.axis_size("feat")
    halos = halo_sources.shape[1]
    sources = tile_sources[0]
    listed = halo_sources[0]
    index = jnp.where((block_counts[0] > 0)[:, None], send_rows[0], count)
    index = index.reshape(-1, GROUP, slots).transpose(0, 2, 1)

    first_weight = spread(w_first, peers)
    arrived = swap(pack(first_layer, index), "dom")
    parts, mixed = layer_parts(
        first_layer, first_layer, arrived, tile_values, first_weight, sources, listed, feats, "layer_first"
    )
    parts, w_second = lax.optimization_barrier((parts, w_second))
    second_weight = spread(w_second, peers)
    got = swap(parts, "feat")
    sending, hidden = hidden_pack(got, mixed, index)
    received = swap(sending, "dom")
    stale = stale_halo.reshape(halos, slots, width)
    order = jnp.arange(halos, dtype=jnp.int32)
    parts_two, mixed_two = layer_parts(
        hidden, first_layer, stale, tile_values, second_weight, sources, order, feats, "layer_second"
    )
    got_two = swap(parts_two, "feat")
    layer_out = final_rows(got_two, mixed_two)
    fresh_halo = compact(received, listed)
    return (layer_out, fresh_halo)


def solution(mesh):
    placed = (
        P("dom", "feat"),
        P("feat", "dom"),
        P("feat", "dom"),
        P("dom", None, None, None),
        P("dom", None, None),
        P("dom", None),
        P("dom", None, None),
        P("dom", None),
        P("dom", "feat"),
    )
    return jax.shard_map(
        shards,
        mesh=mesh,
        in_specs=placed,
        out_specs=(P("dom", "feat"), P("dom", "feat")),
        check_vma=False,
    )
```

time: 385 us -> 267 us (0.69); the launches traced: 379 us -> 265 us
  local copies, waits for them, and re-layouts: 70.9 us -> 7.69 us
  blocking collectives: 170 us -> 118 us
  Pallas kernels: 0 us -> 47.2 us
  other arithmetic: 22.4 us -> 0.72 us
  between operations: 14.4 us -> 0.77 us
  waiting for transfers between devices: 69.3 us -> 56 us
  starting transfers between devices: 30.3 us -> 35.3 us
    all_gather x2 -> x0, blocking collectives: 170 us -> none  [transform(): full_rows = lax.all_gather(weight, 'dom', axis=1, tiled=True)]
    all_to_all x0 -> x3, blocking collectives: none -> 118 us  [swap(): return lax.all_to_all(blocks, axis, split_axis=0, concat_axis=0, tiled=True)]
    unnamed x4 -> x0, waiting for transfers between devices: 69.3 us -> none
    gather x6 -> x0, local copies, waits for them, and re-layouts: 63.8 us -> none  [the longest x2 55.9 us: outgoing(): jnp.take(padded, send_rows[0].reshape(-1), axis=0).reshape(peers, -1, width)]
    all_to_all x2 -> x3, waiting for transfers between devices: 0.01 us -> 56 us  [the longest x1 48.7 us: swap(): return lax.all_to_all(blocks, axis, split_axis=0, concat_axis=0, tiled=True)]
    pallas_call x0 -> x6, Pallas kernels: none -> 47.2 us  [the longest x1 33.8 us: compact(): pl.pallas_call(compact_kernel, in_specs=[pl.BlockSpec(memory_space=pltpu....]
    select_n x10 -> x0, other arithmetic: 17.2 us -> none  [the longest x2 8.54 us: outgoing(): jnp.take(padded, send_rows[0].reshape(-1), axis=0).reshape(peers, -1, width)]
    all_to_all x2 -> x3, starting transfers between devices: 30.2 us -> 35.3 us  [the longest x2 24.9 us: spread(): got = lax.all_to_all(sent, 'dom', split_axis=0, concat_axis=0, tiled=True)]
  transfers between devices with their start and end apart: 4 -> 3, of which waited for: 2 -> 3; matrix products, arithmetic and copies ran while one was open for 2% -> 1% of each run, Pallas kernels for 0% -> 4%
where the time goes in v1:
time: 267 us; the launch traced here: 265 us
  blocking collectives  118 us (44%)
  waiting for transfers between devices  56 us (21%)
  Pallas kernels  47.2 us (18%)
  starting transfers between devices  35.3 us (13%)
  local copies, waits for them, and re-layouts  7.69 us (3%)
    all_to_all x3, blocking collectives, swap(): return lax.all_to_all(blocks, axis, split_axis=0, concat_axis=0, tiled=True)  118 us
    all_to_all x1, waiting for transfers between devices, swap(): return lax.all_to_all(blocks, axis, split_axis=0, concat_axis=0, tiled=True)  48.7 us
    pallas_call x1, Pallas kernels, compact(): pl.pallas_call(compact_kernel, in_specs=[pl.BlockSpec(memory_space=pltpu....  33.8 us
    all_to_all x2, starting transfers between devices, spread(): got = lax.all_to_all(sent, 'dom', split_axis=0, concat_axis=0, tiled=True)  24.9 us
    all_to_all x1, starting transfers between devices, swap(): return lax.all_to_all(blocks, axis, split_axis=0, concat_axis=0, tiled=True)  10.5 us
    all_to_all x2, waiting for transfers between devices, spread(): got = lax.all_to_all(sent, 'dom', split_axis=0, concat_axis=0, tiled=True)  7.26 us
  transfers between devices with their start and end apart: 3, of which 3 were waited for; matrix products, arithmetic and copies ran while one was open for 1% of the time, Pallas kernels for 4%

profile of v1, /device:TPU:7, one launch (start us, length us, event | category | flops | bytes accessed | tf_op | source)
XLA Modules:
  0.0 265.5 jit_solution(14455342512583740068)
XLA Ops:
  0.6 1.4 broadcast_in_dim.27
  2.1 14.3 %all-to-all-start.1 = ((bf16[64,16,128]{2,1,0:T(8,128)(2,1)}), bf16[64,16,128]{2,1,0:T(8,128)(2,1)}, u32[]{:S(2)}, u32[]{:S(2)}) async-start(bf16[64,16,128]{2,1,0:T(8,128)(2,1)} %broadcast_in_dim.27), calls=%async_computation.1 | async-start | bytes 524288 | tf_op jit(solution)/shard_map/all_to_all | solution.py:210
  16.4 1.0 copy.11
  17.4 0.7 compare_reduce_fusion
  18.2 3.6 %pack.1 = bf16[64,128,128]{2,1,0:T(8,128)(2,1)S(1)} custom-call(bf16[512,128]{1,0:T(8,128)(2,1)S(1)} %copy-done.1, s32[8,128,8]{2,1,0:T(8,128)S(1)} %select_bitcast_fusion.index_ref), custom_call_target="tpu_custom_call" | custom-call | flops 1073741824 | bytes 3145728 | tf_op jit(solution)/shard_map/pack/pallas_call | solution.py:59
  21.9 0.8 copy-done.3
  22.7 4.5 %all-to-all-done.1 = bf16[64,16,128]{2,1,0:T(8,128)(2,1)} async-done(((bf16[64,16,128]{2,1,0:T(8,128)(2,1)}), bf16[64,16,128]{2,1,0:T(8,128)(2,1)}, u32[]{:S(2)}, u32[]{:S(2)}) %all-to-all-start.1) | async-done | bytes 262176 | tf_op jit(solution)/shard_map/all_to_all | solution.py:210
  27.2 56.5 %all_to_all.30.refs_2_ = bf16[64,128,128]{2,1,0:T(8,128)(2,1)S(1)} all-to-all(bf16[64,128,128]{2,1,0:T(8,128)(2,1)S(1)} %pack.1), channel_id=1, replica_groups=mesh['dom'=64,'feat'=8] {'dom'}, dimensions={0} | all-to-all | bytes 4194304 | tf_op jit(solution)/shard_map/all_to_all | solution.py:215
  83.7 1.8 layer_first.1
  85.5 32.3 %all_to_all.31.part_ref = bf16[8,512,128]{2,1,0:T(8,128)(2,1)S(1)} all-to-all(bf16[8,512,128]{2,1,0:T(8,128)(2,1)S(1)} %get-tuple-element.11), channel_id=1, replica_groups=mesh['dom'=64,'feat'=8] {'feat'}, dimensions={0} | all-to-all | bytes 2097152 | tf_op jit(solution)/shard_map/all_to_all | solution.py:215
  117.8 0.7 broadcast_in_dim.28
  118.5 10.6 %all-to-all-start.3 = ((bf16[64,16,128]{2,1,0:T(8,128)(2,1)}), bf16[64,16,128]{2,1,0:T(8,128)(2,1)}, u32[]{:S(2)}, u32[]{:S(2)}) async-start(bf16[64,16,128]{2,1,0:T(8,128)(2,1)} %broadcast_in_dim.28), calls=%async_computation.3 | async-start | bytes 524288 | tf_op jit(solution)/shard_map/all_to_all | solution.py:210
  129.1 1.1 copy-done.4
  130.3 0.9 copy-done.10
  131.2 5.2 %hidden_pack.1 = (bf16[64,128,128]{2,1,0:T(8,128)(2,1)}, bf16[512,128]{1,0:T(8,128)(2,1)S(1)}) custom-call(bf16[8,512,128]{2,1,0:T(8,128)(2,1)S(1)} %all_to_all.31.part_ref, f32[512,128]{1,0:T(8,128)S(1)} %copy-done.10, s32[8,128,8]{2,1,0:T(8,128)S(1)} %copy-done.4), custom_call_target="tpu_custom_call" | custom-call | flops 1073741824 | bytes 4194304 | tf_op jit(solution)/shard_map/hidden_pack/pallas_call | solution.py:142
  136.5 0.7 copy-done.5
  137.1 2.8 %all-to-all-done.3 = bf16[64,16,128]{2,1,0:T(8,128)(2,1)} async-done(((bf16[64,16,128]{2,1,0:T(8,128)(2,1)}), bf16[64,16,128]{2,1,0:T(8,128)(2,1)}, u32[]{:S(2)}, u32[]{:S(2)}) %all-to-all-start.3) | async-done | bytes 262176 | tf_op jit(solution)/shard_map/all_to_all | solution.py:210
  139.9 0.9 copy-done.6
  140.8 1.8 layer_second.1
  142.6 29.0 %all_to_all.32.part_ref = bf16[8,512,128]{2,1,0:T(8,128)(2,1)S(1)} all-to-all(bf16[8,512,128]{2,1,0:T(8,128)(2,1)S(1)} %get-tuple-element.15), channel_id=1, replica_groups=mesh['dom'=64,'feat'=8] {'feat'}, dimensions={0} | all-to-all | bytes 2097152 | tf_op jit(solution)/shard_map/all_to_all | solution.py:215
  171.6 10.5 %all-to-all-start.5 = ((bf16[64,128,128]{2,1,0:T(8,128)(2,1)}), bf16[64,128,128]{2,1,0:T(8,128)(2,1)}, u32[]{:S(2)}, u32[]{:S(2)}) async-start(bf16[64,128,128]{2,1,0:T(8,128)(2,1)} %get-tuple-element.17), calls=%async_computation.5 | async-start | bytes 4194304 | tf_op jit(solution)/shard_map/all_to_all | solution.py:215
  182.1 0.8 final_rows.1
  182.9 48.7 %all-to-all-done.5.arrived_ref = bf16[64,128,128]{2,1,0:T(8,128)(2,1)} async-done(((bf16[64,128,128]{2,1,0:T(8,128)(2,1)}), bf16[64,128,128]{2,1,0:T(8,128)(2,1)}, u32[]{:S(2)}, u32[]{:S(2)}) %all-to-all-start.5) | async-done | bytes 2097184 | tf_op jit(solution)/shard_map/all_to_all | solution.py:215
  231.6 33.8 %compact.1 = bf16[32,128,128]{2,1,0:T(8,128)(2,1)} custom-call(s32[32]{0:T(128)} %bitcast.14, bf16[64,128,128]{2,1,0:T(8,128)(2,1)} %all-to-all-done.5.arrived_ref), custom_call_target="tpu_custom_call" | custom-call | bytes 2097152 | tf_op jit(solution)/shard_map/compact/pallas_call | solution.py:195
  (22 shorter events, 0.2 us)
Async XLA Ops:
  0.6 17.6 %copy-start.1 = (bf16[512,128]{1,0:T(8,128)(2,1)S(1)}, bf16[512,128]{1,0:T(8,128)(2,1)}, u32[]{:S(2)}) copy-start(bf16[512,128]{1,0:T(8,128)(2,1)} %refs_1_.3) | copy-start | bytes 393220
  2.1 25.1 %all-to-all-start.1 = ((bf16[64,16,128]{2,1,0:T(8,128)(2,1)}), bf16[64,16,128]{2,1,0:T(8,128)(2,1)}, u32[]{:S(2)}, u32[]{:S(2)}) async-start(bf16[64,16,128]{2,1,0:T(8,128)(2,1)} %broadcast_in_dim.27), calls=%async_computation.1 | async-start | bytes 524288 | tf_op jit(solution)/shard_map/all_to_all | solution.py:210
  21.9 0.8 copy-start.3
  22.7 61.0 %copy-start = (bf16[4,10,128,128]{3,2,1,0:T(8,128)(2,1)S(1)}, bf16[4,10,128,128]{3,2,1,0:T(8,128)(2,1)}, u32[]{:S(2)}) copy-start(bf16[4,10,128,128]{3,2,1,0:T(8,128)(2,1)} %refs_3_.3) | copy-start | bytes 3932164
  22.7 61.0 %copy-start.7 = (s32[1,4,10]{2,1,0:T(4,128)S(1)}, s32[1,4,10]{2,1,0:T(4,128)}, u32[]{:S(2)}) copy-start(s32[1,4,10]{2,1,0:T(4,128)} %param.13) | copy-start | bytes 484
  22.7 61.0 %copy-start.8 = (s32[1,32]{1,0:T(1,128)S(1)}, s32[1,32]{1,0:T(1,128)}, u32[]{:S(2)}) copy-start(s32[1,32]{1,0:T(1,128)} %param.14) | copy-start | bytes 388
  83.6 34.2 %copy-start.11 = (bf16[128,16]{0,1:T(8,128)(2,1)S(1)}, bf16[128,16]{0,1:T(8,128)(2,1)}, u32[]{:S(2)}) copy-start(bf16[128,16]{0,1:T(8,128)(2,1)} %param.11) | copy-start | bytes 12292
  85.5 32.3 %copy-start.9 = (f32[512,128]{1,0:T(8,128)}, f32[512,128]{1,0:T(8,128)S(1)}, u32[]{:S(2)}) copy-start(f32[512,128]{1,0:T(8,128)S(1)} %get-tuple-element.12.mixed_ref) | copy-start | bytes 786436
  118.5 21.3 %all-to-all-start.3 = ((bf16[64,16,128]{2,1,0:T(8,128)(2,1)}), bf16[64,16,128]{2,1,0:T(8,128)(2,1)}, u32[]{:S(2)}, u32[]{:S(2)}) async-start(bf16[64,16,128]{2,1,0:T(8,128)(2,1)} %broadcast_in_dim.28), calls=%async_computation.3 | async-start | bytes 524288 | tf_op jit(solution)/shard_map/all_to_all | solution.py:210
  129.1 10.8 %copy-start.2 = (bf16[4096,128]{1,0:T(8,128)(2,1)S(1)}, bf16[4096,128]{1,0:T(8,128)(2,1)}, u32[]{:S(2)}) copy-start(bf16[4096,128]{1,0:T(8,128)(2,1)} %param.17) | copy-start | bytes 3145732
  129.1 1.1 copy-start.4
  130.3 0.9 copy-start.10
  136.4 0.7 copy-start.5
  139.9 0.9 copy-start.6
  171.6 60.0 %all-to-all-start.5 = ((bf16[64,128,128]{2,1,0:T(8,128)(2,1)}), bf16[64,128,128]{2,1,0:T(8,128)(2,1)}, u32[]{:S(2)}, u32[]{:S(2)}) async-start(bf16[64,128,128]{2,1,0:T(8,128)(2,1)} %get-tuple-element.17), calls=%async_computation.5 | async-start | bytes 4194304 | tf_op jit(solution)/shard_map/all_to_all | solution.py:215

commit v2 on v0

v2 whole, which is shorter than its diff:
```python
import math

import jax
import jax.numpy as jnp
from jax import lax
from jax.experimental import pallas as pl
from jax.experimental.pallas import tpu as pltpu
from jax.sharding import PartitionSpec as P

alpha_mix = 0.1
beta_first = math.log(1.5)
beta_second = math.log(1.25)
VMEM_BYTES = 16 * 1024 * 1024
GROUP = 8
RANKS = 8
bf16 = jnp.bfloat16
f32 = jnp.float32
i32 = jnp.int32
vmem = pl.BlockSpec(memory_space=pltpu.VMEM)
smem = pl.BlockSpec(memory_space=pltpu.SMEM)


def params(limit=VMEM_BYTES):
    return pltpu.CompilerParams(vmem_limit_bytes=limit)


def cost(flops, moved):
    return pl.CostEstimate(flops=flops, bytes_accessed=moved, transcendentals=0)


def in_hbm(*arrays):
    return [pltpu.with_memory_space_constraint(array, pltpu.HBM) for array in arrays]


def dot_nt(left, right):
    return lax.dot_general(left, right, (((1,), (1,)), ((), ())), preferred_element_type=f32)


def fold_rows(rows):
    half = rows.shape[0] // 2
    return jnp.concatenate([rows[:half], rows[half:]], axis=1)


def prepare_index(rows_ref, counts_ref, half, low_ref, high_ref):
    lanes = rows_ref.shape[1]
    copies = lanes // rows_ref.shape[0]
    index = jnp.concatenate([rows_ref[...]] * copies, axis=0).T
    counts = jnp.concatenate([counts_ref[...]] * copies, axis=1)
    high = index >= half
    live = jnp.logical_and(counts > 0, index < 2 * half)
    low = jnp.where(live, index - jnp.where(high, half, 0), half + 44)
    low_ref[...] = low.astype(f32)
    high_ref[...] = jnp.where(high, 1.0, 0.0)


def pick_blocks(folded, low, high, blocks_ref, out_ref, sems):
    half = folded.shape[0]
    width = folded.shape[1] // 2
    targets, slots = blocks_ref.shape[0], blocks_ref.shape[1]
    lanes = low.shape[1]
    places = [
        (lax.broadcasted_iota(i32, (slots, lanes), 1) + first).astype(f32).astype(bf16)
        for first in range(0, half, lanes)
    ]
    one, zero = jnp.ones((slots, lanes), bf16), jnp.zeros((slots, lanes), bf16)
    copies = []
    for t in range(targets):
        wanted = jnp.broadcast_to(low[:, t : t + 1], (slots, lanes)).astype(bf16)
        hot = jnp.concatenate([jnp.where(wanted == place, one, zero) for place in places], axis=1)
        both = jnp.dot(hot, folded, preferred_element_type=f32)
        side = jnp.broadcast_to(high[:, t : t + 1], (slots, width))
        blocks_ref[t] = jnp.where(side > 0.5, both[:, width:], both[:, :width]).astype(bf16)
        if (t + 1) % GROUP == 0:
            span = pl.ds(t + 1 - GROUP, GROUP)
            copy = pltpu.make_async_copy(blocks_ref.at[span], out_ref.at[span], sems.at[t // GROUP])
            copy.start()
            copies.append(copy)
    return copies


def pack_kernel(rows_ref, picks_ref, counts_ref, out_ref, blocks_ref, low_ref, high_ref, sems):
    prepare_index(picks_ref, counts_ref, rows_ref.shape[0] // 2, low_ref, high_ref)
    copies = pick_blocks(fold_rows(rows_ref[...]), low_ref[...], high_ref[...], blocks_ref, out_ref, sems)
    for copy in copies:
        copy.wait()


def pack(rows, picks, counts):
    targets, slots = picks.shape
    count, width = rows.shape
    return pl.pallas_call(
        pack_kernel,
        in_specs=[vmem] * 3,
        out_specs=pl.BlockSpec(memory_space=pltpu.HBM),
        out_shape=pltpu.HBM((targets, slots, width), bf16),
        scratch_shapes=[
            pltpu.VMEM((targets, slots, width), bf16),
            pltpu.VMEM((slots, slots), f32),
            pltpu.VMEM((slots, slots), f32),
            pltpu.SemaphoreType.DMA((targets // GROUP,)),
        ],
        compiler_params=params(),
        cost_estimate=cost(2 * targets * slots * count * width, 3 * 1024 * 1024),
        name="pack",
    )(*in_hbm(rows, picks, counts))


def tile_pairs(tiles_ref, i, firsts, block):
    total = None
    for k in firsts:
        left = jnp.concatenate([tiles_ref[i, k], tiles_ref[i, k + 1]], axis=1)
        right = jnp.concatenate([block(i, k), block(i, k + 1)], axis=0)
        term = jnp.dot(left, right, preferred_element_type=f32)
        total = term if total is None else total + term
    return total


def local_sum(tiles_ref, sources_ref, local_ref, i):
    size = tiles_ref.shape[2]

    def block(i, k):
        return local_ref[pl.ds(pl.multiple_of(sources_ref[i, k] * size, size), size), :]

    return tile_pairs(tiles_ref, i, [0], block)


def halo_sum(tiles_ref, sources_ref, block_of, i):
    blocks, tiles = tiles_ref.shape[0], tiles_ref.shape[1]

    def block(i, k):
        return block_of(sources_ref[i, k] - blocks)

    return tile_pairs(tiles_ref, i, range(2, tiles, 2), block)


def first_kernel(local_ref, halo_ref, tiles_ref, sources_ref, peers_ref, out_ref, mixed_ref, rounded_ref, sems):
    size = tiles_ref.shape[2]
    for i in range(tiles_ref.shape[0]):
        total = local_sum(tiles_ref, sources_ref, local_ref, i)
        total = total + halo_sum(tiles_ref, sources_ref, lambda j: halo_ref[peers_ref[j]], i)
        rows = pl.ds(i * size, size)
        mixed = (1.0 - alpha_mix) * total + alpha_mix * local_ref[rows, :].astype(f32)
        mixed_ref[rows, :] = mixed
        rounded_ref[rows, :] = mixed.astype(bf16)
    copies = [
        pltpu.make_async_copy(rounded_ref, out_ref.at[g], sems.at[g]) for g in range(out_ref.shape[0])
    ]
    for copy in copies:
        copy.start()
    for copy in copies:
        copy.wait()


def first_mixture(rows, halo, tiles, sources, peers, copies):
    count, width = rows.shape
    return pl.pallas_call(
        first_kernel,
        in_specs=[vmem] * 3 + [smem] * 2,
        out_specs=[pl.BlockSpec(memory_space=pltpu.HBM), vmem],
        out_shape=[
            pltpu.HBM((copies, count, width), bf16),
            jax.ShapeDtypeStruct((count, width), f32),
        ],
        scratch_shapes=[pltpu.VMEM((count, width), bf16), pltpu.SemaphoreType.DMA((copies,))],
        compiler_params=params(),
        cost_estimate=cost(170 * 1000 * 1000, 5 * 1024 * 1024),
        name="first_mixture",
    )(rows, halo, tiles, sources, peers)


def stale_kernel(first_ref, stale_ref, tiles_ref, sources_ref, out_ref):
    size = tiles_ref.shape[2]
    for i in range(tiles_ref.shape[0]):
        total = halo_sum(tiles_ref, sources_ref, lambda j: stale_ref[j], i)
        rows = pl.ds(i * size, size)
        out_ref[rows, :] = (1.0 - alpha_mix) * total + alpha_mix * first_ref[rows, :].astype(f32)


def stale_mixture(first_rows, stale, tiles, sources):
    return pl.pallas_call(
        stale_kernel,
        in_specs=[vmem] * 3 + [smem],
        out_specs=vmem,
        out_shape=jax.ShapeDtypeStruct(first_rows.shape, f32),
        compiler_params=params(),
        cost_estimate=cost(140 * 1000 * 1000, 4 * 1024 * 1024),
        name="stale_mixture",
    )(first_rows, stale, tiles, sources)


def columns_of(weight_ref, layer):
    half = weight_ref.shape[1] // 2
    return lambda z: weight_ref[z, pl.ds(layer * half, half), :]


def finished(beta, parts, mixed, weight_of):
    turned = None
    for (z, first), (zz, second) in zip(parts[::2], parts[1::2]):
        left = jnp.concatenate([first[...], second[...]], axis=1)
        right = jnp.concatenate([weight_of(z), weight_of(zz)], axis=1)
        term = dot_nt(left, right)
        turned = term if turned is None else turned + term
    return jax.nn.relu((1.0 - beta) * mixed + beta * turned).astype(bf16)


def hidden_kernel(
    parts_ref,
    mixed_ref,
    weight_ref,
    stale_ref,
    tiles_ref,
    picks_ref,
    counts_ref,
    sources_ref,
    out_ref,
    rounded_ref,
    second_ref,
    blocks_ref,
    hidden_ref,
    low_ref,
    high_ref,
    sems,
):
    prepare_index(picks_ref, counts_ref, mixed_ref.shape[0] // 2, low_ref, high_ref)
    parts = [(z, parts_ref.at[z]) for z in range(parts_ref.shape[0])]
    hidden = finished(beta_first, parts, mixed_ref[...], columns_of(weight_ref, 0))
    hidden_ref[...] = hidden
    copies = pick_blocks(fold_rows(hidden), low_ref[...], high_ref[...], blocks_ref, out_ref, sems)
    size = tiles_ref.shape[2]
    for i in range(tiles_ref.shape[0]):
        rows = pl.ds(i * size, size)
        total = local_sum(tiles_ref, sources_ref, hidden_ref, i)
        mixed = (1.0 - alpha_mix) * total + stale_ref[rows, :]
        second_ref[rows, :] = mixed
        rounded_ref[rows, :] = mixed.astype(bf16)
    for copy in copies:
        copy.wait()


def hidden_pack(parts, mixed, weights, stale_mixed, tiles, picks, counts, sources):
    targets, slots = picks.shape
    feats, count, width = parts.shape

    def part(array, *shape):
        return pl.BlockSpec(shape or array.shape, lambda g: (0,) * array.ndim)

    return pl.pallas_call(
        hidden_kernel,
        grid=(1,),
        in_specs=[
            part(parts),
            part(mixed),
            part(weights),
            part(stale_mixed),
            part(tiles, tiles.shape[0], 2, *tiles.shape[2:]),
            part(picks),
            part(counts),
            smem,
        ],
        out_specs=[
            pl.BlockSpec(memory_space=pltpu.HBM),
            pl.BlockSpec((count, width), lambda g: (0, 0)),
            pl.BlockSpec((count, width), lambda g: (0, 0)),
        ],
        out_shape=[
            pltpu.HBM((targets, slots, width), bf16),
            pltpu.HBM((count, width), bf16),
            pltpu.HBM((count, width), f32),
        ],
        scratch_shapes=[
            pltpu.VMEM((targets, slots, width), bf16),
            pltpu.VMEM((count, width), bf16),
            pltpu.VMEM((slots, slots), f32),
            pltpu.VMEM((slots, slots), f32),
            pltpu.SemaphoreType.DMA((targets // GROUP,)),
        ],
        compiler_params=params(),
        cost_estimate=cost(2 * targets * slots * count * width, 6 * 1024 * 1024),
        name="hidden_pack",
    )(parts, *in_hbm(mixed), weights, *in_hbm(stale_mixed, tiles, picks, counts), sources)


def final_kernel(place_ref, mixed_ref, weight_ref, *refs):
    feats = weight_ref.shape[0]
    parts = [(lax.rem(place_ref[0] + feats - k, feats), refs[k]) for k in range(feats)]
    refs[-1][...] = finished(beta_second, parts, mixed_ref[...], columns_of(weight_ref, 1))


def final_rows(place, mixed, weights, parts):
    return pl.pallas_call(
        final_kernel,
        in_specs=[smem] + [vmem] * (2 + len(parts)),
        out_specs=vmem,
        out_shape=jax.ShapeDtypeStruct(mixed.shape, bf16),
        compiler_params=params(),
        cost_estimate=cost(134 * 1000 * 1000, 3 * 1024 * 1024),
        name="final_rows",
    )(place, mixed, weights, *parts)


def compact_kernel(peers_ref, arrived_ref, out_ref, sems):
    copies = [
        pltpu.make_async_copy(arrived_ref.at[peers_ref[j]], out_ref.at[j], sems.at[j])
        for j in range(out_ref.shape[0])
    ]
    for copy in copies:
        copy.start()
    for copy in copies:
        copy.wait()


def compact(arrived, peers):
    shape = (peers.shape[0],) + arrived.shape[1:]
    out = pl.pallas_call(
        compact_kernel,
        in_specs=[smem, vmem],
        out_specs=pl.BlockSpec(memory_space=pl.ANY),
        out_shape=jax.ShapeDtypeStruct(shape, arrived.dtype),
        scratch_shapes=[pltpu.SemaphoreType.DMA((shape[0],))],
        compiler_params=params(16 * 1024 * 1024),
        cost_estimate=cost(0, 2 * 1024 * 1024),
        name="compact",
    )(peers, arrived)
    return out.reshape(-1, arrived.shape[2])


def slab_columns(w_first, w_second, feats):
    both = jnp.concatenate([w_first.T, w_second.T], axis=0)
    pairs = [
        ((z * RANKS + r) * feats + y, (y * RANKS + r) * feats + z)
        for z in range(feats)
        for r in range(RANKS)
        for y in range(feats)
    ]
    both = lax.ppermute(both, ("dom", "feat"), pairs)
    slabs = [[z * RANKS + r for r in range(RANKS)] for z in range(feats)]
    got = lax.all_gather(both, "dom", axis=0, tiled=True, axis_index_groups=slabs)
    return got.reshape(RANKS, 2, -1, both.shape[1]).swapaxes(0, 1).reshape(got.shape)


def own_columns(rows, feats):
    columns = [[z * RANKS + r for z in range(feats)] for r in range(RANKS)]
    return lax.all_gather(rows, "dom", axis=0, tiled=False, axis_index_groups=columns)


def around(rows, axis):
    size = lax.axis_size(axis)
    return [rows] + [
        lax.ppermute(rows, axis, [(i, (i + k) % size) for i in range(size)]) for k in range(1, size)
    ]


def swap(blocks, axis):
    return lax.all_to_all(blocks, axis, split_axis=0, concat_axis=0, tiled=True)


def shards(
    first_layer,
    w_first,
    w_second,
    tile_values,
    tile_sources,
    halo_sources,
    send_rows,
    block_counts,
    stale_halo,
):
    picks = send_rows[0]
    feats = lax.axis_size("feat")
    sources = tile_sources[0]
    listed = halo_sources[0]
    stale = stale_halo.reshape(listed.shape[0], picks.shape[1], -1)

    leaving = pack(first_layer, picks, block_counts)
    leaving, w_first, w_second = lax.optimization_barrier((leaving, w_first, w_second))
    slab = slab_columns(w_first, w_second, feats)
    arrived = swap(leaving, "dom")
    stale_mixed = stale_mixture(first_layer, stale, tile_values, sources)
    rounded, mixed = first_mixture(first_layer, arrived, tile_values, sources, listed, feats)
    rounded, slab = lax.optimization_barrier((rounded, slab))
    parts = swap(rounded, "feat")
    weights = own_columns(slab, feats)
    sending, rounded_two, mixed_two = hidden_pack(
        parts, mixed, weights, stale_mixed, tile_values, picks, block_counts, sources
    )
    received = swap(sending, "dom")
    place = lax.axis_index("feat").astype(i32).reshape(1)
    layer_out = final_rows(place, mixed_two, weights, around(rounded_two, "feat"))
    fresh_halo = compact(received, listed)
    return (layer_out, fresh_halo)


def solution(mesh):
    placed = (
        P("dom", "feat"),
        P("feat", "dom"),
        P("feat", "dom"),
        P("dom", None, None, None),
        P("dom", None, None),
        P("dom", None),
        P("dom", None, None),
        P("dom", None),
        P("dom", "feat"),
    )
    return jax.shard_map(
        shards,
        mesh=mesh,
        in_specs=placed,
        out_specs=(P("dom", "feat"), P("dom", "feat")),
        check_vma=False,
    )
```

time: 385 us -> 173 us (0.45); the launches traced: 379 us -> 171 us
  blocking collectives: 170 us -> 33.9 us
  local copies, waits for them, and re-layouts: 70.9 us -> 2.08 us
  starting transfers between devices: 30.3 us -> 57 us
  other arithmetic: 22.4 us -> 0.01 us
  Pallas kernels: 0 us -> 15.2 us
  between operations: 14.4 us -> 0.92 us
  waiting for transfers between devices: 69.3 us -> 61.8 us
    all_gather x2, blocking collectives: 170 us -> 33.9 us  [the longest x1 20.6 us: own_columns(): lax.all_gather(rows, 'dom', axis=0, tiled=False, axis_index_groups=columns)]
    unnamed x4 -> x0, waiting for transfers between devices: 69.3 us -> none
    gather x6 -> x0, local copies, waits for them, and re-layouts: 63.8 us -> none  [the longest x2 55.9 us: outgoing(): jnp.take(padded, send_rows[0].reshape(-1), axis=0).reshape(peers, -1, width)]
    all_to_all x2 -> x3, waiting for transfers between devices: 0.01 us -> 50.1 us  [swap(): return lax.all_to_all(blocks, axis, split_axis=0, concat_axis=0, tiled=True)]
    ppermute x0 -> x8, starting transfers between devices: none -> 28.4 us  [the longest x7 27.7 us: around(): lax.ppermute(rows, axis, [(i, (i + k) % size) for i in range(size)])]
    select_n x10 -> x0, other arithmetic: 17.2 us -> none  [the longest x2 8.54 us: outgoing(): jnp.take(padded, send_rows[0].reshape(-1), axis=0).reshape(peers, -1, width)]
    pallas_call x0 -> x6, Pallas kernels: none -> 15.2 us  [the longest x1 4.93 us: hidden_pack(): pl.pallas_call(hidden_kernel, grid=(1,), in_specs=[part(parts), part(mixe...]
    ppermute x0 -> x8, waiting for transfers between devices: none -> 11.7 us  [the longest x7 11.7 us: around(): lax.ppermute(rows, axis, [(i, (i + k) % size) for i in range(size)])]
  transfers between devices with their start and end apart: 4 -> 11, of which waited for: 2 -> 6; matrix products, arithmetic and copies ran while one was open for 2% -> 0% of each run, Pallas kernels for 0% -> 2%
where the time goes in v2:
time: 173 us; the launch traced here: 171 us
  waiting for transfers between devices  61.8 us (36%)
  starting transfers between devices  57 us (33%)
  blocking collectives  33.9 us (20%)
  Pallas kernels  15.2 us (9%)
  local copies, waits for them, and re-layouts  2.08 us (1%)
    all_to_all x3, waiting for transfers between devices, swap(): return lax.all_to_all(blocks, axis, split_axis=0, concat_axis=0, tiled=True)  50.1 us
    all_to_all x3, starting transfers between devices, swap(): return lax.all_to_all(blocks, axis, split_axis=0, concat_axis=0, tiled=True)  28.6 us
    ppermute x7, starting transfers between devices, around(): lax.ppermute(rows, axis, [(i, (i + k) % size) for i in range(size)])  27.7 us
    all_gather x1, blocking collectives, own_columns(): lax.all_gather(rows, 'dom', axis=0, tiled=False, axis_index_groups=columns)  20.6 us
    all_gather x1, blocking collectives, slab_columns(): lax.all_gather(both, 'dom', axis=0, tiled=True, axis_index_groups=slabs)  13.2 us
    ppermute x7, waiting for transfers between devices, around(): lax.ppermute(rows, axis, [(i, (i + k) % size) for i in range(size)])  11.7 us
    pallas_call x1, Pallas kernels, hidden_pack(): pl.pallas_call(hidden_kernel, grid=(1,), in_specs=[part(parts), part(mixe...  4.93 us
  transfers between devices with their start and end apart: 11, of which 6 were waited for; matrix products, arithmetic and copies ran while one was open for 0% of the time, Pallas kernels for 2%

profile of v2, /device:TPU:7, one launch (start us, length us, event | category | flops | bytes accessed | tf_op | source)
XLA Modules:
  0.0 170.8 jit_solution(7979602904700665277)
XLA Ops:
  0.6 3.2 %pack.1 = bf16[64,128,128]{2,1,0:T(8,128)(2,1)} custom-call(bf16[512,128]{1,0:T(8,128)(2,1)} %first_ref.1, s32[64,128]{1,0:T(8,128)} %bitcast.26, s32[1,64]{1,0:T(1,128)} %counts_ref.3), custom_call_target="tpu_custom_call" | custom-call | flops 1073741824 | bytes 3145728 | tf_op jit(solution)/shard_map/pack/pallas_call | solution.py:91
  4.0 14.3 %all-to-all-start = ((bf16[64,128,128]{2,1,0:T(8,128)(2,1)}), bf16[64,128,128]{2,1,0:T(8,128)(2,1)S(1)}, u32[]{:S(2)}, u32[]{:S(2)}) async-start(bf16[64,128,128]{2,1,0:T(8,128)(2,1)} %pack.1), calls=%async_computation | async-start | bytes 4194304 | tf_op jit(solution)/shard_map/all_to_all | solution.py:354
  18.9 13.2 %all_gather.9 = bf16[256,128]{1,0:T(8,128)(2,1)S(1)} all-gather(bf16[32,128]{1,0:T(8,128)(2,1)S(1)} %collective-permute-done), channel_id=1, replica_groups={{0,8,16,24,32,40,48,56},{64,72,80,88,96,104,112,120},{128,136,144,152,1..., dimensions={0}, use_global_device_ids=true | all-gather | bytes 73728 | tf_op jit(solution)/shard_map/all_gather | solution.py:337
  32.8 35.3 %all-to-all-done.halo_ref = bf16[64,128,128]{2,1,0:T(8,128)(2,1)S(1)} async-done(((bf16[64,128,128]{2,1,0:T(8,128)(2,1)}), bf16[64,128,128]{2,1,0:T(8,128)(2,1)S(1)}, u32[]{:S(2)}, u32[]{:S(2)}) %all-to-all-start) | async-done | bytes 2097184 | tf_op jit(solution)/shard_map/all_to_all | solution.py:354
  68.1 2.1 %first_mixture.1 = (bf16[8,512,128]{2,1,0:T(8,128)(2,1)}, f32[512,128]{1,0:T(8,128)S(1)}) custom-call(bf16[512,128]{1,0:T(8,128)(2,1)S(1)} %copy-done.2, bf16[64,128,128]{2,1,0:T(8,128)(2,1)S(1)} %all-to-all-done.halo_ref, bf16[4,10,128,128]{3,2,1,0:T(8,128)(2,1)S(1)} %copy-done, s32[4,10]{1,0:T(4,128)S(1)} %bitcast.16, s32[32]{0:T(128)S(1)} %bitcast.19), custom_call_target="tpu_custom_call" | custom-call | flops 170000000 | bytes 5242880 | tf_op jit(solution)/shard_map/first_mixture/pallas_call | solution.py:156
  70.9 8.7 %all-to-all-start.1 = ((bf16[8,512,128]{2,1,0:T(8,128)(2,1)}), bf16[8,512,128]{2,1,0:T(8,128)(2,1)S(1)}, u32[]{:S(2)}, u32[]{:S(2)}) async-start(bf16[8,512,128]{2,1,0:T(8,128)(2,1)} %get-tuple-element.16), calls=%async_computation.1 | async-start | bytes 2097152 | tf_op jit(solution)/shard_map/all_to_all | solution.py:354
  79.7 1.0 stale_mixture.1.stale_ref
  80.7 0.7 copy-done.4
  81.4 20.6 %all-gather = bf16[2048,128]{1,0:T(8,128)(2,1)S(1)} all-gather(bf16[256,128]{1,0:T(8,128)(2,1)S(1)} %bitcast.22), channel_id=2, replica_groups={{0,64,128,192,256,320,384,448},{8,72,136,200,264,328,392,456},{16,80,14..., dimensions={0}, use_global_device_ids=true | all-gather | bytes 589824 | tf_op jit(solution)/shard_map/all_gather | solution.py:343
  102.0 6.8 %all-to-all-done.1.parts_ref = bf16[8,512,128]{2,1,0:T(8,128)(2,1)S(1)} async-done(((bf16[8,512,128]{2,1,0:T(8,128)(2,1)}), bf16[8,512,128]{2,1,0:T(8,128)(2,1)S(1)}, u32[]{:S(2)}, u32[]{:S(2)}) %all-to-all-start.1) | async-done | bytes 1048608 | tf_op jit(solution)/shard_map/all_to_all | solution.py:354
  108.8 4.9 %hidden_pack.1 = (bf16[64,128,128]{2,1,0:T(8,128)(2,1)}, bf16[512,128]{1,0:T(8,128)(2,1)}, f32[512,128]{1,0:T(8,128)}) custom-call(bf16[8,512,128]{2,1,0:T(8,128)(2,1)S(1)} %all-to-all-done.1.parts_ref, f32[512,128]{1,0:T(8,128)} %copy-done.8, bf16[8,256,128]{2,1,0:T(8,128)(2,1)S(1)} %bitcast.13, f32[512,128]{1,0:T(8,128)} %copy-done.4, ...), custom_call_target="tpu_custom_call" | custom-call | flops 1073741824 | bytes 6291456 | tf_op jit(solution)/shard_map/hidden_pack/pallas_call | solution.py:247
  113.8 5.6 %all-to-all-start.2 = ((bf16[64,128,128]{2,1,0:T(8,128)(2,1)}), bf16[64,128,128]{2,1,0:T(8,128)(2,1)S(1)}, u32[]{:S(2)}, u32[]{:S(2)}) async-start(bf16[64,128,128]{2,1,0:T(8,128)(2,1)} %get-tuple-element.21), calls=%async_computation.2 | async-start | bytes 4194304 | tf_op jit(solution)/shard_map/all_to_all | solution.py:354
  119.4 2.8 %collective-permute-start.1 = (bf16[512,128]{1,0:T(8,128)(2,1)S(1)}, bf16[512,128]{1,0:T(8,128)(2,1)S(1)}, u32[]{:S(2)}, u32[]{:S(2)}) collective-permute-start(bf16[512,128]{1,0:T(8,128)(2,1)S(1)} %copy-done.5), channel_id=1, source_target_pairs={{0,1},{1,2},{2,3},{3,4},{4,5},{5,6},{6,7},{7,0},{8,9},{9,10},{10,1... | collective-permute-start | bytes 393224 | tf_op jit(solution)/shard_map/ppermute | solution.py:349
  122.3 4.0 %collective-permute-start.2 = (bf16[512,128]{1,0:T(8,128)(2,1)S(1)}, bf16[512,128]{1,0:T(8,128)(2,1)S(1)}, u32[]{:S(2)}, u32[]{:S(2)}) collective-permute-start(bf16[512,128]{1,0:T(8,128)(2,1)S(1)} %copy-done.5), channel_id=1, source_target_pairs={{0,2},{1,3},{2,4},{3,5},{4,6},{5,7},{6,0},{7,1},{8,10},{9,11},{10,... | collective-permute-start | bytes 393224 | tf_op jit(solution)/shard_map/ppermute | solution.py:349
  126.3 4.3 %collective-permute-start.3 = (bf16[512,128]{1,0:T(8,128)(2,1)S(1)}, bf16[512,128]{1,0:T(8,128)(2,1)S(1)}, u32[]{:S(2)}, u32[]{:S(2)}) collective-permute-start(bf16[512,128]{1,0:T(8,128)(2,1)S(1)} %copy-done.5), channel_id=1, source_target_pairs={{0,3},{1,4},{2,5},{3,6},{4,7},{5,0},{6,1},{7,2},{8,11},{9,12},{10,... | collective-permute-start | bytes 393224 | tf_op jit(solution)/shard_map/ppermute | solution.py:349
  130.6 4.0 %collective-permute-start.4 = (bf16[512,128]{1,0:T(8,128)(2,1)S(1)}, bf16[512,128]{1,0:T(8,128)(2,1)S(1)}, u32[]{:S(2)}, u32[]{:S(2)}) collective-permute-start(bf16[512,128]{1,0:T(8,128)(2,1)S(1)} %copy-done.5), channel_id=1, source_target_pairs={{0,4},{1,5},{2,6},{3,7},{4,0},{5,1},{6,2},{7,3},{8,12},{9,13},{10,... | collective-permute-start | bytes 393224 | tf_op jit(solution)/shard_map/ppermute | solution.py:349
  134.6 4.3 %collective-permute-start.5 = (bf16[512,128]{1,0:T(8,128)(2,1)S(1)}, bf16[512,128]{1,0:T(8,128)(2,1)}, u32[]{:S(2)}, u32[]{:S(2)}) collective-permute-start(bf16[512,128]{1,0:T(8,128)(2,1)S(1)} %copy-done.5), channel_id=1, source_target_pairs={{0,5},{1,6},{2,7},{3,0},{4,1},{5,2},{6,3},{7,4},{8,13},{9,14},{10,... | collective-permute-start | bytes 393224 | tf_op jit(solution)/shard_map/ppermute | solution.py:349
  138.9 5.2 %collective-permute-start.6 = (bf16[512,128]{1,0:T(8,128)(2,1)S(1)}, bf16[512,128]{1,0:T(8,128)(2,1)}, u32[]{:S(2)}, u32[]{:S(2)}) collective-permute-start(bf16[512,128]{1,0:T(8,128)(2,1)S(1)} %copy-done.5), channel_id=1, source_target_pairs={{0,6},{1,7},{2,0},{3,1},{4,2},{5,3},{6,4},{7,5},{8,14},{9,15},{10,... | collective-permute-start | bytes 393224 | tf_op jit(solution)/shard_map/ppermute | solution.py:349
  144.1 3.1 %collective-permute-start.7 = (bf16[512,128]{1,0:T(8,128)(2,1)S(1)}, bf16[512,128]{1,0:T(8,128)(2,1)}, u32[]{:S(2)}, u32[]{:S(2)}) collective-permute-start(bf16[512,128]{1,0:T(8,128)(2,1)S(1)} %copy-done.5), channel_id=1, source_target_pairs={{0,7},{1,0},{2,1},{3,2},{4,3},{5,4},{6,5},{7,6},{8,15},{9,8},{10,9... | collective-permute-start | bytes 393224 | tf_op jit(solution)/shard_map/ppermute | solution.py:349
  147.2 3.3 %collective-permute-done.5.refs_5_ = bf16[512,128]{1,0:T(8,128)(2,1)} collective-permute-done((bf16[512,128]{1,0:T(8,128)(2,1)S(1)}, bf16[512,128]{1,0:T(8,128)(2,1)}, u32[]{:S(2)}, u32[]{:S(2)}) %collective-permute-start.5) | collective-permute-done | bytes 131104 | tf_op jit(solution)/shard_map/ppermute | solution.py:349
  150.5 8.0 %collective-permute-done.6.refs_6_ = bf16[512,128]{1,0:T(8,128)(2,1)} collective-permute-done((bf16[512,128]{1,0:T(8,128)(2,1)S(1)}, bf16[512,128]{1,0:T(8,128)(2,1)}, u32[]{:S(2)}, u32[]{:S(2)}) %collective-permute-start.6) | collective-permute-done | bytes 131104 | tf_op jit(solution)/shard_map/ppermute | solution.py:349
  159.0 2.1 %final_rows.1 = bf16[512,128]{1,0:T(8,128)(2,1)} custom-call(s32[1]{0:T(128)} %bitcast.place_ref, f32[512,128]{1,0:T(8,128)S(1)} %copy-done.3, bf16[8,256,128]{2,1,0:T(8,128)(2,1)S(1)} %bitcast.14, bf16[512,128]{1,0:T(8,128)(2,1)S(1)} %copy-done.5, bf16[512,128]{1,0:T(8,128)(2,1)S(1)} %collective-permute-done.1.refs_1_, ...), custom_call_target="tpu_custom_call" | custom-call | flops 134000000 | bytes 3145728 | tf_op jit(solution)/shard_map/final_rows/pallas_call | solution.py:290
  161.1 8.0 %all-to-all-done.2.arrived_ref = bf16[64,128,128]{2,1,0:T(8,128)(2,1)S(1)} async-done(((bf16[64,128,128]{2,1,0:T(8,128)(2,1)}), bf16[64,128,128]{2,1,0:T(8,128)(2,1)S(1)}, u32[]{:S(2)}, u32[]{:S(2)}) %all-to-all-start.2) | async-done | bytes 2097184 | tf_op jit(solution)/shard_map/all_to_all | solution.py:354
  169.1 1.8 %compact.1 = bf16[32,128,128]{2,1,0:T(8,128)(2,1)} custom-call(s32[32]{0:T(128)S(1)} %bitcast.20, bf16[64,128,128]{2,1,0:T(8,128)(2,1)S(1)} %all-to-all-done.2.arrived_ref), custom_call_target="tpu_custom_call" | custom-call | bytes 2097152 | tf_op jit(solution)/shard_map/compact/pallas_call | solution.py:314
  (32 shorter events, 2.5 us)
Async XLA Ops:
  3.9 14.4 %copy-start.10 = (bf16[128,16]{0,1:T(8,128)(2,1)S(1)}, bf16[128,16]{0,1:T(8,128)(2,1)}, u32[]{:S(2)}) copy-start(bf16[128,16]{0,1:T(8,128)(2,1)} %param.11) | copy-start | bytes 12292
  3.9 14.3 %copy-start.11 = (bf16[128,16]{0,1:T(8,128)(2,1)S(1)}, bf16[128,16]{0,1:T(8,128)(2,1)}, u32[]{:S(2)}) copy-start(bf16[128,16]{0,1:T(8,128)(2,1)} %param.10) | copy-start | bytes 12292
  3.9 64.2 %copy-start = (bf16[4,10,128,128]{3,2,1,0:T(8,128)(2,1)S(1)}, bf16[4,10,128,128]{3,2,1,0:T(8,128)(2,1)}, u32[]{:S(2)}) copy-start(bf16[4,10,128,128]{3,2,1,0:T(8,128)(2,1)} %tiles_ref.5) | copy-start | bytes 3932164
  3.9 64.2 %copy-start.2 = (bf16[512,128]{1,0:T(8,128)(2,1)S(1)}, bf16[512,128]{1,0:T(8,128)(2,1)}, u32[]{:S(2)}) copy-start(bf16[512,128]{1,0:T(8,128)(2,1)} %first_ref.1) | copy-start | bytes 393220
  3.9 64.2 %copy-start.6 = (s32[1,4,10]{2,1,0:T(4,128)S(1)}, s32[1,4,10]{2,1,0:T(4,128)}, u32[]{:S(2)}) copy-start(s32[1,4,10]{2,1,0:T(4,128)} %param.13) | copy-start | bytes 484
  3.9 64.2 %copy-start.7 = (s32[1,32]{1,0:T(1,128)S(1)}, s32[1,32]{1,0:T(1,128)}, u32[]{:S(2)}) copy-start(s32[1,32]{1,0:T(1,128)} %param.14) | copy-start | bytes 388
  4.0 64.1 %all-to-all-start = ((bf16[64,128,128]{2,1,0:T(8,128)(2,1)}), bf16[64,128,128]{2,1,0:T(8,128)(2,1)S(1)}, u32[]{:S(2)}, u32[]{:S(2)}) async-start(bf16[64,128,128]{2,1,0:T(8,128)(2,1)} %pack.1), calls=%async_computation | async-start | bytes 4194304 | tf_op jit(solution)/shard_map/all_to_all | solution.py:354
  18.3 0.7 collective-permute-start
  70.2 0.7 copy-start.8
  70.9 8.7 %copy-start.1 = (bf16[4096,128]{1,0:T(8,128)(2,1)S(1)}, bf16[4096,128]{1,0:T(8,128)(2,1)}, u32[]{:S(2)}) copy-start(bf16[4096,128]{1,0:T(8,128)(2,1)} %param.17) | copy-start | bytes 3145732
  70.9 37.9 %all-to-all-start.1 = ((bf16[8,512,128]{2,1,0:T(8,128)(2,1)}), bf16[8,512,128]{2,1,0:T(8,128)(2,1)S(1)}, u32[]{:S(2)}, u32[]{:S(2)}) async-start(bf16[8,512,128]{2,1,0:T(8,128)(2,1)} %get-tuple-element.16), calls=%async_computation.1 | async-start | bytes 2097152 | tf_op jit(solution)/shard_map/all_to_all | solution.py:354
  79.6 1.7 %copy-start.9 = (bf16[2,8,16,128]{3,2,1,0:T(8,128)(2,1)S(1)}, bf16[2,8,16,128]{3,2,1,0:T(8,128)(2,1)}, u32[]{:S(2)}) copy-start(bf16[2,8,16,128]{3,2,1,0:T(8,128)(2,1)} %copy.11) | copy-start | bytes 196612
  80.7 0.7 copy-start.4
  113.8 5.7 %copy-start.5 = (bf16[512,128]{1,0:T(8,128)(2,1)S(1)}, bf16[512,128]{1,0:T(8,128)(2,1)}, u32[]{:S(2)}) copy-start(bf16[512,128]{1,0:T(8,128)(2,1)} %get-tuple-element.20.refs_0_) | copy-start | bytes 393220
  113.8 45.2 %copy-start.3 = (f32[512,128]{1,0:T(8,128)S(1)}, f32[512,128]{1,0:T(8,128)}, u32[]{:S(2)}) copy-start(f32[512,128]{1,0:T(8,128)} %get-tuple-element.19.mixed_ref) | copy-start | bytes 786436
  113.8 55.3 %all-to-all-start.2 = ((bf16[64,128,128]{2,1,0:T(8,128)(2,1)}), bf16[64,128,128]{2,1,0:T(8,128)(2,1)S(1)}, u32[]{:S(2)}, u32[]{:S(2)}) async-start(bf16[64,128,128]{2,1,0:T(8,128)(2,1)} %get-tuple-element.21), calls=%async_computation.2 | async-start | bytes 4194304 | tf_op jit(solution)/shard_map/all_to_all | solution.py:354
  119.4 19.4 %collective-permute-start.1 = (bf16[512,128]{1,0:T(8,128)(2,1)S(1)}, bf16[512,128]{1,0:T(8,128)(2,1)S(1)}, u32[]{:S(2)}, u32[]{:S(2)}) collective-permute-start(bf16[512,128]{1,0:T(8,128)(2,1)S(1)} %copy-done.5), channel_id=1, source_target_pairs={{0,1},{1,2},{2,3},{3,4},{4,5},{5,6},{6,7},{7,0},{8,9},{9,10},{10,1... | collective-permute-start | bytes 393224 | tf_op jit(solution)/shard_map/ppermute | solution.py:349
  122.3 21.8 %collective-permute-start.2 = (bf16[512,128]{1,0:T(8,128)(2,1)S(1)}, bf16[512,128]{1,0:T(8,128)(2,1)S(1)}, u32[]{:S(2)}, u32[]{:S(2)}) collective-permute-start(bf16[512,128]{1,0:T(8,128)(2,1)S(1)} %copy-done.5), channel_id=1, source_target_pairs={{0,2},{1,3},{2,4},{3,5},{4,6},{5,7},{6,0},{7,1},{8,10},{9,11},{10,... | collective-permute-start | bytes 393224 | tf_op jit(solution)/shard_map/ppermute | solution.py:349
  126.3 21.0 %collective-permute-start.3 = (bf16[512,128]{1,0:T(8,128)(2,1)S(1)}, bf16[512,128]{1,0:T(8,128)(2,1)S(1)}, u32[]{:S(2)}, u32[]{:S(2)}) collective-permute-start(bf16[512,128]{1,0:T(8,128)(2,1)S(1)} %copy-done.5), channel_id=1, source_target_pairs={{0,3},{1,4},{2,5},{3,6},{4,7},{5,0},{6,1},{7,2},{8,11},{9,12},{10,... | collective-permute-start | bytes 393224 | tf_op jit(solution)/shard_map/ppermute | solution.py:349
  130.6 16.7 %collective-permute-start.4 = (bf16[512,128]{1,0:T(8,128)(2,1)S(1)}, bf16[512,128]{1,0:T(8,128)(2,1)S(1)}, u32[]{:S(2)}, u32[]{:S(2)}) collective-permute-start(bf16[512,128]{1,0:T(8,128)(2,1)S(1)} %copy-done.5), channel_id=1, source_target_pairs={{0,4},{1,5},{2,6},{3,7},{4,0},{5,1},{6,2},{7,3},{8,12},{9,13},{10,... | collective-permute-start | bytes 393224 | tf_op jit(solution)/shard_map/ppermute | solution.py:349
  134.6 15.9 %collective-permute-start.5 = (bf16[512,128]{1,0:T(8,128)(2,1)S(1)}, bf16[512,128]{1,0:T(8,128)(2,1)}, u32[]{:S(2)}, u32[]{:S(2)}) collective-permute-start(bf16[512,128]{1,0:T(8,128)(2,1)S(1)} %copy-done.5), channel_id=1, source_target_pairs={{0,5},{1,6},{2,7},{3,0},{4,1},{5,2},{6,3},{7,4},{8,13},{9,14},{10,... | collective-permute-start | bytes 393224 | tf_op jit(solution)/shard_map/ppermute | solution.py:349
  138.9 19.6 %collective-permute-start.6 = (bf16[512,128]{1,0:T(8,128)(2,1)S(1)}, bf16[512,128]{1,0:T(8,128)(2,1)}, u32[]{:S(2)}, u32[]{:S(2)}) collective-permute-start(bf16[512,128]{1,0:T(8,128)(2,1)S(1)} %copy-done.5), channel_id=1, source_target_pairs={{0,6},{1,7},{2,0},{3,1},{4,2},{5,3},{6,4},{7,5},{8,14},{9,15},{10,... | collective-permute-start | bytes 393224 | tf_op jit(solution)/shard_map/ppermute | solution.py:349
  144.1 14.8 %collective-permute-start.7 = (bf16[512,128]{1,0:T(8,128)(2,1)S(1)}, bf16[512,128]{1,0:T(8,128)(2,1)}, u32[]{:S(2)}, u32[]{:S(2)}) collective-permute-start(bf16[512,128]{1,0:T(8,128)(2,1)S(1)} %copy-done.5), channel_id=1, source_target_pairs={{0,7},{1,0},{2,1},{3,2},{4,3},{5,4},{6,5},{7,6},{8,15},{9,8},{10,9... | collective-permute-start | bytes 393224 | tf_op jit(solution)/shard_map/ppermute | solution.py:349

commit v3 on v2

v3 whole, which is shorter than its diff:
```python
import math

import jax
import jax.numpy as jnp
from jax import lax
from jax.experimental import pallas as pl
from jax.experimental.pallas import tpu as pltpu
from jax.sharding import PartitionSpec as P

alpha_mix = 0.1
beta_first = math.log(1.5)
beta_second = math.log(1.25)
VMEM_BYTES = 16 * 1024 * 1024
RANKS = 8
SEND = 8
GROUP = 2
bf16 = jnp.bfloat16
f32 = jnp.float32
i32 = jnp.int32
vmem = pl.BlockSpec(memory_space=pltpu.VMEM)
smem = pl.BlockSpec(memory_space=pltpu.SMEM)


def params(limit=VMEM_BYTES):
    return pltpu.CompilerParams(vmem_limit_bytes=limit)


def cost(flops, moved):
    return pl.CostEstimate(flops=flops, bytes_accessed=moved, transcendentals=0)


def in_hbm(*arrays):
    return [pltpu.with_memory_space_constraint(array, pltpu.HBM) for array in arrays]


def dot_nt(left, right):
    return lax.dot_general(left, right, (((1,), (1,)), ((), ())), preferred_element_type=f32)


def fold_rows(rows):
    half = rows.shape[0] // 2
    return jnp.concatenate([rows[:half], rows[half:]], axis=1)


def place_of(picks, counts, half):
    targets = picks.shape[0]
    square = (targets, targets)
    same = lax.broadcasted_iota(i32, square, 0) == lax.broadcasted_iota(i32, square, 1)
    listed = jnp.where(same, jnp.broadcast_to(counts, square), 0)
    listed = jnp.sum(listed, axis=1, keepdims=True)
    high = picks >= half
    live = jnp.logical_and(listed > 0, picks < 2 * half)
    low = jnp.where(live, picks - jnp.where(high, half, 0), half + 44)
    return low.astype(f32), jnp.where(high, 1.0, 0.0)


def turned(rows):
    return jnp.concatenate([rows] * (rows.shape[1] // rows.shape[0]), axis=0).T


def picker(half, slots, width):
    lanes = slots
    places = [
        (lax.broadcasted_iota(i32, (slots, lanes), 1) + first).astype(f32).astype(bf16)
        for first in range(0, half, lanes)
    ]
    one, zero = jnp.ones((slots, lanes), bf16), jnp.zeros((slots, lanes), bf16)

    def pick(folded, low, high):
        wanted = jnp.broadcast_to(low, (slots, lanes)).astype(bf16)
        hot = jnp.concatenate([jnp.where(wanted == place, one, zero) for place in places], axis=1)
        both = jnp.dot(hot, folded, preferred_element_type=f32)
        side = jnp.broadcast_to(high, (slots, width))
        return jnp.where(side > 0.5, both[:, width:], both[:, :width]).astype(bf16)

    return pick


def pack_first_kernel(rows_ref, picks_ref, counts_ref, out_ref, index_ref, blocks_ref, places_ref, sems):
    targets, slots, width = blocks_ref.shape
    groups = index_ref.shape[0]
    half = rows_ref.shape[0] // 2
    low, high = place_of(picks_ref[...], counts_ref[...], half)
    per = targets // groups
    for g in range(groups):
        places_ref[g, 0:per, :] = low[g * per : (g + 1) * per].astype(bf16)
        places_ref[g, per : 2 * per, :] = high[g * per : (g + 1) * per].astype(bf16)
    copies = [pltpu.make_async_copy(places_ref, index_ref, sems.at[targets // SEND])]
    copies[0].start()
    low, high = turned(low), turned(high)
    folded = fold_rows(rows_ref[...])
    pick = picker(half, slots, width)
    for t in range(targets):
        blocks_ref[t] = pick(folded, low[:, t : t + 1], high[:, t : t + 1])
        if (t + 1) % SEND == 0:
            span = pl.ds(t + 1 - SEND, SEND)
            copies.append(pltpu.make_async_copy(blocks_ref.at[span], out_ref.at[span], sems.at[t // SEND]))
            copies[-1].start()
    for copy in copies:
        copy.wait()


def pack_first(rows, picks, counts, groups):
    targets, slots = picks.shape
    count, width = rows.shape
    index = (groups, 2 * targets // groups, slots)
    return pl.pallas_call(
        pack_first_kernel,
        in_specs=[vmem] * 3,
        out_specs=[pl.BlockSpec(memory_space=pltpu.HBM)] * 2,
        out_shape=[pltpu.HBM((targets, slots, width), bf16), pltpu.HBM(index, bf16)],
        scratch_shapes=[
            pltpu.VMEM((targets, slots, width), bf16),
            pltpu.VMEM(index, bf16),
            pltpu.SemaphoreType.DMA((targets // SEND + 1,)),
        ],
        compiler_params=params(),
        cost_estimate=cost(2 * targets * slots * count * width, 3 * 1024 * 1024),
        name="pack_first",
    )(*in_hbm(rows, picks, counts))


def pack_second_kernel(group_ref, rows_ref, *refs):
    groups = rows_ref.shape[0]
    index_refs, (out_ref, blocks_ref, sems) = refs[:groups], refs[groups:]
    targets, _, slots, width = blocks_ref.shape
    half = rows_ref.shape[1] // 2
    own = group_ref[0]
    places = [ref[own].astype(f32) for ref in index_refs]
    low = turned(jnp.concatenate([place[:targets] for place in places], axis=0))
    high = turned(jnp.concatenate([place[targets:] for place in places], axis=0))
    sources = [lax.rem(own + groups - k, groups) for k in range(groups)]
    folded = [fold_rows(rows_ref[source]) for source in sources]
    pick = picker(half, slots, width)
    copies = []
    for t in range(targets):
        for k in range(groups):
            c = k * targets + t
            blocks_ref[t, sources[k]] = pick(folded[k], low[:, c : c + 1], high[:, c : c + 1])
        if (t + 1) % GROUP == 0:
            span = pl.ds(t + 1 - GROUP, GROUP)
            copies.append(pltpu.make_async_copy(blocks_ref.at[span], out_ref.at[span], sems.at[t // GROUP]))
            copies[-1].start()
    for copy in copies:
        copy.wait()


def pack_second(group, rows, index, targets):
    groups, count, width = rows.shape
    shape = (targets, groups, width, width)
    return pl.pallas_call(
        pack_second_kernel,
        in_specs=[smem] + [vmem] * (1 + groups),
        out_specs=pl.BlockSpec(memory_space=pltpu.HBM),
        out_shape=pltpu.HBM(shape, bf16),
        scratch_shapes=[pltpu.VMEM(shape, bf16), pltpu.SemaphoreType.DMA((shape[0] // GROUP,))],
        compiler_params=params(),
        cost_estimate=cost(2 * shape[0] * groups * width * count * width, 3 * 1024 * 1024),
        name="pack_second",
    )(group, rows, *index)


def arrival(source, ranks, groups):
    return lax.rem(source, ranks) * groups + lax.div(source, ranks)


def tile_pairs(tiles_ref, i, firsts, block):
    total = None
    for k in firsts:
        left = jnp.concatenate([tiles_ref[i, k], tiles_ref[i, k + 1]], axis=1)
        right = jnp.concatenate([block(i, k), block(i, k + 1)], axis=0)
        term = jnp.dot(left, right, preferred_element_type=f32)
        total = term if total is None else total + term
    return total


def local_sum(tiles_ref, sources_ref, local_ref, i):
    size = tiles_ref.shape[2]

    def block(i, k):
        return local_ref[pl.ds(pl.multiple_of(sources_ref[i, k] * size, size), size), :]

    return tile_pairs(tiles_ref, i, [0], block)


def halo_sum(tiles_ref, sources_ref, block_of, i):
    blocks, tiles = tiles_ref.shape[0], tiles_ref.shape[1]

    def block(i, k):
        return block_of(sources_ref[i, k] - blocks)

    return tile_pairs(tiles_ref, i, range(2, tiles, 2), block)


def first_kernel(local_ref, halo_ref, tiles_ref, sources_ref, peers_ref, out_ref, rounded_ref, sems):
    size = tiles_ref.shape[2]
    for i in range(tiles_ref.shape[0]):
        total = local_sum(tiles_ref, sources_ref, local_ref, i)
        total = total + halo_sum(tiles_ref, sources_ref, lambda j: halo_ref[peers_ref[j]], i)
        rows = pl.ds(i * size, size)
        mixed = (1.0 - alpha_mix) * total + alpha_mix * local_ref[rows, :].astype(f32)
        rounded_ref[rows, :] = mixed.astype(bf16)
    copies = [
        pltpu.make_async_copy(rounded_ref, out_ref.at[g], sems.at[g]) for g in range(out_ref.shape[0])
    ]
    for copy in copies:
        copy.start()
    for copy in copies:
        copy.wait()


def first_mixture(rows, halo, tiles, sources, peers, copies):
    count, width = rows.shape
    return pl.pallas_call(
        first_kernel,
        in_specs=[vmem] * 3 + [smem] * 2,
        out_specs=pl.BlockSpec(memory_space=pltpu.HBM),
        out_shape=pltpu.HBM((copies, count, width), bf16),
        scratch_shapes=[pltpu.VMEM((count, width), bf16), pltpu.SemaphoreType.DMA((copies,))],
        compiler_params=params(),
        cost_estimate=cost(170 * 1000 * 1000, 5 * 1024 * 1024),
        name="first_mixture",
    )(rows, halo, tiles, sources, peers)


def stale_kernel(first_ref, stale_ref, tiles_ref, sources_ref, out_ref):
    size = tiles_ref.shape[2]
    for i in range(tiles_ref.shape[0]):
        total = halo_sum(tiles_ref, sources_ref, lambda j: stale_ref[j], i)
        rows = pl.ds(i * size, size)
        out_ref[rows, :] = (1.0 - alpha_mix) * total + alpha_mix * first_ref[rows, :].astype(f32)


def stale_mixture(first_rows, stale, tiles, sources):
    return pl.pallas_call(
        stale_kernel,
        in_specs=[vmem] * 3 + [smem],
        out_specs=vmem,
        out_shape=pltpu.HBM(first_rows.shape, f32),
        compiler_params=params(),
        cost_estimate=cost(140 * 1000 * 1000, 4 * 1024 * 1024),
        name="stale_mixture",
    )(first_rows, stale, tiles, sources)


def second_kernel(hidden_ref, stale_ref, tiles_ref, sources_ref, rounded_ref):
    size = tiles_ref.shape[2]
    for i in range(tiles_ref.shape[0]):
        rows = pl.ds(i * size, size)
        total = local_sum(tiles_ref, sources_ref, hidden_ref.at[0], i)
        rounded_ref[rows, :] = ((1.0 - alpha_mix) * total + stale_ref[rows, :]).astype(bf16)


def second_mixture(hidden_copies, stale_mixed, tiles, sources):
    shape = stale_mixed.shape
    return pl.pallas_call(
        second_kernel,
        grid=(1,),
        in_specs=[
            pl.BlockSpec((1,) + shape, lambda g: (0, 0, 0)),
            pl.BlockSpec(shape, lambda g: (0, 0)),
            pl.BlockSpec((tiles.shape[0], 2) + tiles.shape[2:], lambda g: (0, 0, 0, 0)),
            smem,
        ],
        out_specs=pl.BlockSpec(shape, lambda g: (0, 0)),
        out_shape=jax.ShapeDtypeStruct(shape, bf16),
        compiler_params=params(),
        cost_estimate=cost(34 * 1000 * 1000, 2 * 1024 * 1024),
        name="second_mixture",
    )(*in_hbm(hidden_copies, stale_mixed, tiles), sources)


def columns_of(weight_ref, layer):
    half = weight_ref.shape[1] // 2
    return lambda z: weight_ref[z, pl.ds(layer * half, half), :]


def finished(beta, parts, own, weight_of):
    turned = None
    for (z, first), (zz, second) in zip(parts[::2], parts[1::2]):
        left = jnp.concatenate([first, second], axis=1)
        right = jnp.concatenate([weight_of(z), weight_of(zz)], axis=1)
        term = dot_nt(left, right)
        turned = term if turned is None else turned + term
    return jax.nn.relu((1.0 - beta) * own.astype(f32) + beta * turned).astype(bf16)


def hidden_kernel(place_ref, parts_ref, weight_ref, out_ref, hidden_ref, sems):
    parts = [(z, parts_ref[z]) for z in range(parts_ref.shape[0])]
    hidden_ref[...] = finished(beta_first, parts, parts_ref[place_ref[0]], columns_of(weight_ref, 0))
    copies = [
        pltpu.make_async_copy(hidden_ref, out_ref.at[g], sems.at[g]) for g in range(out_ref.shape[0])
    ]
    for copy in copies:
        copy.start()
    for copy in copies:
        copy.wait()


def hidden_copies(place, parts, weights, groups):
    shape = parts.shape[1:]
    return pl.pallas_call(
        hidden_kernel,
        in_specs=[smem] + [vmem] * 2,
        out_specs=pl.BlockSpec(memory_space=pltpu.HBM),
        out_shape=pltpu.HBM((groups,) + shape, bf16),
        scratch_shapes=[pltpu.VMEM(shape, bf16), pltpu.SemaphoreType.DMA((groups,))],
        compiler_params=params(),
        cost_estimate=cost(134 * 1000 * 1000, 3 * 1024 * 1024),
        name="hidden",
    )(place, parts, weights)


def final_kernel(places, place_ref, weight_ref, *refs):
    feats = len(places)
    parts = [(lax.rem(place_ref[0] + (feats - k), feats), ref[...]) for k, ref in zip(places, refs)]
    refs[-1][...] = finished(beta_second, parts, refs[0][...], columns_of(weight_ref, 1))


def final_rows(place, weights, parts):
    places = list(parts)

    def kernel(*refs):
        final_kernel(places, *refs)

    return pl.pallas_call(
        kernel,
        in_specs=[smem] + [vmem] * (1 + len(parts)),
        out_specs=vmem,
        out_shape=jax.ShapeDtypeStruct(parts[0].shape, bf16),
        compiler_params=params(),
        cost_estimate=cost(134 * 1000 * 1000, 3 * 1024 * 1024),
        name="final_rows",
    )(place, weights, *parts.values())


def compact_kernel(groups, peers_ref, arrived_ref, out_ref, sems):
    ranks = arrived_ref.shape[0] // groups
    copies = [
        pltpu.make_async_copy(
            arrived_ref.at[arrival(peers_ref[j], ranks, groups)], out_ref.at[j], sems.at[j]
        )
        for j in range(out_ref.shape[0])
    ]
    for copy in copies:
        copy.start()
    for copy in copies:
        copy.wait()


def compact(arrived, peers, groups):
    shape = (peers.shape[0],) + arrived.shape[1:]

    def kernel(*refs):
        compact_kernel(groups, *refs)

    out = pl.pallas_call(
        kernel,
        in_specs=[smem, vmem],
        out_specs=pl.BlockSpec(memory_space=pl.ANY),
        out_shape=jax.ShapeDtypeStruct(shape, arrived.dtype),
        scratch_shapes=[pltpu.SemaphoreType.DMA((shape[0],))],
        compiler_params=params(),
        cost_estimate=cost(0, 2 * 1024 * 1024),
        name="compact",
    )(peers, arrived)
    return out.reshape(-1, arrived.shape[2])


def slab_columns(w_first, w_second, feats):
    both = jnp.concatenate([w_first.T, w_second.T], axis=0)
    pairs = [
        ((z * RANKS + r) * feats + y, (y * RANKS + r) * feats + z)
        for z in range(feats)
        for r in range(RANKS)
        for y in range(feats)
    ]
    both = lax.ppermute(both, ("dom", "feat"), pairs)
    slabs = [[z * RANKS + r for r in range(RANKS)] for z in range(feats)]
    got = lax.all_gather(both, "dom", axis=0, tiled=True, axis_index_groups=slabs)
    return got.reshape(RANKS, 2, -1, both.shape[1]).swapaxes(0, 1).reshape(got.shape)


def own_columns(rows, feats):
    columns = [[z * RANKS + r for z in range(feats)] for r in range(RANKS)]
    return lax.all_gather(rows, "dom", axis=0, tiled=False, axis_index_groups=columns)


def swap(blocks, axis, groups=None):
    return lax.all_to_all(blocks, axis, split_axis=0, concat_axis=0, axis_index_groups=groups, tiled=True)


def moved(rows, axis, by):
    size = lax.axis_size(axis)
    return lax.ppermute(rows, axis, [(i, (i + by) % size) for i in range(size)])


def shards(
    first_layer,
    w_first,
    w_second,
    tile_values,
    tile_sources,
    halo_sources,
    send_rows,
    block_counts,
    stale_halo,
):
    count = first_layer.shape[0]
    picks = send_rows[0]
    feats = lax.axis_size("feat")
    sources = tile_sources[0]
    listed = halo_sources[0]
    stale = stale_halo.reshape(listed.shape[0], picks.shape[1], -1)
    near = 2 * RANKS
    groups = picks.shape[0] // near
    far_groups = [[a * near + m for a in range(groups)] for m in range(near)]
    near_groups = [[a * near + m for m in range(near)] for a in range(groups)]
    place = lax.axis_index("feat").astype(i32).reshape(1)
    group = (lax.axis_index("dom") // near).astype(i32).reshape(1)

    leaving, index = pack_first(first_layer, picks, block_counts, groups)
    leaving, index, w_first, w_second, stale = lax.optimization_barrier(
        (leaving, index, w_first, w_second, stale)
    )
    index = [index] + [moved(index, "dom", k * near) for k in range(1, groups)]
    slab = slab_columns(w_first, w_second, feats)
    arrived = swap(leaving, "dom")
    stale_mixed = stale_mixture(first_layer, stale, tile_values, sources)
    rounded = first_mixture(first_layer, arrived, tile_values, sources, listed, feats)
    rounded, slab, stale_mixed, *index = lax.optimization_barrier((rounded, slab, stale_mixed, *index))
    parts = swap(rounded, "feat")
    weights = own_columns(slab, feats)

    hidden = hidden_copies(place, parts, weights, groups)
    spread_hidden = swap(hidden, "dom", far_groups)
    own = second_mixture(hidden, stale_mixed, tile_values, sources)
    before, after = moved(own, "feat", 1), moved(own, "feat", -1)
    spread_hidden, before, after = lax.optimization_barrier((spread_hidden, before, after))
    blocks = pack_second(group, spread_hidden, index, near)
    blocks, before, after = lax.optimization_barrier((blocks, before, after))
    received = swap(blocks, "dom", near_groups).reshape((-1,) + blocks.shape[2:])
    parts = {0: own, 1: before, -1: after}
    parts.update({4: moved(before, "feat", 3), 3: moved(before, "feat", 2), -3: moved(after, "feat", -2)})
    parts.update({2: moved(before, "feat", 1), -2: moved(after, "feat", -1)})
    layer_out = final_rows(place, weights, parts)
    fresh_halo = compact(received, listed, groups)
    return (layer_out, fresh_halo)


def solution(mesh):
    placed = (
        P("dom", "feat"),
        P("feat", "dom"),
        P("feat", "dom"),
        P("dom", None, None, None),
        P("dom", None, None),
        P("dom", None),
        P("dom", None, None),
        P("dom", None),
        P("dom", "feat"),
    )
    return jax.shard_map(
        shards,
        mesh=mesh,
        in_specs=placed,
        out_specs=(P("dom", "feat"), P("dom", "feat")),
        check_vma=False,
    )
```

time: 173 us -> 169 us (0.977)
  waiting for transfers between devices: 61.8 us -> 45.8 us
  starting transfers between devices: 57 us -> 69.1 us
    all_to_all x3 -> x4, waiting for transfers between devices: 50.1 us -> 37.5 us  [swap(): lax.all_to_all(blocks, axis, split_axis=0, concat_axis=0, axis_index_grou...]
    ppermute x7 -> x10, starting transfers between devices: 27.7 us -> 36.8 us  [moved(): return lax.ppermute(rows, axis, [(i, (i + by) % size) for i in range(size)])]
    ppermute x7 -> x10, waiting for transfers between devices: 11.7 us -> 8.29 us  [moved(): return lax.ppermute(rows, axis, [(i, (i + by) % size) for i in range(size)])]
    all_to_all x3 -> x4, starting transfers between devices: 28.6 us -> 31.6 us  [swap(): lax.all_to_all(blocks, axis, split_axis=0, concat_axis=0, axis_index_grou...]
    pallas_call x4 -> x6, Pallas kernels: 12.1 us -> 12 us  [the longest x1 3.38 us: pack_first(): pl.pallas_call(pack_first_kernel, in_specs=[vmem] * 3, out_specs=[pl.Bloc...]
  transfers between devices with their start and end apart: 11 -> 15, of which waited for: 6 -> 9; matrix products, arithmetic and copies ran while one was open for 0% -> 0% of each run, Pallas kernels for 2% -> 4%
where the time goes in v3:
time: 169 us; the launch traced here: 168 us
  starting transfers between devices  69.1 us (41%)
  waiting for transfers between devices  45.8 us (27%)
  blocking collectives  34.7 us (21%)
  Pallas kernels  15.8 us (9%)
  local copies, waits for them, and re-layouts  1.9 us (1%)
    all_to_all x4, waiting for transfers between devices, swap(): lax.all_to_all(blocks, axis, split_axis=0, concat_axis=0, axis_index_grou...  37.5 us
    ppermute x10, starting transfers between devices, moved(): return lax.ppermute(rows, axis, [(i, (i + by) % size) for i in range(size)])  36.8 us
    all_to_all x4, starting transfers between devices, swap(): lax.all_to_all(blocks, axis, split_axis=0, concat_axis=0, axis_index_grou...  31.6 us
    all_gather x1, blocking collectives, own_columns(): lax.all_gather(rows, 'dom', axis=0, tiled=False, axis_index_groups=columns)  21 us
    all_gather x1, blocking collectives, slab_columns(): lax.all_gather(both, 'dom', axis=0, tiled=True, axis_index_groups=slabs)  13.8 us
    ppermute x10, waiting for transfers between devices, moved(): return lax.ppermute(rows, axis, [(i, (i + by) % size) for i in range(size)])  8.29 us
  transfers between devices with their start and end apart: 15, of which 9 were waited for; matrix products, arithmetic and copies ran while one was open for 0% of the time, Pallas kernels for 4%

profile of v3, /device:TPU:7, one launch (start us, length us, event | category | flops | bytes accessed | tf_op | source)
XLA Modules:
  0.0 168.3 jit_solution(8893582036480803723)
XLA Ops:
  0.6 3.4 %pack_first.1 = (bf16[64,128,128]{2,1,0:T(8,128)(2,1)}, bf16[4,32,128]{2,1,0:T(8,128)(2,1)}) custom-call(bf16[512,128]{1,0:T(8,128)(2,1)} %first_ref.1, s32[64,128]{1,0:T(8,128)} %bitcast.29, s32[1,64]{1,0:T(1,128)} %counts_ref.1), custom_call_target="tpu_custom_call" | custom-call | flops 1073741824 | bytes 3145728 | tf_op jit(solution)/shard_map/pack_first/pallas_call | solution.py:107
  4.1 14.3 %all-to-all-start = ((bf16[64,128,128]{2,1,0:T(8,128)(2,1)}), bf16[64,128,128]{2,1,0:T(8,128)(2,1)S(1)}, u32[]{:S(2)}, u32[]{:S(2)}) async-start(bf16[64,128,128]{2,1,0:T(8,128)(2,1)} %get-tuple-element.24), calls=%async_computation | async-start | bytes 4194304 | tf_op jit(solution)/shard_map/all_to_all | solution.py:390
  18.4 4.0 %collective-permute-start.1 = (bf16[4,32,128]{2,1,0:T(8,128)(2,1)}, bf16[4,32,128]{2,1,0:T(8,128)(2,1)}, u32[]{:S(2)}, u32[]{:S(2)}) collective-permute-start(bf16[4,32,128]{2,1,0:T(8,128)(2,1)} %get-tuple-element.33.refs_0_), channel_id=1, source_target_pairs={{0,128},{8,136},{16,144},{24,152},{32,160},{40,168},{48,176},{56,1... | collective-permute-start | bytes 98312 | tf_op jit(solution)/shard_map/ppermute | solution.py:395
  22.4 5.4 %collective-permute-start.2 = (bf16[4,32,128]{2,1,0:T(8,128)(2,1)}, bf16[4,32,128]{2,1,0:T(8,128)(2,1)}, u32[]{:S(2)}, u32[]{:S(2)}) collective-permute-start(bf16[4,32,128]{2,1,0:T(8,128)(2,1)} %get-tuple-element.33.refs_0_), channel_id=1, source_target_pairs={{0,256},{8,264},{16,272},{24,280},{32,288},{40,296},{48,304},{56,3... | collective-permute-start | bytes 98312 | tf_op jit(solution)/shard_map/ppermute | solution.py:395
  27.8 5.1 %collective-permute-start.3 = (bf16[4,32,128]{2,1,0:T(8,128)(2,1)}, bf16[4,32,128]{2,1,0:T(8,128)(2,1)}, u32[]{:S(2)}, u32[]{:S(2)}) collective-permute-start(bf16[4,32,128]{2,1,0:T(8,128)(2,1)} %get-tuple-element.33.refs_0_), channel_id=1, source_target_pairs={{0,384},{8,392},{16,400},{24,408},{32,416},{40,424},{48,432},{56,4... | collective-permute-start | bytes 98312 | tf_op jit(solution)/shard_map/ppermute | solution.py:395
  36.6 13.8 %all_gather.9 = bf16[256,128]{1,0:T(8,128)(2,1)S(1)} all-gather(bf16[32,128]{1,0:T(8,128)(2,1)S(1)} %collective-permute-done), channel_id=1, replica_groups={{0,8,16,24,32,40,48,56},{64,72,80,88,96,104,112,120},{128,136,144,152,1..., dimensions={0}, use_global_device_ids=true | all-gather | bytes 73728 | tf_op jit(solution)/shard_map/all_gather | solution.py:380
  51.0 17.9 %all-to-all-done.halo_ref = bf16[64,128,128]{2,1,0:T(8,128)(2,1)S(1)} async-done(((bf16[64,128,128]{2,1,0:T(8,128)(2,1)}), bf16[64,128,128]{2,1,0:T(8,128)(2,1)S(1)}, u32[]{:S(2)}, u32[]{:S(2)}) %all-to-all-start) | async-done | bytes 2097184 | tf_op jit(solution)/shard_map/all_to_all | solution.py:390
  68.9 2.1 %first_mixture.1 = bf16[8,512,128]{2,1,0:T(8,128)(2,1)} custom-call(bf16[512,128]{1,0:T(8,128)(2,1)S(1)} %copy-done.2, bf16[64,128,128]{2,1,0:T(8,128)(2,1)S(1)} %all-to-all-done.halo_ref, bf16[4,10,128,128]{3,2,1,0:T(8,128)(2,1)S(1)} %copy-done, s32[4,10]{1,0:T(4,128)S(1)} %bitcast.20, s32[32]{0:T(128)S(1)} %bitcast.22), custom_call_target="tpu_custom_call" | custom-call | flops 170000000 | bytes 5242880 | tf_op jit(solution)/shard_map/first_mixture/pallas_call | solution.py:214
  71.6 8.1 %all-to-all-start.1 = ((bf16[8,512,128]{2,1,0:T(8,128)(2,1)}), bf16[8,512,128]{2,1,0:T(8,128)(2,1)S(1)}, u32[]{:S(2)}, u32[]{:S(2)}) async-start(bf16[8,512,128]{2,1,0:T(8,128)(2,1)} %first_mixture.1), calls=%async_computation.1 | async-start | bytes 2097152 | tf_op jit(solution)/shard_map/all_to_all | solution.py:390
  79.7 21.0 %all-gather = bf16[2048,128]{1,0:T(8,128)(2,1)S(1)} all-gather(bf16[256,128]{1,0:T(8,128)(2,1)S(1)} %bitcast.25), channel_id=2, replica_groups={{0,64,128,192,256,320,384,448},{8,72,136,200,264,328,392,456},{16,80,14..., dimensions={0}, use_global_device_ids=true | all-gather | bytes 589824 | tf_op jit(solution)/shard_map/all_gather | solution.py:386
  100.7 8.2 %all-to-all-done.1.parts_ref = bf16[8,512,128]{2,1,0:T(8,128)(2,1)S(1)} async-done(((bf16[8,512,128]{2,1,0:T(8,128)(2,1)}), bf16[8,512,128]{2,1,0:T(8,128)(2,1)S(1)}, u32[]{:S(2)}, u32[]{:S(2)}) %all-to-all-start.1) | async-done | bytes 1048608 | tf_op jit(solution)/shard_map/all_to_all | solution.py:390
  110.2 3.5 %all-to-all-start.2 = ((bf16[4,512,128]{2,1,0:T(8,128)(2,1)}), bf16[4,512,128]{2,1,0:T(8,128)(2,1)S(1)}, u32[]{:S(2)}, u32[]{:S(2)}) async-start(bf16[4,512,128]{2,1,0:T(8,128)(2,1)} %hidden.1.hidden_ref), calls=%async_computation.2 | async-start | bytes 1048576 | tf_op jit(solution)/shard_map/all_to_all | solution.py:390
  115.0 1.9 %collective-permute-start.4 = (bf16[512,128]{1,0:T(8,128)(2,1)S(1)}, bf16[512,128]{1,0:T(8,128)(2,1)S(1)}, u32[]{:S(2)}, u32[]{:S(2)}) collective-permute-start(bf16[512,128]{1,0:T(8,128)(2,1)S(1)} %second_mixture.1.refs_2_), channel_id=1, source_target_pairs={{0,1},{1,2},{2,3},{3,4},{4,5},{5,6},{6,7},{7,0},{8,9},{9,10},{10,1... | collective-permute-start | bytes 393224 | tf_op jit(solution)/shard_map/ppermute | solution.py:395
  116.9 4.6 %collective-permute-start.5 = (bf16[512,128]{1,0:T(8,128)(2,1)S(1)}, bf16[512,128]{1,0:T(8,128)(2,1)S(1)}, u32[]{:S(2)}, u32[]{:S(2)}) collective-permute-start(bf16[512,128]{1,0:T(8,128)(2,1)S(1)} %second_mixture.1.refs_2_), channel_id=1, source_target_pairs={{0,7},{1,0},{2,1},{3,2},{4,3},{5,4},{6,5},{7,6},{8,15},{9,8},{10,9... | collective-permute-start | bytes 393224 | tf_op jit(solution)/shard_map/ppermute | solution.py:395
  123.4 4.7 %all-to-all-done.2.rows_ref = bf16[4,512,128]{2,1,0:T(8,128)(2,1)S(1)} async-done(((bf16[4,512,128]{2,1,0:T(8,128)(2,1)}), bf16[4,512,128]{2,1,0:T(8,128)(2,1)S(1)}, u32[]{:S(2)}, u32[]{:S(2)}) %all-to-all-start.2) | async-done | bytes 524320 | tf_op jit(solution)/shard_map/all_to_all | solution.py:390
  128.1 3.1 %pack_second.1 = bf16[16,4,128,128]{3,2,1,0:T(8,128)(2,1)} custom-call(s32[1]{0:T(128)} %bitcast.11.group_ref, bf16[4,512,128]{2,1,0:T(8,128)(2,1)S(1)} %all-to-all-done.2.rows_ref, bf16[4,32,128]{2,1,0:T(8,128)(2,1)S(1)} %copy-done.5, bf16[4,32,128]{2,1,0:T(8,128)(2,1)} %collective-permute-done.1.refs_1_, ...), custom_call_target="tpu_custom_call" | custom-call | flops 1073741824 | bytes 3145728 | tf_op jit(solution)/shard_map/pack_second/pallas_call | solution.py:151
  131.2 5.8 %all-to-all-start.3 = ((bf16[16,4,128,128]{3,2,1,0:T(8,128)(2,1)}), bf16[16,4,128,128]{3,2,1,0:T(8,128)(2,1)S(1)}, u32[]{:S(2)}, u32[]{:S(2)}) async-start(bf16[16,4,128,128]{3,2,1,0:T(8,128)(2,1)} %pack_second.1), calls=%async_computation.3 | async-start | bytes 4194304 | tf_op jit(solution)/shard_map/all_to_all | solution.py:390
  137.0 1.9 %collective-permute-start.6 = (bf16[512,128]{1,0:T(8,128)(2,1)S(1)}, bf16[512,128]{1,0:T(8,128)(2,1)S(1)}, u32[]{:S(2)}, u32[]{:S(2)}) collective-permute-start(bf16[512,128]{1,0:T(8,128)(2,1)S(1)} %collective-permute-done.4.refs_3_), channel_id=1, source_target_pairs={{0,3},{1,4},{2,5},{3,6},{4,7},{5,0},{6,1},{7,2},{8,11},{9,12},{10,... | collective-permute-start | bytes 393224 | tf_op jit(solution)/shard_map/ppermute | solution.py:395
  138.9 3.1 %collective-permute-start.7 = (bf16[512,128]{1,0:T(8,128)(2,1)S(1)}, bf16[512,128]{1,0:T(8,128)(2,1)S(1)}, u32[]{:S(2)}, u32[]{:S(2)}) collective-permute-start(bf16[512,128]{1,0:T(8,128)(2,1)S(1)} %collective-permute-done.4.refs_3_), channel_id=1, source_target_pairs={{0,2},{1,3},{2,4},{3,5},{4,6},{5,7},{6,0},{7,1},{8,10},{9,11},{10,... | collective-permute-start | bytes 393224 | tf_op jit(solution)/shard_map/ppermute | solution.py:395
  142.0 4.3 %collective-permute-start.8 = (bf16[512,128]{1,0:T(8,128)(2,1)S(1)}, bf16[512,128]{1,0:T(8,128)(2,1)S(1)}, u32[]{:S(2)}, u32[]{:S(2)}) collective-permute-start(bf16[512,128]{1,0:T(8,128)(2,1)S(1)} %collective-permute-done.5.refs_4_), channel_id=1, source_target_pairs={{0,6},{1,7},{2,0},{3,1},{4,2},{5,3},{6,4},{7,5},{8,14},{9,15},{10,... | collective-permute-start | bytes 393224 | tf_op jit(solution)/shard_map/ppermute | solution.py:395
  146.3 2.6 %collective-permute-start.9 = (bf16[512,128]{1,0:T(8,128)(2,1)S(1)}, bf16[512,128]{1,0:T(8,128)(2,1)S(1)}, u32[]{:S(2)}, u32[]{:S(2)}) collective-permute-start(bf16[512,128]{1,0:T(8,128)(2,1)S(1)} %collective-permute-done.4.refs_3_), channel_id=1, source_target_pairs={{0,1},{1,2},{2,3},{3,4},{4,5},{5,6},{6,7},{7,0},{8,9},{9,10},{10,1... | collective-permute-start | bytes 393224 | tf_op jit(solution)/shard_map/ppermute | solution.py:395
  149.0 3.9 %collective-permute-start.10 = (bf16[512,128]{1,0:T(8,128)(2,1)S(1)}, bf16[512,128]{1,0:T(8,128)(2,1)S(1)}, u32[]{:S(2)}, u32[]{:S(2)}) collective-permute-start(bf16[512,128]{1,0:T(8,128)(2,1)S(1)} %collective-permute-done.5.refs_4_), channel_id=1, source_target_pairs={{0,7},{1,0},{2,1},{3,2},{4,3},{5,4},{6,5},{7,6},{8,15},{9,8},{10,9... | collective-permute-start | bytes 393224 | tf_op jit(solution)/shard_map/ppermute | solution.py:395
  153.6 5.1 %collective-permute-done.9.refs_8_ = bf16[512,128]{1,0:T(8,128)(2,1)S(1)} collective-permute-done((bf16[512,128]{1,0:T(8,128)(2,1)S(1)}, bf16[512,128]{1,0:T(8,128)(2,1)S(1)}, u32[]{:S(2)}, u32[]{:S(2)}) %collective-permute-start.9) | collective-permute-done | bytes 131104 | tf_op jit(solution)/shard_map/ppermute | solution.py:395
  159.8 6.8 %all-to-all-done.3 = bf16[16,4,128,128]{3,2,1,0:T(8,128)(2,1)S(1)} async-done(((bf16[16,4,128,128]{3,2,1,0:T(8,128)(2,1)}), bf16[16,4,128,128]{3,2,1,0:T(8,128)(2,1)S(1)}, u32[]{:S(2)}, u32[]{:S(2)}) %all-to-all-start.3) | async-done | bytes 2097184 | tf_op jit(solution)/shard_map/all_to_all | solution.py:390
  (36 shorter events, 13.0 us)
Async XLA Ops:
  4.0 28.9 %copy-start.7 = (bf16[128,16]{0,1:T(8,128)(2,1)S(1)}, bf16[128,16]{0,1:T(8,128)(2,1)}, u32[]{:S(2)}) copy-start(bf16[128,16]{0,1:T(8,128)(2,1)} %param.11) | copy-start | bytes 12292
  4.0 28.9 %copy-start.8 = (bf16[128,16]{0,1:T(8,128)(2,1)S(1)}, bf16[128,16]{0,1:T(8,128)(2,1)}, u32[]{:S(2)}) copy-start(bf16[128,16]{0,1:T(8,128)(2,1)} %param.10) | copy-start | bytes 12292
  4.0 29.6 %copy-start = (bf16[4,10,128,128]{3,2,1,0:T(8,128)(2,1)S(1)}, bf16[4,10,128,128]{3,2,1,0:T(8,128)(2,1)}, u32[]{:S(2)}) copy-start(bf16[4,10,128,128]{3,2,1,0:T(8,128)(2,1)} %tiles_ref.5) | copy-start | bytes 3932164
  4.0 29.6 %copy-start.2 = (bf16[512,128]{1,0:T(8,128)(2,1)S(1)}, bf16[512,128]{1,0:T(8,128)(2,1)}, u32[]{:S(2)}) copy-start(bf16[512,128]{1,0:T(8,128)(2,1)} %first_ref.1) | copy-start | bytes 393220
  4.1 29.6 %copy-start.3 = (s32[1,4,10]{2,1,0:T(4,128)S(1)}, s32[1,4,10]{2,1,0:T(4,128)}, u32[]{:S(2)}) copy-start(s32[1,4,10]{2,1,0:T(4,128)} %param.13) | copy-start | bytes 484
  4.1 64.8 %all-to-all-start = ((bf16[64,128,128]{2,1,0:T(8,128)(2,1)}), bf16[64,128,128]{2,1,0:T(8,128)(2,1)S(1)}, u32[]{:S(2)}, u32[]{:S(2)}) async-start(bf16[64,128,128]{2,1,0:T(8,128)(2,1)} %get-tuple-element.24), calls=%async_computation | async-start | bytes 4194304 | tf_op jit(solution)/shard_map/all_to_all | solution.py:390
  18.3 50.5 %copy-start.4 = (s32[1,32]{1,0:T(1,128)S(1)}, s32[1,32]{1,0:T(1,128)}, u32[]{:S(2)}) copy-start(s32[1,32]{1,0:T(1,128)} %param.14) | copy-start | bytes 388
  18.4 52.7 %collective-permute-start.1 = (bf16[4,32,128]{2,1,0:T(8,128)(2,1)}, bf16[4,32,128]{2,1,0:T(8,128)(2,1)}, u32[]{:S(2)}, u32[]{:S(2)}) collective-permute-start(bf16[4,32,128]{2,1,0:T(8,128)(2,1)} %get-tuple-element.33.refs_0_), channel_id=1, source_target_pairs={{0,128},{8,136},{16,144},{24,152},{32,160},{40,168},{48,176},{56,1... | collective-permute-start | bytes 98312 | tf_op jit(solution)/shard_map/ppermute | solution.py:395
  22.4 49.2 %collective-permute-start.2 = (bf16[4,32,128]{2,1,0:T(8,128)(2,1)}, bf16[4,32,128]{2,1,0:T(8,128)(2,1)}, u32[]{:S(2)}, u32[]{:S(2)}) collective-permute-start(bf16[4,32,128]{2,1,0:T(8,128)(2,1)} %get-tuple-element.33.refs_0_), channel_id=1, source_target_pairs={{0,256},{8,264},{16,272},{24,280},{32,288},{40,296},{48,304},{56,3... | collective-permute-start | bytes 98312 | tf_op jit(solution)/shard_map/ppermute | solution.py:395
  27.8 43.8 %collective-permute-start.3 = (bf16[4,32,128]{2,1,0:T(8,128)(2,1)}, bf16[4,32,128]{2,1,0:T(8,128)(2,1)}, u32[]{:S(2)}, u32[]{:S(2)}) collective-permute-start(bf16[4,32,128]{2,1,0:T(8,128)(2,1)} %get-tuple-element.33.refs_0_), channel_id=1, source_target_pairs={{0,384},{8,392},{16,400},{24,408},{32,416},{40,424},{48,432},{56,4... | collective-permute-start | bytes 98312 | tf_op jit(solution)/shard_map/ppermute | solution.py:395
  32.9 3.6 %collective-permute-start = (bf16[32,128]{1,0:T(8,128)(2,1)S(1)}, bf16[32,128]{1,0:T(8,128)(2,1)S(1)}, u32[]{:S(2)}, u32[]{:S(2)}) collective-permute-start(bf16[32,128]{1,0:T(8,128)(2,1)S(1)} %pad_maximum_fusion), channel_id=1, source_target_pairs={{0,0},{1,64},{2,128},{3,192},{4,256},{5,320},{6,384},{7,448},{8,8}... | collective-permute-start | bytes 24584 | tf_op jit(solution)/shard_map/ppermute | solution.py:378
  33.6 1.2 copy-start.1
  71.0 8.7 %copy-start.6 = (bf16[2,8,16,128]{3,2,1,0:T(8,128)(2,1)S(1)}, bf16[2,8,16,128]{3,2,1,0:T(8,128)(2,1)}, u32[]{:S(2)}) copy-start(bf16[2,8,16,128]{3,2,1,0:T(8,128)(2,1)} %copy.11) | copy-start | bytes 196612
  71.6 37.3 %all-to-all-start.1 = ((bf16[8,512,128]{2,1,0:T(8,128)(2,1)}), bf16[8,512,128]{2,1,0:T(8,128)(2,1)S(1)}, u32[]{:S(2)}, u32[]{:S(2)}) async-start(bf16[8,512,128]{2,1,0:T(8,128)(2,1)} %first_mixture.1), calls=%async_computation.1 | async-start | bytes 2097152 | tf_op jit(solution)/shard_map/all_to_all | solution.py:390
  110.2 17.9 %copy-start.5 = (bf16[4,32,128]{2,1,0:T(8,128)(2,1)S(1)}, bf16[4,32,128]{2,1,0:T(8,128)(2,1)}, u32[]{:S(2)}) copy-start(bf16[4,32,128]{2,1,0:T(8,128)(2,1)} %get-tuple-element.33.refs_0_) | copy-start | bytes 98308
  110.2 17.9 %all-to-all-start.2 = ((bf16[4,512,128]{2,1,0:T(8,128)(2,1)}), bf16[4,512,128]{2,1,0:T(8,128)(2,1)S(1)}, u32[]{:S(2)}, u32[]{:S(2)}) async-start(bf16[4,512,128]{2,1,0:T(8,128)(2,1)} %hidden.1.hidden_ref), calls=%async_computation.2 | async-start | bytes 1048576 | tf_op jit(solution)/shard_map/all_to_all | solution.py:390
  115.0 7.7 %collective-permute-start.4 = (bf16[512,128]{1,0:T(8,128)(2,1)S(1)}, bf16[512,128]{1,0:T(8,128)(2,1)S(1)}, u32[]{:S(2)}, u32[]{:S(2)}) collective-permute-start(bf16[512,128]{1,0:T(8,128)(2,1)S(1)} %second_mixture.1.refs_2_), channel_id=1, source_target_pairs={{0,1},{1,2},{2,3},{3,4},{4,5},{5,6},{6,7},{7,0},{8,9},{9,10},{10,1... | collective-permute-start | bytes 393224 | tf_op jit(solution)/shard_map/ppermute | solution.py:395
  116.9 6.5 %collective-permute-start.5 = (bf16[512,128]{1,0:T(8,128)(2,1)S(1)}, bf16[512,128]{1,0:T(8,128)(2,1)S(1)}, u32[]{:S(2)}, u32[]{:S(2)}) collective-permute-start(bf16[512,128]{1,0:T(8,128)(2,1)S(1)} %second_mixture.1.refs_2_), channel_id=1, source_target_pairs={{0,7},{1,0},{2,1},{3,2},{4,3},{5,4},{6,5},{7,6},{8,15},{9,8},{10,9... | collective-permute-start | bytes 393224 | tf_op jit(solution)/shard_map/ppermute | solution.py:395
  131.2 35.3 %all-to-all-start.3 = ((bf16[16,4,128,128]{3,2,1,0:T(8,128)(2,1)}), bf16[16,4,128,128]{3,2,1,0:T(8,128)(2,1)S(1)}, u32[]{:S(2)}, u32[]{:S(2)}) async-start(bf16[16,4,128,128]{3,2,1,0:T(8,128)(2,1)} %pack_second.1), calls=%async_computation.3 | async-start | bytes 4194304 | tf_op jit(solution)/shard_map/all_to_all | solution.py:390
  137.0 15.8 %collective-permute-start.6 = (bf16[512,128]{1,0:T(8,128)(2,1)S(1)}, bf16[512,128]{1,0:T(8,128)(2,1)S(1)}, u32[]{:S(2)}, u32[]{:S(2)}) collective-permute-start(bf16[512,128]{1,0:T(8,128)(2,1)S(1)} %collective-permute-done.4.refs_3_), channel_id=1, source_target_pairs={{0,3},{1,4},{2,5},{3,6},{4,7},{5,0},{6,1},{7,2},{8,11},{9,12},{10,... | collective-permute-start | bytes 393224 | tf_op jit(solution)/shard_map/ppermute | solution.py:395
  138.9 14.7 %collective-permute-start.7 = (bf16[512,128]{1,0:T(8,128)(2,1)S(1)}, bf16[512,128]{1,0:T(8,128)(2,1)S(1)}, u32[]{:S(2)}, u32[]{:S(2)}) collective-permute-start(bf16[512,128]{1,0:T(8,128)(2,1)S(1)} %collective-permute-done.4.refs_3_), channel_id=1, source_target_pairs={{0,2},{1,3},{2,4},{3,5},{4,6},{5,7},{6,0},{7,1},{8,10},{9,11},{10,... | collective-permute-start | bytes 393224 | tf_op jit(solution)/shard_map/ppermute | solution.py:395
  142.0 11.6 %collective-permute-start.8 = (bf16[512,128]{1,0:T(8,128)(2,1)S(1)}, bf16[512,128]{1,0:T(8,128)(2,1)S(1)}, u32[]{:S(2)}, u32[]{:S(2)}) collective-permute-start(bf16[512,128]{1,0:T(8,128)(2,1)S(1)} %collective-permute-done.5.refs_4_), channel_id=1, source_target_pairs={{0,6},{1,7},{2,0},{3,1},{4,2},{5,3},{6,4},{7,5},{8,14},{9,15},{10,... | collective-permute-start | bytes 393224 | tf_op jit(solution)/shard_map/ppermute | solution.py:395
  146.3 12.3 %collective-permute-start.9 = (bf16[512,128]{1,0:T(8,128)(2,1)S(1)}, bf16[512,128]{1,0:T(8,128)(2,1)S(1)}, u32[]{:S(2)}, u32[]{:S(2)}) collective-permute-start(bf16[512,128]{1,0:T(8,128)(2,1)S(1)} %collective-permute-done.4.refs_3_), channel_id=1, source_target_pairs={{0,1},{1,2},{2,3},{3,4},{4,5},{5,6},{6,7},{7,0},{8,9},{9,10},{10,1... | collective-permute-start | bytes 393224 | tf_op jit(solution)/shard_map/ppermute | solution.py:395
  149.0 9.7 %collective-permute-start.10 = (bf16[512,128]{1,0:T(8,128)(2,1)S(1)}, bf16[512,128]{1,0:T(8,128)(2,1)S(1)}, u32[]{:S(2)}, u32[]{:S(2)}) collective-permute-start(bf16[512,128]{1,0:T(8,128)(2,1)S(1)} %collective-permute-done.5.refs_4_), channel_id=1, source_target_pairs={{0,7},{1,0},{2,1},{3,2},{4,3},{5,4},{6,5},{7,6},{8,15},{9,8},{10,9... | collective-permute-start | bytes 393224 | tf_op jit(solution)/shard_map/ppermute | solution.py:395

commit v4 on v3

--- a/solution.py
+++ b/solution.py
@@ -126,7 +126,7 @@
     targets, _, slots, width = blocks_ref.shape
     half = rows_ref.shape[1] // 2
     own = group_ref[0]
-    places = [ref[own].astype(f32) for ref in index_refs]
+    places = [ref[...].astype(f32) for ref in index_refs]
     low = turned(jnp.concatenate([place[:targets] for place in places], axis=0))
     high = turned(jnp.concatenate([place[targets:] for place in places], axis=0))
     sources = [lax.rem(own + groups - k, groups) for k in range(groups)]
@@ -194,17 +194,20 @@
 
 def first_kernel(local_ref, halo_ref, tiles_ref, sources_ref, peers_ref, out_ref, rounded_ref, sems):
     size = tiles_ref.shape[2]
-    for i in range(tiles_ref.shape[0]):
+    blocks = tiles_ref.shape[0]
+    copies = []
+    for i in range(blocks):
         total = local_sum(tiles_ref, sources_ref, local_ref, i)
         total = total + halo_sum(tiles_ref, sources_ref, lambda j: halo_ref[peers_ref[j]], i)
         rows = pl.ds(i * size, size)
         mixed = (1.0 - alpha_mix) * total + alpha_mix * local_ref[rows, :].astype(f32)
         rounded_ref[rows, :] = mixed.astype(bf16)
-    copies = [
-        pltpu.make_async_copy(rounded_ref, out_ref.at[g], sems.at[g]) for g in range(out_ref.shape[0])
-    ]
-    for copy in copies:
-        copy.start()
+        if i % 2 == 1:
+            ready = pl.ds((i - 1) * size, 2 * size)
+            for g in range(out_ref.shape[0]):
+                copy = pltpu.make_async_copy(rounded_ref.at[ready], out_ref.at[g, ready], sems.at[i // 2, g])
+                copy.start()
+                copies.append(copy)
     for copy in copies:
         copy.wait()
 
@@ -216,7 +219,7 @@
         in_specs=[vmem] * 3 + [smem] * 2,
         out_specs=pl.BlockSpec(memory_space=pltpu.HBM),
         out_shape=pltpu.HBM((copies, count, width), bf16),
-        scratch_shapes=[pltpu.VMEM((count, width), bf16), pltpu.SemaphoreType.DMA((copies,))],
+        scratch_shapes=[pltpu.VMEM((count, width), bf16), pltpu.SemaphoreType.DMA((tiles.shape[0] // 2, copies))],
         compiler_params=params(),
         cost_estimate=cost(170 * 1000 * 1000, 5 * 1024 * 1024),
         name="first_mixture",
@@ -423,7 +426,10 @@
     leaving, index, w_first, w_second, stale = lax.optimization_barrier(
         (leaving, index, w_first, w_second, stale)
     )
-    index = [index] + [moved(index, "dom", k * near) for k in range(1, groups)]
+    index = [
+        lax.dynamic_index_in_dim(index, lax.rem(group[0] + k, groups), keepdims=False) for k in range(groups)
+    ]
+    index = index[:1] + [moved(index[k], "dom", k * near) for k in range(1, groups)]
     slab = slab_columns(w_first, w_second, feats)
     arrived = swap(leaving, "dom")
     stale_mixed = stale_mixture(first_layer, stale, tile_values, sources)
@@ -436,7 +442,6 @@
     spread_hidden = swap(hidden, "dom", far_groups)
     own = second_mixture(hidden, stale_mixed, tile_values, sources)
     before, after = moved(own, "feat", 1), moved(own, "feat", -1)
-    spread_hidden, before, after = lax.optimization_barrier((spread_hidden, before, after))
     blocks = pack_second(group, spread_hidden, index, near)
     blocks, before, after = lax.optimization_barrier((blocks, before, after))
     received = swap(blocks, "dom", near_groups).reshape((-1,) + blocks.shape[2:])

time: 169 us -> 168 us (level)
  waiting for transfers between devices: 45.8 us -> 35.3 us
  starting transfers between devices: 69.1 us -> 76.4 us
    all_to_all x4, waiting for transfers between devices: 37.5 us -> 30.7 us  [swap(): lax.all_to_all(blocks, axis, split_axis=0, concat_axis=0, axis_index_grou...]
    ppermute x10, starting transfers between devices: 36.8 us -> 42.3 us  [moved(): return lax.ppermute(rows, axis, [(i, (i + by) % size) for i in range(size)])]
    ppermute x10, waiting for transfers between devices: 8.29 us -> 4.61 us  [moved(): return lax.ppermute(rows, axis, [(i, (i + by) % size) for i in range(size)])]
  transfers between devices with their start and end apart: 15 -> 15, of which waited for: 9 -> 5; matrix products, arithmetic and copies ran while one was open for 0% -> 2% of each run, Pallas kernels for 4% -> 6%
where the time goes in v4:
time: 168 us; the launch traced here: 167 us
  starting transfers between devices  76.4 us (45%)
  waiting for transfers between devices  35.3 us (21%)
  blocking collectives  35.3 us (21%)
  Pallas kernels  15.6 us (9%)
  local copies, waits for them, and re-layouts  3.25 us (2%)
    ppermute x10, starting transfers between devices, moved(): return lax.ppermute(rows, axis, [(i, (i + by) % size) for i in range(size)])  42.3 us
    all_to_all x4, starting transfers between devices, swap(): lax.all_to_all(blocks, axis, split_axis=0, concat_axis=0, axis_index_grou...  32.3 us
    all_to_all x4, waiting for transfers between devices, swap(): lax.all_to_all(blocks, axis, split_axis=0, concat_axis=0, axis_index_grou...  30.7 us
    all_gather x1, blocking collectives, own_columns(): lax.all_gather(rows, 'dom', axis=0, tiled=False, axis_index_groups=columns)  21 us
    all_gather x1, blocking collectives, slab_columns(): lax.all_gather(both, 'dom', axis=0, tiled=True, axis_index_groups=slabs)  14.3 us
    ppermute x10, waiting for transfers between devices, moved(): return lax.ppermute(rows, axis, [(i, (i + by) % size) for i in range(size)])  4.61 us
    pallas_call x1, Pallas kernels, pack_first(): pl.pallas_call(pack_first_kernel, in_specs=[vmem] * 3, out_specs=[pl.Bloc...  3.37 us
  transfers between devices with their start and end apart: 15, of which 5 were waited for; matrix products, arithmetic and copies ran while one was open for 2% of the time, Pallas kernels for 6%

profile of v4, /device:TPU:7, one launch (start us, length us, event | category | flops | bytes accessed | tf_op | source)
XLA Modules:
  0.0 167.5 jit_solution(17586694255779393778)
XLA Ops:
  0.6 3.4 %pack_first.1 = (bf16[64,128,128]{2,1,0:T(8,128)(2,1)}, bf16[4,32,128]{2,1,0:T(8,128)(2,1)}) custom-call(bf16[512,128]{1,0:T(8,128)(2,1)} %first_ref.1, s32[64,128]{1,0:T(8,128)} %bitcast.37, s32[1,64]{1,0:T(1,128)} %counts_ref.1), custom_call_target="tpu_custom_call" | custom-call | flops 1073741824 | bytes 3145728 | tf_op jit(solution)/shard_map/pack_first/pallas_call | solution.py:107
  4.1 14.3 %all-to-all-start = ((bf16[64,128,128]{2,1,0:T(8,128)(2,1)}), bf16[64,128,128]{2,1,0:T(8,128)(2,1)S(1)}, u32[]{:S(2)}, u32[]{:S(2)}) async-start(bf16[64,128,128]{2,1,0:T(8,128)(2,1)} %get-tuple-element.21), calls=%async_computation | async-start | bytes 4194304 | tf_op jit(solution)/shard_map/all_to_all | solution.py:393
  19.0 1.9 %collective-permute-start = (bf16[32,128]{1,0:T(8,128)(2,1)}, bf16[32,128]{1,0:T(8,128)(2,1)}, u32[]{:S(2)}, u32[]{:S(2)}) collective-permute-start(bf16[32,128]{1,0:T(8,128)(2,1)} %pad_maximum_fusion), channel_id=1, source_target_pairs={{0,0},{1,64},{2,128},{3,192},{4,256},{5,320},{6,384},{7,448},{8,8}... | collective-permute-start | bytes 24584 | tf_op jit(solution)/shard_map/ppermute | solution.py:381
  22.3 6.3 %collective-permute-start.1 = (bf16[32,128]{1,0:T(8,128)(2,1)}, bf16[32,128]{1,0:T(8,128)(2,1)}, u32[]{:S(2)}, u32[]{:S(2)}) collective-permute-start(bf16[32,128]{1,0:T(8,128)(2,1)} %get-tuple-element.38), channel_id=1, source_target_pairs={{0,128},{8,136},{16,144},{24,152},{32,160},{40,168},{48,176},{56,1... | collective-permute-start | bytes 24584 | tf_op jit(solution)/shard_map/ppermute | solution.py:398
  28.6 8.2 %collective-permute-start.2 = (bf16[32,128]{1,0:T(8,128)(2,1)}, bf16[32,128]{1,0:T(8,128)(2,1)}, u32[]{:S(2)}, u32[]{:S(2)}) collective-permute-start(bf16[32,128]{1,0:T(8,128)(2,1)} %get-tuple-element.37), channel_id=1, source_target_pairs={{0,256},{8,264},{16,272},{24,280},{32,288},{40,296},{48,304},{56,3... | collective-permute-start | bytes 24584 | tf_op jit(solution)/shard_map/ppermute | solution.py:398
  36.8 5.5 %collective-permute-start.3 = (bf16[32,128]{1,0:T(8,128)(2,1)}, bf16[32,128]{1,0:T(8,128)(2,1)}, u32[]{:S(2)}, u32[]{:S(2)}) collective-permute-start(bf16[32,128]{1,0:T(8,128)(2,1)} %get-tuple-element.36), channel_id=1, source_target_pairs={{0,384},{8,392},{16,400},{24,408},{32,416},{40,424},{48,432},{56,4... | collective-permute-start | bytes 24584 | tf_op jit(solution)/shard_map/ppermute | solution.py:398
  45.2 14.3 %all_gather.9 = bf16[256,128]{1,0:T(8,128)(2,1)S(1)} all-gather(bf16[32,128]{1,0:T(8,128)(2,1)} %collective-permute-done), channel_id=1, replica_groups={{0,8,16,24,32,40,48,56},{64,72,80,88,96,104,112,120},{128,136,144,152,1..., dimensions={0}, use_global_device_ids=true | all-gather | bytes 73728 | tf_op jit(solution)/shard_map/all_gather | solution.py:383
  60.2 8.3 %all-to-all-done.halo_ref = bf16[64,128,128]{2,1,0:T(8,128)(2,1)S(1)} async-done(((bf16[64,128,128]{2,1,0:T(8,128)(2,1)}), bf16[64,128,128]{2,1,0:T(8,128)(2,1)S(1)}, u32[]{:S(2)}, u32[]{:S(2)}) %all-to-all-start) | async-done | bytes 2097184 | tf_op jit(solution)/shard_map/all_to_all | solution.py:393
  68.5 2.0 %first_mixture.1 = bf16[8,512,128]{2,1,0:T(8,128)(2,1)} custom-call(bf16[512,128]{1,0:T(8,128)(2,1)S(1)} %copy-done.2, bf16[64,128,128]{2,1,0:T(8,128)(2,1)S(1)} %all-to-all-done.halo_ref, bf16[4,10,128,128]{3,2,1,0:T(8,128)(2,1)S(1)} %copy-done, s32[4,10]{1,0:T(4,128)S(1)} %bitcast.28, s32[32]{0:T(128)S(1)} %bitcast.30), custom_call_target="tpu_custom_call" | custom-call | flops 170000000 | bytes 5242880 | tf_op jit(solution)/shard_map/first_mixture/pallas_call | solution.py:217
  70.5 8.7 %all-to-all-start.1 = ((bf16[8,512,128]{2,1,0:T(8,128)(2,1)}), bf16[8,512,128]{2,1,0:T(8,128)(2,1)S(1)}, u32[]{:S(2)}, u32[]{:S(2)}) async-start(bf16[8,512,128]{2,1,0:T(8,128)(2,1)} %first_mixture.1), calls=%async_computation.1 | async-start | bytes 2097152 | tf_op jit(solution)/shard_map/all_to_all | solution.py:393
  79.2 21.0 %all-gather = bf16[2048,128]{1,0:T(8,128)(2,1)S(1)} all-gather(bf16[256,128]{1,0:T(8,128)(2,1)S(1)} %bitcast.33), channel_id=2, replica_groups={{0,64,128,192,256,320,384,448},{8,72,136,200,264,328,392,456},{16,80,14..., dimensions={0}, use_global_device_ids=true | all-gather | bytes 589824 | tf_op jit(solution)/shard_map/all_gather | solution.py:389
  100.2 8.2 %all-to-all-done.1.parts_ref = bf16[8,512,128]{2,1,0:T(8,128)(2,1)S(1)} async-done(((bf16[8,512,128]{2,1,0:T(8,128)(2,1)}), bf16[8,512,128]{2,1,0:T(8,128)(2,1)S(1)}, u32[]{:S(2)}, u32[]{:S(2)}) %all-to-all-start.1) | async-done | bytes 1048608 | tf_op jit(solution)/shard_map/all_to_all | solution.py:393
  109.7 3.5 %all-to-all-start.2 = ((bf16[4,512,128]{2,1,0:T(8,128)(2,1)}), bf16[4,512,128]{2,1,0:T(8,128)(2,1)S(1)}, u32[]{:S(2)}, u32[]{:S(2)}) async-start(bf16[4,512,128]{2,1,0:T(8,128)(2,1)} %hidden.1.hidden_ref), calls=%async_computation.2 | async-start | bytes 1048576 | tf_op jit(solution)/shard_map/all_to_all | solution.py:393
  114.5 1.9 %collective-permute-start.4 = (bf16[512,128]{1,0:T(8,128)(2,1)S(1)}, bf16[512,128]{1,0:T(8,128)(2,1)S(1)}, u32[]{:S(2)}, u32[]{:S(2)}) collective-permute-start(bf16[512,128]{1,0:T(8,128)(2,1)S(1)} %second_mixture.1.refs_2_), channel_id=1, source_target_pairs={{0,1},{1,2},{2,3},{3,4},{4,5},{5,6},{6,7},{7,0},{8,9},{9,10},{10,1... | collective-permute-start | bytes 393224 | tf_op jit(solution)/shard_map/ppermute | solution.py:398
  116.4 4.6 %collective-permute-start.5 = (bf16[512,128]{1,0:T(8,128)(2,1)S(1)}, bf16[512,128]{1,0:T(8,128)(2,1)S(1)}, u32[]{:S(2)}, u32[]{:S(2)}) collective-permute-start(bf16[512,128]{1,0:T(8,128)(2,1)S(1)} %second_mixture.1.refs_2_), channel_id=1, source_target_pairs={{0,7},{1,0},{2,1},{3,2},{4,3},{5,4},{6,5},{7,6},{8,15},{9,8},{10,9... | collective-permute-start | bytes 393224 | tf_op jit(solution)/shard_map/ppermute | solution.py:398
  121.0 6.4 %all-to-all-done.2.rows_ref = bf16[4,512,128]{2,1,0:T(8,128)(2,1)S(1)} async-done(((bf16[4,512,128]{2,1,0:T(8,128)(2,1)}), bf16[4,512,128]{2,1,0:T(8,128)(2,1)S(1)}, u32[]{:S(2)}, u32[]{:S(2)}) %all-to-all-start.2) | async-done | bytes 524320 | tf_op jit(solution)/shard_map/all_to_all | solution.py:393
  127.4 3.1 %pack_second.1 = bf16[16,4,128,128]{3,2,1,0:T(8,128)(2,1)} custom-call(s32[1]{0:T(128)} %bitcast.15.group_ref, bf16[4,512,128]{2,1,0:T(8,128)(2,1)S(1)} %all-to-all-done.2.rows_ref, bf16[32,128]{1,0:T(8,128)(2,1)S(1)} %get-tuple-element.29.refs_0_, bf16[32,128]{1,0:T(8,128)(2,1)} %collective-permute-done.1.refs_1_, ...), custom_call_target="tpu_custom_call" | custom-call | flops 1073741824 | bytes 3145728 | tf_op jit(solution)/shard_map/pack_second/pallas_call | solution.py:151
  130.5 5.8 %all-to-all-start.3 = ((bf16[16,4,128,128]{3,2,1,0:T(8,128)(2,1)}), bf16[16,4,128,128]{3,2,1,0:T(8,128)(2,1)S(1)}, u32[]{:S(2)}, u32[]{:S(2)}) async-start(bf16[16,4,128,128]{3,2,1,0:T(8,128)(2,1)} %pack_second.1), calls=%async_computation.3 | async-start | bytes 4194304 | tf_op jit(solution)/shard_map/all_to_all | solution.py:393
  138.3 2.5 %collective-permute-start.7 = (bf16[512,128]{1,0:T(8,128)(2,1)S(1)}, bf16[512,128]{1,0:T(8,128)(2,1)S(1)}, u32[]{:S(2)}, u32[]{:S(2)}) collective-permute-start(bf16[512,128]{1,0:T(8,128)(2,1)S(1)} %collective-permute-done.4.refs_3_), channel_id=1, source_target_pairs={{0,2},{1,3},{2,4},{3,5},{4,6},{5,7},{6,0},{7,1},{8,10},{9,11},{10,... | collective-permute-start | bytes 393224 | tf_op jit(solution)/shard_map/ppermute | solution.py:398
  140.7 4.9 %collective-permute-start.8 = (bf16[512,128]{1,0:T(8,128)(2,1)S(1)}, bf16[512,128]{1,0:T(8,128)(2,1)S(1)}, u32[]{:S(2)}, u32[]{:S(2)}) collective-permute-start(bf16[512,128]{1,0:T(8,128)(2,1)S(1)} %collective-permute-done.5.refs_4_), channel_id=1, source_target_pairs={{0,6},{1,7},{2,0},{3,1},{4,2},{5,3},{6,4},{7,5},{8,14},{9,15},{10,... | collective-permute-start | bytes 393224 | tf_op jit(solution)/shard_map/ppermute | solution.py:398
  145.7 1.9 %collective-permute-start.9 = (bf16[512,128]{1,0:T(8,128)(2,1)S(1)}, bf16[512,128]{1,0:T(8,128)(2,1)S(1)}, u32[]{:S(2)}, u32[]{:S(2)}) collective-permute-start(bf16[512,128]{1,0:T(8,128)(2,1)S(1)} %collective-permute-done.4.refs_3_), channel_id=1, source_target_pairs={{0,1},{1,2},{2,3},{3,4},{4,5},{5,6},{6,7},{7,0},{8,9},{9,10},{10,1... | collective-permute-start | bytes 393224 | tf_op jit(solution)/shard_map/ppermute | solution.py:398
  147.6 4.6 %collective-permute-start.10 = (bf16[512,128]{1,0:T(8,128)(2,1)S(1)}, bf16[512,128]{1,0:T(8,128)(2,1)S(1)}, u32[]{:S(2)}, u32[]{:S(2)}) collective-permute-start(bf16[512,128]{1,0:T(8,128)(2,1)S(1)} %collective-permute-done.5.refs_4_), channel_id=1, source_target_pairs={{0,7},{1,0},{2,1},{3,2},{4,3},{5,4},{6,5},{7,6},{8,15},{9,8},{10,9... | collective-permute-start | bytes 393224 | tf_op jit(solution)/shard_map/ppermute | solution.py:398
  152.2 4.6 %collective-permute-done.9.refs_8_ = bf16[512,128]{1,0:T(8,128)(2,1)S(1)} collective-permute-done((bf16[512,128]{1,0:T(8,128)(2,1)S(1)}, bf16[512,128]{1,0:T(8,128)(2,1)S(1)}, u32[]{:S(2)}, u32[]{:S(2)}) %collective-permute-start.9) | collective-permute-done | bytes 131104 | tf_op jit(solution)/shard_map/ppermute | solution.py:398
  157.9 7.8 %all-to-all-done.3 = bf16[16,4,128,128]{3,2,1,0:T(8,128)(2,1)S(1)} async-done(((bf16[16,4,128,128]{3,2,1,0:T(8,128)(2,1)}), bf16[16,4,128,128]{3,2,1,0:T(8,128)(2,1)S(1)}, u32[]{:S(2)}, u32[]{:S(2)}) %all-to-all-start.3) | async-done | bytes 2097184 | tf_op jit(solution)/shard_map/all_to_all | solution.py:393
  (35 shorter events, 13.0 us)
Async XLA Ops:
  4.0 14.4 %copy-start.6 = (bf16[128,16]{0,1:T(8,128)(2,1)S(1)}, bf16[128,16]{0,1:T(8,128)(2,1)}, u32[]{:S(2)}) copy-start(bf16[128,16]{0,1:T(8,128)(2,1)} %param.11) | copy-start | bytes 12292
  4.0 14.3 %copy-start.7 = (bf16[128,16]{0,1:T(8,128)(2,1)S(1)}, bf16[128,16]{0,1:T(8,128)(2,1)}, u32[]{:S(2)}) copy-start(bf16[128,16]{0,1:T(8,128)(2,1)} %param.10) | copy-start | bytes 12292
  4.0 38.2 %copy-start = (bf16[4,10,128,128]{3,2,1,0:T(8,128)(2,1)S(1)}, bf16[4,10,128,128]{3,2,1,0:T(8,128)(2,1)}, u32[]{:S(2)}) copy-start(bf16[4,10,128,128]{3,2,1,0:T(8,128)(2,1)} %tiles_ref.5) | copy-start | bytes 3932164
  4.0 38.2 %copy-start.2 = (bf16[512,128]{1,0:T(8,128)(2,1)S(1)}, bf16[512,128]{1,0:T(8,128)(2,1)}, u32[]{:S(2)}) copy-start(bf16[512,128]{1,0:T(8,128)(2,1)} %first_ref.1) | copy-start | bytes 393220
  4.1 38.2 %copy-start.3 = (s32[1,4,10]{2,1,0:T(4,128)S(1)}, s32[1,4,10]{2,1,0:T(4,128)}, u32[]{:S(2)}) copy-start(s32[1,4,10]{2,1,0:T(4,128)} %param.13) | copy-start | bytes 484
  4.1 64.4 %all-to-all-start = ((bf16[64,128,128]{2,1,0:T(8,128)(2,1)}), bf16[64,128,128]{2,1,0:T(8,128)(2,1)S(1)}, u32[]{:S(2)}, u32[]{:S(2)}) async-start(bf16[64,128,128]{2,1,0:T(8,128)(2,1)} %get-tuple-element.21), calls=%async_computation | async-start | bytes 4194304 | tf_op jit(solution)/shard_map/all_to_all | solution.py:393
  18.3 50.1 %copy-start.4 = (s32[1,32]{1,0:T(1,128)S(1)}, s32[1,32]{1,0:T(1,128)}, u32[]{:S(2)}) copy-start(s32[1,32]{1,0:T(1,128)} %param.14) | copy-start | bytes 388
  19.0 26.2 %collective-permute-start = (bf16[32,128]{1,0:T(8,128)(2,1)}, bf16[32,128]{1,0:T(8,128)(2,1)}, u32[]{:S(2)}, u32[]{:S(2)}) collective-permute-start(bf16[32,128]{1,0:T(8,128)(2,1)} %pad_maximum_fusion), channel_id=1, source_target_pairs={{0,0},{1,64},{2,128},{3,192},{4,256},{5,320},{6,384},{7,448},{8,8}... | collective-permute-start | bytes 24584 | tf_op jit(solution)/shard_map/ppermute | solution.py:381
  22.3 48.2 %collective-permute-start.1 = (bf16[32,128]{1,0:T(8,128)(2,1)}, bf16[32,128]{1,0:T(8,128)(2,1)}, u32[]{:S(2)}, u32[]{:S(2)}) collective-permute-start(bf16[32,128]{1,0:T(8,128)(2,1)} %get-tuple-element.38), channel_id=1, source_target_pairs={{0,128},{8,136},{16,144},{24,152},{32,160},{40,168},{48,176},{56,1... | collective-permute-start | bytes 24584 | tf_op jit(solution)/shard_map/ppermute | solution.py:398
  28.6 41.9 %collective-permute-start.2 = (bf16[32,128]{1,0:T(8,128)(2,1)}, bf16[32,128]{1,0:T(8,128)(2,1)}, u32[]{:S(2)}, u32[]{:S(2)}) collective-permute-start(bf16[32,128]{1,0:T(8,128)(2,1)} %get-tuple-element.37), channel_id=1, source_target_pairs={{0,256},{8,264},{16,272},{24,280},{32,288},{40,296},{48,304},{56,3... | collective-permute-start | bytes 24584 | tf_op jit(solution)/shard_map/ppermute | solution.py:398
  36.8 33.7 %collective-permute-start.3 = (bf16[32,128]{1,0:T(8,128)(2,1)}, bf16[32,128]{1,0:T(8,128)(2,1)}, u32[]{:S(2)}, u32[]{:S(2)}) collective-permute-start(bf16[32,128]{1,0:T(8,128)(2,1)} %get-tuple-element.36), channel_id=1, source_target_pairs={{0,384},{8,392},{16,400},{24,408},{32,416},{40,424},{48,432},{56,4... | collective-permute-start | bytes 24584 | tf_op jit(solution)/shard_map/ppermute | solution.py:398
  42.3 1.2 copy-start.1
  70.5 8.7 %copy-start.5 = (bf16[2,8,16,128]{3,2,1,0:T(8,128)(2,1)S(1)}, bf16[2,8,16,128]{3,2,1,0:T(8,128)(2,1)}, u32[]{:S(2)}) copy-start(bf16[2,8,16,128]{3,2,1,0:T(8,128)(2,1)} %copy.11) | copy-start | bytes 196612
  70.5 37.9 %all-to-all-start.1 = ((bf16[8,512,128]{2,1,0:T(8,128)(2,1)}), bf16[8,512,128]{2,1,0:T(8,128)(2,1)S(1)}, u32[]{:S(2)}, u32[]{:S(2)}) async-start(bf16[8,512,128]{2,1,0:T(8,128)(2,1)} %first_mixture.1), calls=%async_computation.1 | async-start | bytes 2097152 | tf_op jit(solution)/shard_map/all_to_all | solution.py:393
  109.7 17.8 %all-to-all-start.2 = ((bf16[4,512,128]{2,1,0:T(8,128)(2,1)}), bf16[4,512,128]{2,1,0:T(8,128)(2,1)S(1)}, u32[]{:S(2)}, u32[]{:S(2)}) async-start(bf16[4,512,128]{2,1,0:T(8,128)(2,1)} %hidden.1.hidden_ref), calls=%async_computation.2 | async-start | bytes 1048576 | tf_op jit(solution)/shard_map/all_to_all | solution.py:393
  114.5 16.0 %collective-permute-start.4 = (bf16[512,128]{1,0:T(8,128)(2,1)S(1)}, bf16[512,128]{1,0:T(8,128)(2,1)S(1)}, u32[]{:S(2)}, u32[]{:S(2)}) collective-permute-start(bf16[512,128]{1,0:T(8,128)(2,1)S(1)} %second_mixture.1.refs_2_), channel_id=1, source_target_pairs={{0,1},{1,2},{2,3},{3,4},{4,5},{5,6},{6,7},{7,0},{8,9},{9,10},{10,1... | collective-permute-start | bytes 393224 | tf_op jit(solution)/shard_map/ppermute | solution.py:398
  116.4 14.1 %collective-permute-start.5 = (bf16[512,128]{1,0:T(8,128)(2,1)S(1)}, bf16[512,128]{1,0:T(8,128)(2,1)S(1)}, u32[]{:S(2)}, u32[]{:S(2)}) collective-permute-start(bf16[512,128]{1,0:T(8,128)(2,1)S(1)} %second_mixture.1.refs_2_), channel_id=1, source_target_pairs={{0,7},{1,0},{2,1},{3,2},{4,3},{5,4},{6,5},{7,6},{8,15},{9,8},{10,9... | collective-permute-start | bytes 393224 | tf_op jit(solution)/shard_map/ppermute | solution.py:398
  130.5 35.1 %all-to-all-start.3 = ((bf16[16,4,128,128]{3,2,1,0:T(8,128)(2,1)}), bf16[16,4,128,128]{3,2,1,0:T(8,128)(2,1)S(1)}, u32[]{:S(2)}, u32[]{:S(2)}) async-start(bf16[16,4,128,128]{3,2,1,0:T(8,128)(2,1)} %pack_second.1), calls=%async_computation.3 | async-start | bytes 4194304 | tf_op jit(solution)/shard_map/all_to_all | solution.py:393
  136.3 15.8 %collective-permute-start.6 = (bf16[512,128]{1,0:T(8,128)(2,1)S(1)}, bf16[512,128]{1,0:T(8,128)(2,1)S(1)}, u32[]{:S(2)}, u32[]{:S(2)}) collective-permute-start(bf16[512,128]{1,0:T(8,128)(2,1)S(1)} %collective-permute-done.4.refs_3_), channel_id=1, source_target_pairs={{0,3},{1,4},{2,5},{3,6},{4,7},{5,0},{6,1},{7,2},{8,11},{9,12},{10,... | collective-permute-start | bytes 393224 | tf_op jit(solution)/shard_map/ppermute | solution.py:398
  138.3 13.9 %collective-permute-start.7 = (bf16[512,128]{1,0:T(8,128)(2,1)S(1)}, bf16[512,128]{1,0:T(8,128)(2,1)S(1)}, u32[]{:S(2)}, u32[]{:S(2)}) collective-permute-start(bf16[512,128]{1,0:T(8,128)(2,1)S(1)} %collective-permute-done.4.refs_3_), channel_id=1, source_target_pairs={{0,2},{1,3},{2,4},{3,5},{4,6},{5,7},{6,0},{7,1},{8,10},{9,11},{10,... | collective-permute-start | bytes 393224 | tf_op jit(solution)/shard_map/ppermute | solution.py:398
  140.7 11.5 %collective-permute-start.8 = (bf16[512,128]{1,0:T(8,128)(2,1)S(1)}, bf16[512,128]{1,0:T(8,128)(2,1)S(1)}, u32[]{:S(2)}, u32[]{:S(2)}) collective-permute-start(bf16[512,128]{1,0:T(8,128)(2,1)S(1)} %collective-permute-done.5.refs_4_), channel_id=1, source_target_pairs={{0,6},{1,7},{2,0},{3,1},{4,2},{5,3},{6,4},{7,5},{8,14},{9,15},{10,... | collective-permute-start | bytes 393224 | tf_op jit(solution)/shard_map/ppermute | solution.py:398
  145.7 11.1 %collective-permute-start.9 = (bf16[512,128]{1,0:T(8,128)(2,1)S(1)}, bf16[512,128]{1,0:T(8,128)(2,1)S(1)}, u32[]{:S(2)}, u32[]{:S(2)}) collective-permute-start(bf16[512,128]{1,0:T(8,128)(2,1)S(1)} %collective-permute-done.4.refs_3_), channel_id=1, source_target_pairs={{0,1},{1,2},{2,3},{3,4},{4,5},{5,6},{6,7},{7,0},{8,9},{9,10},{10,1... | collective-permute-start | bytes 393224 | tf_op jit(solution)/shard_map/ppermute | solution.py:398
  147.6 9.2 %collective-permute-start.10 = (bf16[512,128]{1,0:T(8,128)(2,1)S(1)}, bf16[512,128]{1,0:T(8,128)(2,1)S(1)}, u32[]{:S(2)}, u32[]{:S(2)}) collective-permute-start(bf16[512,128]{1,0:T(8,128)(2,1)S(1)} %collective-permute-done.5.refs_4_), channel_id=1, source_target_pairs={{0,7},{1,0},{2,1},{3,2},{4,3},{5,4},{6,5},{7,6},{8,15},{9,8},{10,9... | collective-permute-start | bytes 393224 | tf_op jit(solution)/shard_map/ppermute | solution.py:398

commit v5 on v4

--- a/solution.py
+++ b/solution.py
@@ -120,23 +120,16 @@
     )(*in_hbm(rows, picks, counts))
 
 
-def pack_second_kernel(group_ref, rows_ref, *refs):
-    groups = rows_ref.shape[0]
-    index_refs, (out_ref, blocks_ref, sems) = refs[:groups], refs[groups:]
-    targets, _, slots, width = blocks_ref.shape
-    half = rows_ref.shape[1] // 2
-    own = group_ref[0]
-    places = [ref[...].astype(f32) for ref in index_refs]
-    low = turned(jnp.concatenate([place[:targets] for place in places], axis=0))
-    high = turned(jnp.concatenate([place[targets:] for place in places], axis=0))
-    sources = [lax.rem(own + groups - k, groups) for k in range(groups)]
-    folded = [fold_rows(rows_ref[source]) for source in sources]
-    pick = picker(half, slots, width)
+def pack_second_kernel(rows_ref, columns_ref, out_ref, blocks_ref, sems):
+    targets, groups, slots, width = blocks_ref.shape
+    low, high = columns_ref[0].astype(f32), columns_ref[1].astype(f32)
+    folded = [fold_rows(rows_ref[a]) for a in range(groups)]
+    pick = picker(rows_ref.shape[1] // 2, slots, width)
     copies = []
     for t in range(targets):
-        for k in range(groups):
-            c = k * targets + t
-            blocks_ref[t, sources[k]] = pick(folded[k], low[:, c : c + 1], high[:, c : c + 1])
+        for a in range(groups):
+            c = a * targets + t
+            blocks_ref[t, a] = pick(folded[a], low[:, c : c + 1], high[:, c : c + 1])
         if (t + 1) % GROUP == 0:
             span = pl.ds(t + 1 - GROUP, GROUP)
             copies.append(pltpu.make_async_copy(blocks_ref.at[span], out_ref.at[span], sems.at[t // GROUP]))
@@ -145,19 +138,19 @@
         copy.wait()
 
 
-def pack_second(group, rows, index, targets):
+def pack_second(rows, columns, targets):
     groups, count, width = rows.shape
     shape = (targets, groups, width, width)
     return pl.pallas_call(
         pack_second_kernel,
-        in_specs=[smem] + [vmem] * (1 + groups),
+        in_specs=[vmem] * 2,
         out_specs=pl.BlockSpec(memory_space=pltpu.HBM),
         out_shape=pltpu.HBM(shape, bf16),
         scratch_shapes=[pltpu.VMEM(shape, bf16), pltpu.SemaphoreType.DMA((shape[0] // GROUP,))],
         compiler_params=params(),
         cost_estimate=cost(2 * shape[0] * groups * width * count * width, 3 * 1024 * 1024),
         name="pack_second",
-    )(group, rows, *index)
+    )(rows, columns)
 
 
 def arrival(source, ranks, groups):
@@ -246,31 +239,46 @@
     )(first_rows, stale, tiles, sources)
 
 
-def second_kernel(hidden_ref, stale_ref, tiles_ref, sources_ref, rounded_ref):
+def second_kernel(sources_ref, group_ref, hidden_ref, stale_ref, tiles_ref, *refs):
+    index_refs, (rounded_ref, columns_ref, low_ref, high_ref) = refs[:-4], refs[-4:]
+    groups = len(index_refs)
+    targets = index_refs[0].shape[0] // 2
     size = tiles_ref.shape[2]
     for i in range(tiles_ref.shape[0]):
         rows = pl.ds(i * size, size)
         total = local_sum(tiles_ref, sources_ref, hidden_ref.at[0], i)
         rounded_ref[rows, :] = ((1.0 - alpha_mix) * total + stale_ref[rows, :]).astype(bf16)
-
-
-def second_mixture(hidden_copies, stale_mixed, tiles, sources):
+    for k, ref in enumerate(index_refs):
+        source = lax.rem(group_ref[0] + groups - k, groups)
+        span = pl.ds(pl.multiple_of(source * targets, targets), targets)
+        place = ref[...].astype(f32)
+        low_ref[span, :] = place[:targets]
+        high_ref[span, :] = place[targets:]
+    columns_ref[0] = turned(low_ref[...]).astype(bf16)
+    columns_ref[1] = turned(high_ref[...]).astype(bf16)
+
+
+def second_mixture(group, hidden_copies, stale_mixed, tiles, sources, index):
     shape = stale_mixed.shape
+    used = len(index) * index[0].shape[0] // 2
+    square = (2, shape[1], shape[1])
     return pl.pallas_call(
         second_kernel,
         grid=(1,),
-        in_specs=[
+        in_specs=[smem] * 2
+        + [
             pl.BlockSpec((1,) + shape, lambda g: (0, 0, 0)),
             pl.BlockSpec(shape, lambda g: (0, 0)),
             pl.BlockSpec((tiles.shape[0], 2) + tiles.shape[2:], lambda g: (0, 0, 0, 0)),
-            smem,
-        ],
-        out_specs=pl.BlockSpec(shape, lambda g: (0, 0)),
-        out_shape=jax.ShapeDtypeStruct(shape, bf16),
+        ]
+        + [pl.BlockSpec(index[0].shape, lambda g: (0, 0))] * len(index),
+        out_specs=[pl.BlockSpec(shape, lambda g: (0, 0)), pl.BlockSpec(square, lambda g: (0, 0, 0))],
+        out_shape=[jax.ShapeDtypeStruct(shape, bf16), jax.ShapeDtypeStruct(square, bf16)],
+        scratch_shapes=[pltpu.VMEM((used, shape[1]), f32)] * 2,
         compiler_params=params(),
         cost_estimate=cost(34 * 1000 * 1000, 2 * 1024 * 1024),
         name="second_mixture",
-    )(*in_hbm(hidden_copies, stale_mixed, tiles), sources)
+    )(sources, group, *in_hbm(hidden_copies, stale_mixed, tiles), *index)
 
 
 def columns_of(weight_ref, layer):
@@ -440,9 +448,9 @@
 
     hidden = hidden_copies(place, parts, weights, groups)
     spread_hidden = swap(hidden, "dom", far_groups)
-    own = second_mixture(hidden, stale_mixed, tile_values, sources)
+    own, columns = second_mixture(group, hidden, stale_mixed, tile_values, sources, index)
     before, after = moved(own, "feat", 1), moved(own, "feat", -1)
-    blocks = pack_second(group, spread_hidden, index, near)
+    blocks = pack_second(spread_hidden, columns, near)
     blocks, before, after = lax.optimization_barrier((blocks, before, after))
     received = swap(blocks, "dom", near_groups).reshape((-1,) + blocks.shape[2:])
     parts = {0: own, 1: before, -1: after}

time: 168 us -> 167 us (level)
  transfers between devices with their start and end apart: 15 -> 15, of which waited for: 5 -> 5; matrix products, arithmetic and copies ran while one was open for 2% -> 2% of each run, Pallas kernels for 6% -> 5%
where the time goes in v5:
time: 167 us
  starting transfers between devices  76.4 us (46%)
  waiting for transfers between devices  35.3 us (21%)
  blocking collectives  35.3 us (21%)
  Pallas kernels  14.7 us (9%)
  local copies, waits for them, and re-layouts  3.25 us (2%)
    ppermute x10, starting transfers between devices, moved(): return lax.ppermute(rows, axis, [(i, (i + by) % size) for i in range(size)])  42.3 us
    all_to_all x4, starting transfers between devices, swap(): lax.all_to_all(blocks, axis, split_axis=0, concat_axis=0, axis_index_grou...  32.3 us
    all_to_all x4, waiting for transfers between devices, swap(): lax.all_to_all(blocks, axis, split_axis=0, concat_axis=0, axis_index_grou...  30.7 us
    all_gather x1, blocking collectives, own_columns(): lax.all_gather(rows, 'dom', axis=0, tiled=False, axis_index_groups=columns)  21 us
    all_gather x1, blocking collectives, slab_columns(): lax.all_gather(both, 'dom', axis=0, tiled=True, axis_index_groups=slabs)  14.3 us
    ppermute x10, waiting for transfers between devices, moved(): return lax.ppermute(rows, axis, [(i, (i + by) % size) for i in range(size)])  4.61 us
    pallas_call x1, Pallas kernels, pack_first(): pl.pallas_call(pack_first_kernel, in_specs=[vmem] * 3, out_specs=[pl.Bloc...  3.37 us
  transfers between devices with their start and end apart: 15, of which 5 were waited for; matrix products, arithmetic and copies ran while one was open for 2% of the time, Pallas kernels for 5%

profile of v5, /device:TPU:7, one launch (start us, length us, event | category | flops | bytes accessed | tf_op | source)
XLA Modules:
  0.0 166.6 jit_solution(303206203707431403)
XLA Ops:
  0.6 3.4 %pack_first.1 = (bf16[64,128,128]{2,1,0:T(8,128)(2,1)}, bf16[4,32,128]{2,1,0:T(8,128)(2,1)}) custom-call(bf16[512,128]{1,0:T(8,128)(2,1)} %first_ref.1, s32[64,128]{1,0:T(8,128)} %bitcast.37, s32[1,64]{1,0:T(1,128)} %counts_ref.1), custom_call_target="tpu_custom_call" | custom-call | flops 1073741824 | bytes 3145728 | tf_op jit(solution)/shard_map/pack_first/pallas_call | solution.py:107
  4.1 14.3 %all-to-all-start = ((bf16[64,128,128]{2,1,0:T(8,128)(2,1)}), bf16[64,128,128]{2,1,0:T(8,128)(2,1)S(1)}, u32[]{:S(2)}, u32[]{:S(2)}) async-start(bf16[64,128,128]{2,1,0:T(8,128)(2,1)} %get-tuple-element.23), calls=%async_computation | async-start | bytes 4194304 | tf_op jit(solution)/shard_map/all_to_all | solution.py:401
  19.0 1.9 %collective-permute-start = (bf16[32,128]{1,0:T(8,128)(2,1)}, bf16[32,128]{1,0:T(8,128)(2,1)}, u32[]{:S(2)}, u32[]{:S(2)}) collective-permute-start(bf16[32,128]{1,0:T(8,128)(2,1)} %pad_maximum_fusion), channel_id=1, source_target_pairs={{0,0},{1,64},{2,128},{3,192},{4,256},{5,320},{6,384},{7,448},{8,8}... | collective-permute-start | bytes 24584 | tf_op jit(solution)/shard_map/ppermute | solution.py:389
  22.3 6.3 %collective-permute-start.1 = (bf16[32,128]{1,0:T(8,128)(2,1)}, bf16[32,128]{1,0:T(8,128)(2,1)}, u32[]{:S(2)}, u32[]{:S(2)}) collective-permute-start(bf16[32,128]{1,0:T(8,128)(2,1)} %get-tuple-element.42), channel_id=1, source_target_pairs={{0,128},{8,136},{16,144},{24,152},{32,160},{40,168},{48,176},{56,1... | collective-permute-start | bytes 24584 | tf_op jit(solution)/shard_map/ppermute | solution.py:406
  28.6 8.2 %collective-permute-start.2 = (bf16[32,128]{1,0:T(8,128)(2,1)}, bf16[32,128]{1,0:T(8,128)(2,1)}, u32[]{:S(2)}, u32[]{:S(2)}) collective-permute-start(bf16[32,128]{1,0:T(8,128)(2,1)} %get-tuple-element.41), channel_id=1, source_target_pairs={{0,256},{8,264},{16,272},{24,280},{32,288},{40,296},{48,304},{56,3... | collective-permute-start | bytes 24584 | tf_op jit(solution)/shard_map/ppermute | solution.py:406
  36.8 5.5 %collective-permute-start.3 = (bf16[32,128]{1,0:T(8,128)(2,1)}, bf16[32,128]{1,0:T(8,128)(2,1)}, u32[]{:S(2)}, u32[]{:S(2)}) collective-permute-start(bf16[32,128]{1,0:T(8,128)(2,1)} %get-tuple-element.40), channel_id=1, source_target_pairs={{0,384},{8,392},{16,400},{24,408},{32,416},{40,424},{48,432},{56,4... | collective-permute-start | bytes 24584 | tf_op jit(solution)/shard_map/ppermute | solution.py:406
  45.2 14.3 %all_gather.9 = bf16[256,128]{1,0:T(8,128)(2,1)S(1)} all-gather(bf16[32,128]{1,0:T(8,128)(2,1)} %collective-permute-done), channel_id=1, replica_groups={{0,8,16,24,32,40,48,56},{64,72,80,88,96,104,112,120},{128,136,144,152,1..., dimensions={0}, use_global_device_ids=true | all-gather | bytes 73728 | tf_op jit(solution)/shard_map/all_gather | solution.py:391
  60.2 8.3 %all-to-all-done.halo_ref = bf16[64,128,128]{2,1,0:T(8,128)(2,1)S(1)} async-done(((bf16[64,128,128]{2,1,0:T(8,128)(2,1)}), bf16[64,128,128]{2,1,0:T(8,128)(2,1)S(1)}, u32[]{:S(2)}, u32[]{:S(2)}) %all-to-all-start) | async-done | bytes 2097184 | tf_op jit(solution)/shard_map/all_to_all | solution.py:401
  68.5 2.0 %first_mixture.1 = bf16[8,512,128]{2,1,0:T(8,128)(2,1)} custom-call(bf16[512,128]{1,0:T(8,128)(2,1)S(1)} %copy-done.2, bf16[64,128,128]{2,1,0:T(8,128)(2,1)S(1)} %all-to-all-done.halo_ref, bf16[4,10,128,128]{3,2,1,0:T(8,128)(2,1)S(1)} %copy-done, s32[4,10]{1,0:T(4,128)S(1)} %bitcast.28, s32[32]{0:T(128)S(1)} %bitcast.30), custom_call_target="tpu_custom_call" | custom-call | flops 170000000 | bytes 5242880 | tf_op jit(solution)/shard_map/first_mixture/pallas_call | solution.py:210
  70.5 8.7 %all-to-all-start.1 = ((bf16[8,512,128]{2,1,0:T(8,128)(2,1)}), bf16[8,512,128]{2,1,0:T(8,128)(2,1)S(1)}, u32[]{:S(2)}, u32[]{:S(2)}) async-start(bf16[8,512,128]{2,1,0:T(8,128)(2,1)} %first_mixture.1), calls=%async_computation.1 | async-start | bytes 2097152 | tf_op jit(solution)/shard_map/all_to_all | solution.py:401
  79.2 21.0 %all-gather = bf16[2048,128]{1,0:T(8,128)(2,1)S(1)} all-gather(bf16[256,128]{1,0:T(8,128)(2,1)S(1)} %bitcast.33), channel_id=2, replica_groups={{0,64,128,192,256,320,384,448},{8,72,136,200,264,328,392,456},{16,80,14..., dimensions={0}, use_global_device_ids=true | all-gather | bytes 589824 | tf_op jit(solution)/shard_map/all_gather | solution.py:397
  100.2 8.2 %all-to-all-done.1.parts_ref = bf16[8,512,128]{2,1,0:T(8,128)(2,1)S(1)} async-done(((bf16[8,512,128]{2,1,0:T(8,128)(2,1)}), bf16[8,512,128]{2,1,0:T(8,128)(2,1)S(1)}, u32[]{:S(2)}, u32[]{:S(2)}) %all-to-all-start.1) | async-done | bytes 1048608 | tf_op jit(solution)/shard_map/all_to_all | solution.py:401
  109.7 3.5 %all-to-all-start.2 = ((bf16[4,512,128]{2,1,0:T(8,128)(2,1)}), bf16[4,512,128]{2,1,0:T(8,128)(2,1)S(1)}, u32[]{:S(2)}, u32[]{:S(2)}) async-start(bf16[4,512,128]{2,1,0:T(8,128)(2,1)} %hidden.1.hidden_ref), calls=%async_computation.2 | async-start | bytes 1048576 | tf_op jit(solution)/shard_map/all_to_all | solution.py:401
  114.5 1.9 %collective-permute-start.4 = (bf16[512,128]{1,0:T(8,128)(2,1)S(1)}, bf16[512,128]{1,0:T(8,128)(2,1)S(1)}, u32[]{:S(2)}, u32[]{:S(2)}) collective-permute-start(bf16[512,128]{1,0:T(8,128)(2,1)S(1)} %get-tuple-element.35.refs_2_), channel_id=1, source_target_pairs={{0,1},{1,2},{2,3},{3,4},{4,5},{5,6},{6,7},{7,0},{8,9},{9,10},{10,1... | collective-permute-start | bytes 393224 | tf_op jit(solution)/shard_map/ppermute | solution.py:406
  116.4 4.6 %collective-permute-start.5 = (bf16[512,128]{1,0:T(8,128)(2,1)S(1)}, bf16[512,128]{1,0:T(8,128)(2,1)S(1)}, u32[]{:S(2)}, u32[]{:S(2)}) collective-permute-start(bf16[512,128]{1,0:T(8,128)(2,1)S(1)} %get-tuple-element.35.refs_2_), channel_id=1, source_target_pairs={{0,7},{1,0},{2,1},{3,2},{4,3},{5,4},{6,5},{7,6},{8,15},{9,8},{10,9... | collective-permute-start | bytes 393224 | tf_op jit(solution)/shard_map/ppermute | solution.py:406
  121.0 6.4 %all-to-all-done.2.rows_ref = bf16[4,512,128]{2,1,0:T(8,128)(2,1)S(1)} async-done(((bf16[4,512,128]{2,1,0:T(8,128)(2,1)}), bf16[4,512,128]{2,1,0:T(8,128)(2,1)S(1)}, u32[]{:S(2)}, u32[]{:S(2)}) %all-to-all-start.2) | async-done | bytes 524320 | tf_op jit(solution)/shard_map/all_to_all | solution.py:401
  127.5 2.2 %pack_second.1 = bf16[16,4,128,128]{3,2,1,0:T(8,128)(2,1)} custom-call(bf16[4,512,128]{2,1,0:T(8,128)(2,1)S(1)} %all-to-all-done.2.rows_ref, bf16[2,128,128]{2,1,0:T(8,128)(2,1)S(1)} %get-tuple-element.36.columns_ref), custom_call_target="tpu_custom_call" | custom-call | flops 1073741824 | bytes 3145728 | tf_op jit(solution)/shard_map/pack_second/pallas_call | solution.py:144
  129.7 5.8 %all-to-all-start.3 = ((bf16[16,4,128,128]{3,2,1,0:T(8,128)(2,1)}), bf16[16,4,128,128]{3,2,1,0:T(8,128)(2,1)S(1)}, u32[]{:S(2)}, u32[]{:S(2)}) async-start(bf16[16,4,128,128]{3,2,1,0:T(8,128)(2,1)} %pack_second.1), calls=%async_computation.3 | async-start | bytes 4194304 | tf_op jit(solution)/shard_map/all_to_all | solution.py:401
  137.4 2.5 %collective-permute-start.7 = (bf16[512,128]{1,0:T(8,128)(2,1)S(1)}, bf16[512,128]{1,0:T(8,128)(2,1)S(1)}, u32[]{:S(2)}, u32[]{:S(2)}) collective-permute-start(bf16[512,128]{1,0:T(8,128)(2,1)S(1)} %collective-permute-done.4.refs_3_), channel_id=1, source_target_pairs={{0,2},{1,3},{2,4},{3,5},{4,6},{5,7},{6,0},{7,1},{8,10},{9,11},{10,... | collective-permute-start | bytes 393224 | tf_op jit(solution)/shard_map/ppermute | solution.py:406
  139.9 4.9 %collective-permute-start.8 = (bf16[512,128]{1,0:T(8,128)(2,1)S(1)}, bf16[512,128]{1,0:T(8,128)(2,1)S(1)}, u32[]{:S(2)}, u32[]{:S(2)}) collective-permute-start(bf16[512,128]{1,0:T(8,128)(2,1)S(1)} %collective-permute-done.5.refs_4_), channel_id=1, source_target_pairs={{0,6},{1,7},{2,0},{3,1},{4,2},{5,3},{6,4},{7,5},{8,14},{9,15},{10,... | collective-permute-start | bytes 393224 | tf_op jit(solution)/shard_map/ppermute | solution.py:406
  144.8 1.9 %collective-permute-start.9 = (bf16[512,128]{1,0:T(8,128)(2,1)S(1)}, bf16[512,128]{1,0:T(8,128)(2,1)S(1)}, u32[]{:S(2)}, u32[]{:S(2)}) collective-permute-start(bf16[512,128]{1,0:T(8,128)(2,1)S(1)} %collective-permute-done.4.refs_3_), channel_id=1, source_target_pairs={{0,1},{1,2},{2,3},{3,4},{4,5},{5,6},{6,7},{7,0},{8,9},{9,10},{10,1... | collective-permute-start | bytes 393224 | tf_op jit(solution)/shard_map/ppermute | solution.py:406
  146.7 4.6 %collective-permute-start.10 = (bf16[512,128]{1,0:T(8,128)(2,1)S(1)}, bf16[512,128]{1,0:T(8,128)(2,1)S(1)}, u32[]{:S(2)}, u32[]{:S(2)}) collective-permute-start(bf16[512,128]{1,0:T(8,128)(2,1)S(1)} %collective-permute-done.5.refs_4_), channel_id=1, source_target_pairs={{0,7},{1,0},{2,1},{3,2},{4,3},{5,4},{6,5},{7,6},{8,15},{9,8},{10,9... | collective-permute-start | bytes 393224 | tf_op jit(solution)/shard_map/ppermute | solution.py:406
  151.3 4.6 %collective-permute-done.9.refs_8_ = bf16[512,128]{1,0:T(8,128)(2,1)S(1)} collective-permute-done((bf16[512,128]{1,0:T(8,128)(2,1)S(1)}, bf16[512,128]{1,0:T(8,128)(2,1)S(1)}, u32[]{:S(2)}, u32[]{:S(2)}) %collective-permute-start.9) | collective-permute-done | bytes 131104 | tf_op jit(solution)/shard_map/ppermute | solution.py:406
  157.0 7.8 %all-to-all-done.3 = bf16[16,4,128,128]{3,2,1,0:T(8,128)(2,1)S(1)} async-done(((bf16[16,4,128,128]{3,2,1,0:T(8,128)(2,1)}), bf16[16,4,128,128]{3,2,1,0:T(8,128)(2,1)S(1)}, u32[]{:S(2)}, u32[]{:S(2)}) %all-to-all-start.3) | async-done | bytes 2097184 | tf_op jit(solution)/shard_map/all_to_all | solution.py:401
  (35 shorter events, 13.0 us)
Async XLA Ops:
  4.0 14.4 %copy-start.6 = (bf16[128,16]{0,1:T(8,128)(2,1)S(1)}, bf16[128,16]{0,1:T(8,128)(2,1)}, u32[]{:S(2)}) copy-start(bf16[128,16]{0,1:T(8,128)(2,1)} %param.11) | copy-start | bytes 12292
  4.0 14.3 %copy-start.7 = (bf16[128,16]{0,1:T(8,128)(2,1)S(1)}, bf16[128,16]{0,1:T(8,128)(2,1)}, u32[]{:S(2)}) copy-start(bf16[128,16]{0,1:T(8,128)(2,1)} %param.10) | copy-start | bytes 12292
  4.0 38.2 %copy-start = (bf16[4,10,128,128]{3,2,1,0:T(8,128)(2,1)S(1)}, bf16[4,10,128,128]{3,2,1,0:T(8,128)(2,1)}, u32[]{:S(2)}) copy-start(bf16[4,10,128,128]{3,2,1,0:T(8,128)(2,1)} %tiles_ref.5) | copy-start | bytes 3932164
  4.0 38.2 %copy-start.2 = (bf16[512,128]{1,0:T(8,128)(2,1)S(1)}, bf16[512,128]{1,0:T(8,128)(2,1)}, u32[]{:S(2)}) copy-start(bf16[512,128]{1,0:T(8,128)(2,1)} %first_ref.1) | copy-start | bytes 393220
  4.1 38.2 %copy-start.3 = (s32[1,4,10]{2,1,0:T(4,128)S(1)}, s32[1,4,10]{2,1,0:T(4,128)}, u32[]{:S(2)}) copy-start(s32[1,4,10]{2,1,0:T(4,128)} %param.13) | copy-start | bytes 484
  4.1 64.4 %all-to-all-start = ((bf16[64,128,128]{2,1,0:T(8,128)(2,1)}), bf16[64,128,128]{2,1,0:T(8,128)(2,1)S(1)}, u32[]{:S(2)}, u32[]{:S(2)}) async-start(bf16[64,128,128]{2,1,0:T(8,128)(2,1)} %get-tuple-element.23), calls=%async_computation | async-start | bytes 4194304 | tf_op jit(solution)/shard_map/all_to_all | solution.py:401
  18.3 50.1 %copy-start.4 = (s32[1,32]{1,0:T(1,128)S(1)}, s32[1,32]{1,0:T(1,128)}, u32[]{:S(2)}) copy-start(s32[1,32]{1,0:T(1,128)} %param.14) | copy-start | bytes 388
  19.0 26.2 %collective-permute-start = (bf16[32,128]{1,0:T(8,128)(2,1)}, bf16[32,128]{1,0:T(8,128)(2,1)}, u32[]{:S(2)}, u32[]{:S(2)}) collective-permute-start(bf16[32,128]{1,0:T(8,128)(2,1)} %pad_maximum_fusion), channel_id=1, source_target_pairs={{0,0},{1,64},{2,128},{3,192},{4,256},{5,320},{6,384},{7,448},{8,8}... | collective-permute-start | bytes 24584 | tf_op jit(solution)/shard_map/ppermute | solution.py:389
  22.3 48.2 %collective-permute-start.1 = (bf16[32,128]{1,0:T(8,128)(2,1)}, bf16[32,128]{1,0:T(8,128)(2,1)}, u32[]{:S(2)}, u32[]{:S(2)}) collective-permute-start(bf16[32,128]{1,0:T(8,128)(2,1)} %get-tuple-element.42), channel_id=1, source_target_pairs={{0,128},{8,136},{16,144},{24,152},{32,160},{40,168},{48,176},{56,1... | collective-permute-start | bytes 24584 | tf_op jit(solution)/shard_map/ppermute | solution.py:406
  28.6 41.9 %collective-permute-start.2 = (bf16[32,128]{1,0:T(8,128)(2,1)}, bf16[32,128]{1,0:T(8,128)(2,1)}, u32[]{:S(2)}, u32[]{:S(2)}) collective-permute-start(bf16[32,128]{1,0:T(8,128)(2,1)} %get-tuple-element.41), channel_id=1, source_target_pairs={{0,256},{8,264},{16,272},{24,280},{32,288},{40,296},{48,304},{56,3... | collective-permute-start | bytes 24584 | tf_op jit(solution)/shard_map/ppermute | solution.py:406
  36.8 33.7 %collective-permute-start.3 = (bf16[32,128]{1,0:T(8,128)(2,1)}, bf16[32,128]{1,0:T(8,128)(2,1)}, u32[]{:S(2)}, u32[]{:S(2)}) collective-permute-start(bf16[32,128]{1,0:T(8,128)(2,1)} %get-tuple-element.40), channel_id=1, source_target_pairs={{0,384},{8,392},{16,400},{24,408},{32,416},{40,424},{48,432},{56,4... | collective-permute-start | bytes 24584 | tf_op jit(solution)/shard_map/ppermute | solution.py:406
  42.3 1.2 copy-start.1
  70.5 8.7 %copy-start.5 = (bf16[2,8,16,128]{3,2,1,0:T(8,128)(2,1)S(1)}, bf16[2,8,16,128]{3,2,1,0:T(8,128)(2,1)}, u32[]{:S(2)}) copy-start(bf16[2,8,16,128]{3,2,1,0:T(8,128)(2,1)} %copy.11) | copy-start | bytes 196612
  70.5 37.9 %all-to-all-start.1 = ((bf16[8,512,128]{2,1,0:T(8,128)(2,1)}), bf16[8,512,128]{2,1,0:T(8,128)(2,1)S(1)}, u32[]{:S(2)}, u32[]{:S(2)}) async-start(bf16[8,512,128]{2,1,0:T(8,128)(2,1)} %first_mixture.1), calls=%async_computation.1 | async-start | bytes 2097152 | tf_op jit(solution)/shard_map/all_to_all | solution.py:401
  109.7 17.8 %all-to-all-start.2 = ((bf16[4,512,128]{2,1,0:T(8,128)(2,1)}), bf16[4,512,128]{2,1,0:T(8,128)(2,1)S(1)}, u32[]{:S(2)}, u32[]{:S(2)}) async-start(bf16[4,512,128]{2,1,0:T(8,128)(2,1)} %hidden.1.hidden_ref), calls=%async_computation.2 | async-start | bytes 1048576 | tf_op jit(solution)/shard_map/all_to_all | solution.py:401
  114.5 15.1 %collective-permute-start.4 = (bf16[512,128]{1,0:T(8,128)(2,1)S(1)}, bf16[512,128]{1,0:T(8,128)(2,1)S(1)}, u32[]{:S(2)}, u32[]{:S(2)}) collective-permute-start(bf16[512,128]{1,0:T(8,128)(2,1)S(1)} %get-tuple-element.35.refs_2_), channel_id=1, source_target_pairs={{0,1},{1,2},{2,3},{3,4},{4,5},{5,6},{6,7},{7,0},{8,9},{9,10},{10,1... | collective-permute-start | bytes 393224 | tf_op jit(solution)/shard_map/ppermute | solution.py:406
  116.4 13.2 %collective-permute-start.5 = (bf16[512,128]{1,0:T(8,128)(2,1)S(1)}, bf16[512,128]{1,0:T(8,128)(2,1)S(1)}, u32[]{:S(2)}, u32[]{:S(2)}) collective-permute-start(bf16[512,128]{1,0:T(8,128)(2,1)S(1)} %get-tuple-element.35.refs_2_), channel_id=1, source_target_pairs={{0,7},{1,0},{2,1},{3,2},{4,3},{5,4},{6,5},{7,6},{8,15},{9,8},{10,9... | collective-permute-start | bytes 393224 | tf_op jit(solution)/shard_map/ppermute | solution.py:406
  129.7 35.1 %all-to-all-start.3 = ((bf16[16,4,128,128]{3,2,1,0:T(8,128)(2,1)}), bf16[16,4,128,128]{3,2,1,0:T(8,128)(2,1)S(1)}, u32[]{:S(2)}, u32[]{:S(2)}) async-start(bf16[16,4,128,128]{3,2,1,0:T(8,128)(2,1)} %pack_second.1), calls=%async_computation.3 | async-start | bytes 4194304 | tf_op jit(solution)/shard_map/all_to_all | solution.py:401
  135.5 15.8 %collective-permute-start.6 = (bf16[512,128]{1,0:T(8,128)(2,1)S(1)}, bf16[512,128]{1,0:T(8,128)(2,1)S(1)}, u32[]{:S(2)}, u32[]{:S(2)}) collective-permute-start(bf16[512,128]{1,0:T(8,128)(2,1)S(1)} %collective-permute-done.4.refs_3_), channel_id=1, source_target_pairs={{0,3},{1,4},{2,5},{3,6},{4,7},{5,0},{6,1},{7,2},{8,11},{9,12},{10,... | collective-permute-start | bytes 393224 | tf_op jit(solution)/shard_map/ppermute | solution.py:406
  137.4 13.9 %collective-permute-start.7 = (bf16[512,128]{1,0:T(8,128)(2,1)S(1)}, bf16[512,128]{1,0:T(8,128)(2,1)S(1)}, u32[]{:S(2)}, u32[]{:S(2)}) collective-permute-start(bf16[512,128]{1,0:T(8,128)(2,1)S(1)} %collective-permute-done.4.refs_3_), channel_id=1, source_target_pairs={{0,2},{1,3},{2,4},{3,5},{4,6},{5,7},{6,0},{7,1},{8,10},{9,11},{10,... | collective-permute-start | bytes 393224 | tf_op jit(solution)/shard_map/ppermute | solution.py:406
  139.9 11.5 %collective-permute-start.8 = (bf16[512,128]{1,0:T(8,128)(2,1)S(1)}, bf16[512,128]{1,0:T(8,128)(2,1)S(1)}, u32[]{:S(2)}, u32[]{:S(2)}) collective-permute-start(bf16[512,128]{1,0:T(8,128)(2,1)S(1)} %collective-permute-done.5.refs_4_), channel_id=1, source_target_pairs={{0,6},{1,7},{2,0},{3,1},{4,2},{5,3},{6,4},{7,5},{8,14},{9,15},{10,... | collective-permute-start | bytes 393224 | tf_op jit(solution)/shard_map/ppermute | solution.py:406
  144.8 11.1 %collective-permute-start.9 = (bf16[512,128]{1,0:T(8,128)(2,1)S(1)}, bf16[512,128]{1,0:T(8,128)(2,1)S(1)}, u32[]{:S(2)}, u32[]{:S(2)}) collective-permute-start(bf16[512,128]{1,0:T(8,128)(2,1)S(1)} %collective-permute-done.4.refs_3_), channel_id=1, source_target_pairs={{0,1},{1,2},{2,3},{3,4},{4,5},{5,6},{6,7},{7,0},{8,9},{9,10},{10,1... | collective-permute-start | bytes 393224 | tf_op jit(solution)/shard_map/ppermute | solution.py:406
  146.7 9.2 %collective-permute-start.10 = (bf16[512,128]{1,0:T(8,128)(2,1)S(1)}, bf16[512,128]{1,0:T(8,128)(2,1)S(1)}, u32[]{:S(2)}, u32[]{:S(2)}) collective-permute-start(bf16[512,128]{1,0:T(8,128)(2,1)S(1)} %collective-permute-done.5.refs_4_), channel_id=1, source_target_pairs={{0,7},{1,0},{2,1},{3,2},{4,3},{5,4},{6,5},{7,6},{8,15},{9,8},{10,9... | collective-permute-start | bytes 393224 | tf_op jit(solution)/shard_map/ppermute | solution.py:406

commit v6 on v5

--- a/solution.py
+++ b/solution.py
@@ -393,8 +393,11 @@
 
 
 def own_columns(rows, feats):
-    columns = [[z * RANKS + r for z in range(feats)] for r in range(RANKS)]
-    return lax.all_gather(rows, "dom", axis=0, tiled=False, axis_index_groups=columns)
+    pairs = [[(z + e) * RANKS + r for e in (0, 1)] for z in range(0, feats, 2) for r in range(RANKS)]
+    strides = [[z * RANKS + r for z in range(e, feats, 2)] for e in (0, 1) for r in range(RANKS)]
+    both = lax.all_gather(rows, "dom", axis=0, tiled=True, axis_index_groups=pairs)
+    got = lax.all_gather(both, "dom", axis=0, tiled=True, axis_index_groups=strides)
+    return got.reshape(feats, -1, rows.shape[1])
 
 
 def swap(blocks, axis, groups=None):

time: 167 us -> 167 us (level)
  blocking collectives: 35.3 us -> 32.3 us
  waiting for transfers between devices: 35.3 us -> 38.3 us
    all_to_all x4, waiting for transfers between devices: 30.7 us -> 33.8 us  [swap(): lax.all_to_all(blocks, axis, split_axis=0, concat_axis=0, axis_index_grou...]
    all_gather x1 -> x2, blocking collectives: 21 us -> 17.9 us  [the longest x1 14.1 us: own_columns(): lax.all_gather(both, 'dom', axis=0, tiled=True, axis_index_groups=strides)]
where the time goes in v6:
time: 167 us
  starting transfers between devices  76.4 us (46%)
  waiting for transfers between devices  38.3 us (23%)
  blocking collectives  32.3 us (19%)
  Pallas kernels  14.7 us (9%)
  local copies, waits for them, and re-layouts  3.25 us (2%)
    ppermute x10, starting transfers between devices, moved(): return lax.ppermute(rows, axis, [(i, (i + by) % size) for i in range(size)])  42.3 us
    all_to_all x4, waiting for transfers between devices, swap(): lax.all_to_all(blocks, axis, split_axis=0, concat_axis=0, axis_index_grou...  33.8 us
    all_to_all x4, starting transfers between devices, swap(): lax.all_to_all(blocks, axis, split_axis=0, concat_axis=0, axis_index_grou...  32.3 us
    all_gather x1, blocking collectives, slab_columns(): lax.all_gather(both, 'dom', axis=0, tiled=True, axis_index_groups=slabs)  14.3 us
    all_gather x1, blocking collectives, own_columns(): lax.all_gather(both, 'dom', axis=0, tiled=True, axis_index_groups=strides)  14.1 us
    ppermute x10, waiting for transfers between devices, moved(): return lax.ppermute(rows, axis, [(i, (i + by) % size) for i in range(size)])  4.52 us
    all_gather x1, blocking collectives, own_columns(): lax.all_gather(rows, 'dom', axis=0, tiled=True, axis_index_groups=pairs)  3.79 us
    pallas_call x1, Pallas kernels, pack_first(): pl.pallas_call(pack_first_kernel, in_specs=[vmem] * 3, out_specs=[pl.Bloc...  3.37 us
  transfers between devices with their start and end apart: 15, of which 5 were waited for; matrix products, arithmetic and copies ran while one was open for 2% of the time, Pallas kernels for 5%

profile of v6, /device:TPU:7, one launch (start us, length us, event | category | flops | bytes accessed | tf_op | source)
XLA Modules:
  0.0 166.6 jit_solution(7905435697680866718)
XLA Ops:
  0.6 3.4 %pack_first.1 = (bf16[64,128,128]{2,1,0:T(8,128)(2,1)}, bf16[4,32,128]{2,1,0:T(8,128)(2,1)}) custom-call(bf16[512,128]{1,0:T(8,128)(2,1)} %first_ref.1, s32[64,128]{1,0:T(8,128)} %bitcast.37, s32[1,64]{1,0:T(1,128)} %counts_ref.1), custom_call_target="tpu_custom_call" | custom-call | flops 1073741824 | bytes 3145728 | tf_op jit(solution)/shard_map/pack_first/pallas_call | solution.py:107
  4.1 14.3 %all-to-all-start = ((bf16[64,128,128]{2,1,0:T(8,128)(2,1)}), bf16[64,128,128]{2,1,0:T(8,128)(2,1)S(1)}, u32[]{:S(2)}, u32[]{:S(2)}) async-start(bf16[64,128,128]{2,1,0:T(8,128)(2,1)} %get-tuple-element.23), calls=%async_computation | async-start | bytes 4194304 | tf_op jit(solution)/shard_map/all_to_all | solution.py:404
  19.0 1.9 %collective-permute-start = (bf16[32,128]{1,0:T(8,128)(2,1)}, bf16[32,128]{1,0:T(8,128)(2,1)}, u32[]{:S(2)}, u32[]{:S(2)}) collective-permute-start(bf16[32,128]{1,0:T(8,128)(2,1)} %pad_maximum_fusion), channel_id=1, source_target_pairs={{0,0},{1,64},{2,128},{3,192},{4,256},{5,320},{6,384},{7,448},{8,8}... | collective-permute-start | bytes 24584 | tf_op jit(solution)/shard_map/ppermute | solution.py:389
  22.3 6.3 %collective-permute-start.1 = (bf16[32,128]{1,0:T(8,128)(2,1)}, bf16[32,128]{1,0:T(8,128)(2,1)}, u32[]{:S(2)}, u32[]{:S(2)}) collective-permute-start(bf16[32,128]{1,0:T(8,128)(2,1)} %get-tuple-element.42), channel_id=1, source_target_pairs={{0,128},{8,136},{16,144},{24,152},{32,160},{40,168},{48,176},{56,1... | collective-permute-start | bytes 24584 | tf_op jit(solution)/shard_map/ppermute | solution.py:409
  28.6 8.2 %collective-permute-start.2 = (bf16[32,128]{1,0:T(8,128)(2,1)}, bf16[32,128]{1,0:T(8,128)(2,1)}, u32[]{:S(2)}, u32[]{:S(2)}) collective-permute-start(bf16[32,128]{1,0:T(8,128)(2,1)} %get-tuple-element.41), channel_id=1, source_target_pairs={{0,256},{8,264},{16,272},{24,280},{32,288},{40,296},{48,304},{56,3... | collective-permute-start | bytes 24584 | tf_op jit(solution)/shard_map/ppermute | solution.py:409
  36.8 5.5 %collective-permute-start.3 = (bf16[32,128]{1,0:T(8,128)(2,1)}, bf16[32,128]{1,0:T(8,128)(2,1)}, u32[]{:S(2)}, u32[]{:S(2)}) collective-permute-start(bf16[32,128]{1,0:T(8,128)(2,1)} %get-tuple-element.40), channel_id=1, source_target_pairs={{0,384},{8,392},{16,400},{24,408},{32,416},{40,424},{48,432},{56,4... | collective-permute-start | bytes 24584 | tf_op jit(solution)/shard_map/ppermute | solution.py:409
  45.2 14.3 %all_gather.9 = bf16[256,128]{1,0:T(8,128)(2,1)S(1)} all-gather(bf16[32,128]{1,0:T(8,128)(2,1)} %collective-permute-done), channel_id=1, replica_groups={{0,8,16,24,32,40,48,56},{64,72,80,88,96,104,112,120},{128,136,144,152,1..., dimensions={0}, use_global_device_ids=true | all-gather | bytes 73728 | tf_op jit(solution)/shard_map/all_gather | solution.py:391
  60.2 8.3 %all-to-all-done.halo_ref = bf16[64,128,128]{2,1,0:T(8,128)(2,1)S(1)} async-done(((bf16[64,128,128]{2,1,0:T(8,128)(2,1)}), bf16[64,128,128]{2,1,0:T(8,128)(2,1)S(1)}, u32[]{:S(2)}, u32[]{:S(2)}) %all-to-all-start) | async-done | bytes 2097184 | tf_op jit(solution)/shard_map/all_to_all | solution.py:404
  68.5 2.0 %first_mixture.1 = bf16[8,512,128]{2,1,0:T(8,128)(2,1)} custom-call(bf16[512,128]{1,0:T(8,128)(2,1)S(1)} %copy-done.2, bf16[64,128,128]{2,1,0:T(8,128)(2,1)S(1)} %all-to-all-done.halo_ref, bf16[4,10,128,128]{3,2,1,0:T(8,128)(2,1)S(1)} %copy-done, s32[4,10]{1,0:T(4,128)S(1)} %bitcast.28, s32[32]{0:T(128)S(1)} %bitcast.30), custom_call_target="tpu_custom_call" | custom-call | flops 170000000 | bytes 5242880 | tf_op jit(solution)/shard_map/first_mixture/pallas_call | solution.py:210
  70.5 8.7 %all-to-all-start.1 = ((bf16[8,512,128]{2,1,0:T(8,128)(2,1)}), bf16[8,512,128]{2,1,0:T(8,128)(2,1)S(1)}, u32[]{:S(2)}, u32[]{:S(2)}) async-start(bf16[8,512,128]{2,1,0:T(8,128)(2,1)} %first_mixture.1), calls=%async_computation.1 | async-start | bytes 2097152 | tf_op jit(solution)/shard_map/all_to_all | solution.py:404
  79.2 3.8 %all_gather.10 = bf16[512,128]{1,0:T(8,128)(2,1)S(1)} all-gather(bf16[256,128]{1,0:T(8,128)(2,1)S(1)} %bitcast.33), channel_id=1, replica_groups={{0,64},{8,72},{16,80},{24,88},{32,96},{40,104},{48,112},{56,120},{128,1..., dimensions={0}, use_global_device_ids=true | all-gather | bytes 196608 | tf_op jit(solution)/shard_map/all_gather | solution.py:398
  83.0 14.1 %all_gather.11 = bf16[2048,128]{1,0:T(8,128)(2,1)S(1)} all-gather(bf16[512,128]{1,0:T(8,128)(2,1)S(1)} %all_gather.10), channel_id=1, replica_groups={{0,128,256,384},{8,136,264,392},{16,144,272,400},{24,152,280,408},{32,1..., dimensions={0}, use_global_device_ids=true | all-gather | bytes 655360 | tf_op jit(solution)/shard_map/all_gather | solution.py:399
  97.1 11.3 %all-to-all-done.1.parts_ref = bf16[8,512,128]{2,1,0:T(8,128)(2,1)S(1)} async-done(((bf16[8,512,128]{2,1,0:T(8,128)(2,1)}), bf16[8,512,128]{2,1,0:T(8,128)(2,1)S(1)}, u32[]{:S(2)}, u32[]{:S(2)}) %all-to-all-start.1) | async-done | bytes 1048608 | tf_op jit(solution)/shard_map/all_to_all | solution.py:404
  109.7 3.5 %all-to-all-start.2 = ((bf16[4,512,128]{2,1,0:T(8,128)(2,1)}), bf16[4,512,128]{2,1,0:T(8,128)(2,1)S(1)}, u32[]{:S(2)}, u32[]{:S(2)}) async-start(bf16[4,512,128]{2,1,0:T(8,128)(2,1)} %hidden.1.hidden_ref), calls=%async_computation.2 | async-start | bytes 1048576 | tf_op jit(solution)/shard_map/all_to_all | solution.py:404
  114.5 1.9 %collective-permute-start.4 = (bf16[512,128]{1,0:T(8,128)(2,1)S(1)}, bf16[512,128]{1,0:T(8,128)(2,1)S(1)}, u32[]{:S(2)}, u32[]{:S(2)}) collective-permute-start(bf16[512,128]{1,0:T(8,128)(2,1)S(1)} %get-tuple-element.35.refs_2_), channel_id=1, source_target_pairs={{0,1},{1,2},{2,3},{3,4},{4,5},{5,6},{6,7},{7,0},{8,9},{9,10},{10,1... | collective-permute-start | bytes 393224 | tf_op jit(solution)/shard_map/ppermute | solution.py:409
  116.4 4.6 %collective-permute-start.5 = (bf16[512,128]{1,0:T(8,128)(2,1)S(1)}, bf16[512,128]{1,0:T(8,128)(2,1)S(1)}, u32[]{:S(2)}, u32[]{:S(2)}) collective-permute-start(bf16[512,128]{1,0:T(8,128)(2,1)S(1)} %get-tuple-element.35.refs_2_), channel_id=1, source_target_pairs={{0,7},{1,0},{2,1},{3,2},{4,3},{5,4},{6,5},{7,6},{8,15},{9,8},{10,9... | collective-permute-start | bytes 393224 | tf_op jit(solution)/shard_map/ppermute | solution.py:409
  121.0 6.4 %all-to-all-done.2.rows_ref = bf16[4,512,128]{2,1,0:T(8,128)(2,1)S(1)} async-done(((bf16[4,512,128]{2,1,0:T(8,128)(2,1)}), bf16[4,512,128]{2,1,0:T(8,128)(2,1)S(1)}, u32[]{:S(2)}, u32[]{:S(2)}) %all-to-all-start.2) | async-done | bytes 524320 | tf_op jit(solution)/shard_map/all_to_all | solution.py:404
  127.5 2.2 %pack_second.1 = bf16[16,4,128,128]{3,2,1,0:T(8,128)(2,1)} custom-call(bf16[4,512,128]{2,1,0:T(8,128)(2,1)S(1)} %all-to-all-done.2.rows_ref, bf16[2,128,128]{2,1,0:T(8,128)(2,1)S(1)} %get-tuple-element.36.columns_ref), custom_call_target="tpu_custom_call" | custom-call | flops 1073741824 | bytes 3145728 | tf_op jit(solution)/shard_map/pack_second/pallas_call | solution.py:144
  129.7 5.8 %all-to-all-start.3 = ((bf16[16,4,128,128]{3,2,1,0:T(8,128)(2,1)}), bf16[16,4,128,128]{3,2,1,0:T(8,128)(2,1)S(1)}, u32[]{:S(2)}, u32[]{:S(2)}) async-start(bf16[16,4,128,128]{3,2,1,0:T(8,128)(2,1)} %pack_second.1), calls=%async_computation.3 | async-start | bytes 4194304 | tf_op jit(solution)/shard_map/all_to_all | solution.py:404
  137.4 2.5 %collective-permute-start.7 = (bf16[512,128]{1,0:T(8,128)(2,1)S(1)}, bf16[512,128]{1,0:T(8,128)(2,1)S(1)}, u32[]{:S(2)}, u32[]{:S(2)}) collective-permute-start(bf16[512,128]{1,0:T(8,128)(2,1)S(1)} %collective-permute-done.4.refs_3_), channel_id=1, source_target_pairs={{0,2},{1,3},{2,4},{3,5},{4,6},{5,7},{6,0},{7,1},{8,10},{9,11},{10,... | collective-permute-start | bytes 393224 | tf_op jit(solution)/shard_map/ppermute | solution.py:409
  139.9 4.9 %collective-permute-start.8 = (bf16[512,128]{1,0:T(8,128)(2,1)S(1)}, bf16[512,128]{1,0:T(8,128)(2,1)S(1)}, u32[]{:S(2)}, u32[]{:S(2)}) collective-permute-start(bf16[512,128]{1,0:T(8,128)(2,1)S(1)} %collective-permute-done.5.refs_4_), channel_id=1, source_target_pairs={{0,6},{1,7},{2,0},{3,1},{4,2},{5,3},{6,4},{7,5},{8,14},{9,15},{10,... | collective-permute-start | bytes 393224 | tf_op jit(solution)/shard_map/ppermute | solution.py:409
  146.7 4.6 %collective-permute-start.10 = (bf16[512,128]{1,0:T(8,128)(2,1)S(1)}, bf16[512,128]{1,0:T(8,128)(2,1)S(1)}, u32[]{:S(2)}, u32[]{:S(2)}) collective-permute-start(bf16[512,128]{1,0:T(8,128)(2,1)S(1)} %collective-permute-done.5.refs_4_), channel_id=1, source_target_pairs={{0,7},{1,0},{2,1},{3,2},{4,3},{5,4},{6,5},{7,6},{8,15},{9,8},{10,9... | collective-permute-start | bytes 393224 | tf_op jit(solution)/shard_map/ppermute | solution.py:409
  151.3 4.5 %collective-permute-done.9.refs_8_ = bf16[512,128]{1,0:T(8,128)(2,1)S(1)} collective-permute-done((bf16[512,128]{1,0:T(8,128)(2,1)S(1)}, bf16[512,128]{1,0:T(8,128)(2,1)S(1)}, u32[]{:S(2)}, u32[]{:S(2)}) %collective-permute-start.9) | collective-permute-done | bytes 131104 | tf_op jit(solution)/shard_map/ppermute | solution.py:409
  156.9 7.9 %all-to-all-done.3 = bf16[16,4,128,128]{3,2,1,0:T(8,128)(2,1)S(1)} async-done(((bf16[16,4,128,128]{3,2,1,0:T(8,128)(2,1)}), bf16[16,4,128,128]{3,2,1,0:T(8,128)(2,1)S(1)}, u32[]{:S(2)}, u32[]{:S(2)}) %all-to-all-start.3) | async-done | bytes 2097184 | tf_op jit(solution)/shard_map/all_to_all | solution.py:404
  (36 shorter events, 14.9 us)
Async XLA Ops:
  4.0 14.4 %copy-start.6 = (bf16[128,16]{0,1:T(8,128)(2,1)S(1)}, bf16[128,16]{0,1:T(8,128)(2,1)}, u32[]{:S(2)}) copy-start(bf16[128,16]{0,1:T(8,128)(2,1)} %param.11) | copy-start | bytes 12292
  4.0 14.3 %copy-start.7 = (bf16[128,16]{0,1:T(8,128)(2,1)S(1)}, bf16[128,16]{0,1:T(8,128)(2,1)}, u32[]{:S(2)}) copy-start(bf16[128,16]{0,1:T(8,128)(2,1)} %param.10) | copy-start | bytes 12292
  4.0 38.2 %copy-start = (bf16[4,10,128,128]{3,2,1,0:T(8,128)(2,1)S(1)}, bf16[4,10,128,128]{3,2,1,0:T(8,128)(2,1)}, u32[]{:S(2)}) copy-start(bf16[4,10,128,128]{3,2,1,0:T(8,128)(2,1)} %tiles_ref.5) | copy-start | bytes 3932164
  4.0 38.2 %copy-start.2 = (bf16[512,128]{1,0:T(8,128)(2,1)S(1)}, bf16[512,128]{1,0:T(8,128)(2,1)}, u32[]{:S(2)}) copy-start(bf16[512,128]{1,0:T(8,128)(2,1)} %first_ref.1) | copy-start | bytes 393220
  4.1 38.2 %copy-start.3 = (s32[1,4,10]{2,1,0:T(4,128)S(1)}, s32[1,4,10]{2,1,0:T(4,128)}, u32[]{:S(2)}) copy-start(s32[1,4,10]{2,1,0:T(4,128)} %param.13) | copy-start | bytes 484
  4.1 64.4 %all-to-all-start = ((bf16[64,128,128]{2,1,0:T(8,128)(2,1)}), bf16[64,128,128]{2,1,0:T(8,128)(2,1)S(1)}, u32[]{:S(2)}, u32[]{:S(2)}) async-start(bf16[64,128,128]{2,1,0:T(8,128)(2,1)} %get-tuple-element.23), calls=%async_computation | async-start | bytes 4194304 | tf_op jit(solution)/shard_map/all_to_all | solution.py:404
  18.3 50.1 %copy-start.4 = (s32[1,32]{1,0:T(1,128)S(1)}, s32[1,32]{1,0:T(1,128)}, u32[]{:S(2)}) copy-start(s32[1,32]{1,0:T(1,128)} %param.14) | copy-start | bytes 388
  19.0 26.2 %collective-permute-start = (bf16[32,128]{1,0:T(8,128)(2,1)}, bf16[32,128]{1,0:T(8,128)(2,1)}, u32[]{:S(2)}, u32[]{:S(2)}) collective-permute-start(bf16[32,128]{1,0:T(8,128)(2,1)} %pad_maximum_fusion), channel_id=1, source_target_pairs={{0,0},{1,64},{2,128},{3,192},{4,256},{5,320},{6,384},{7,448},{8,8}... | collective-permute-start | bytes 24584 | tf_op jit(solution)/shard_map/ppermute | solution.py:389
  22.3 48.2 %collective-permute-start.1 = (bf16[32,128]{1,0:T(8,128)(2,1)}, bf16[32,128]{1,0:T(8,128)(2,1)}, u32[]{:S(2)}, u32[]{:S(2)}) collective-permute-start(bf16[32,128]{1,0:T(8,128)(2,1)} %get-tuple-element.42), channel_id=1, source_target_pairs={{0,128},{8,136},{16,144},{24,152},{32,160},{40,168},{48,176},{56,1... | collective-permute-start | bytes 24584 | tf_op jit(solution)/shard_map/ppermute | solution.py:409
  28.6 41.9 %collective-permute-start.2 = (bf16[32,128]{1,0:T(8,128)(2,1)}, bf16[32,128]{1,0:T(8,128)(2,1)}, u32[]{:S(2)}, u32[]{:S(2)}) collective-permute-start(bf16[32,128]{1,0:T(8,128)(2,1)} %get-tuple-element.41), channel_id=1, source_target_pairs={{0,256},{8,264},{16,272},{24,280},{32,288},{40,296},{48,304},{56,3... | collective-permute-start | bytes 24584 | tf_op jit(solution)/shard_map/ppermute | solution.py:409
  36.8 33.7 %collective-permute-start.3 = (bf16[32,128]{1,0:T(8,128)(2,1)}, bf16[32,128]{1,0:T(8,128)(2,1)}, u32[]{:S(2)}, u32[]{:S(2)}) collective-permute-start(bf16[32,128]{1,0:T(8,128)(2,1)} %get-tuple-element.40), channel_id=1, source_target_pairs={{0,384},{8,392},{16,400},{24,408},{32,416},{40,424},{48,432},{56,4... | collective-permute-start | bytes 24584 | tf_op jit(solution)/shard_map/ppermute | solution.py:409
  42.3 1.2 copy-start.1
  70.5 8.7 %copy-start.5 = (bf16[2,8,16,128]{3,2,1,0:T(8,128)(2,1)S(1)}, bf16[2,8,16,128]{3,2,1,0:T(8,128)(2,1)}, u32[]{:S(2)}) copy-start(bf16[2,8,16,128]{3,2,1,0:T(8,128)(2,1)} %copy.11) | copy-start | bytes 196612
  70.5 37.9 %all-to-all-start.1 = ((bf16[8,512,128]{2,1,0:T(8,128)(2,1)}), bf16[8,512,128]{2,1,0:T(8,128)(2,1)S(1)}, u32[]{:S(2)}, u32[]{:S(2)}) async-start(bf16[8,512,128]{2,1,0:T(8,128)(2,1)} %first_mixture.1), calls=%async_computation.1 | async-start | bytes 2097152 | tf_op jit(solution)/shard_map/all_to_all | solution.py:404
  109.7 17.8 %all-to-all-start.2 = ((bf16[4,512,128]{2,1,0:T(8,128)(2,1)}), bf16[4,512,128]{2,1,0:T(8,128)(2,1)S(1)}, u32[]{:S(2)}, u32[]{:S(2)}) async-start(bf16[4,512,128]{2,1,0:T(8,128)(2,1)} %hidden.1.hidden_ref), calls=%async_computation.2 | async-start | bytes 1048576 | tf_op jit(solution)/shard_map/all_to_all | solution.py:404
  114.5 15.1 %collective-permute-start.4 = (bf16[512,128]{1,0:T(8,128)(2,1)S(1)}, bf16[512,128]{1,0:T(8,128)(2,1)S(1)}, u32[]{:S(2)}, u32[]{:S(2)}) collective-permute-start(bf16[512,128]{1,0:T(8,128)(2,1)S(1)} %get-tuple-element.35.refs_2_), channel_id=1, source_target_pairs={{0,1},{1,2},{2,3},{3,4},{4,5},{5,6},{6,7},{7,0},{8,9},{9,10},{10,1... | collective-permute-start | bytes 393224 | tf_op jit(solution)/shard_map/ppermute | solution.py:409
  116.4 13.2 %collective-permute-start.5 = (bf16[512,128]{1,0:T(8,128)(2,1)S(1)}, bf16[512,128]{1,0:T(8,128)(2,1)S(1)}, u32[]{:S(2)}, u32[]{:S(2)}) collective-permute-start(bf16[512,128]{1,0:T(8,128)(2,1)S(1)} %get-tuple-element.35.refs_2_), channel_id=1, source_target_pairs={{0,7},{1,0},{2,1},{3,2},{4,3},{5,4},{6,5},{7,6},{8,15},{9,8},{10,9... | collective-permute-start | bytes 393224 | tf_op jit(solution)/shard_map/ppermute | solution.py:409
  129.7 35.1 %all-to-all-start.3 = ((bf16[16,4,128,128]{3,2,1,0:T(8,128)(2,1)}), bf16[16,4,128,128]{3,2,1,0:T(8,128)(2,1)S(1)}, u32[]{:S(2)}, u32[]{:S(2)}) async-start(bf16[16,4,128,128]{3,2,1,0:T(8,128)(2,1)} %pack_second.1), calls=%async_computation.3 | async-start | bytes 4194304 | tf_op jit(solution)/shard_map/all_to_all | solution.py:404
  135.5 15.8 %collective-permute-start.6 = (bf16[512,128]{1,0:T(8,128)(2,1)S(1)}, bf16[512,128]{1,0:T(8,128)(2,1)S(1)}, u32[]{:S(2)}, u32[]{:S(2)}) collective-permute-start(bf16[512,128]{1,0:T(8,128)(2,1)S(1)} %collective-permute-done.4.refs_3_), channel_id=1, source_target_pairs={{0,3},{1,4},{2,5},{3,6},{4,7},{5,0},{6,1},{7,2},{8,11},{9,12},{10,... | collective-permute-start | bytes 393224 | tf_op jit(solution)/shard_map/ppermute | solution.py:409
  137.4 13.9 %collective-permute-start.7 = (bf16[512,128]{1,0:T(8,128)(2,1)S(1)}, bf16[512,128]{1,0:T(8,128)(2,1)S(1)}, u32[]{:S(2)}, u32[]{:S(2)}) collective-permute-start(bf16[512,128]{1,0:T(8,128)(2,1)S(1)} %collective-permute-done.4.refs_3_), channel_id=1, source_target_pairs={{0,2},{1,3},{2,4},{3,5},{4,6},{5,7},{6,0},{7,1},{8,10},{9,11},{10,... | collective-permute-start | bytes 393224 | tf_op jit(solution)/shard_map/ppermute | solution.py:409
  139.9 11.4 %collective-permute-start.8 = (bf16[512,128]{1,0:T(8,128)(2,1)S(1)}, bf16[512,128]{1,0:T(8,128)(2,1)S(1)}, u32[]{:S(2)}, u32[]{:S(2)}) collective-permute-start(bf16[512,128]{1,0:T(8,128)(2,1)S(1)} %collective-permute-done.5.refs_4_), channel_id=1, source_target_pairs={{0,6},{1,7},{2,0},{3,1},{4,2},{5,3},{6,4},{7,5},{8,14},{9,15},{10,... | collective-permute-start | bytes 393224 | tf_op jit(solution)/shard_map/ppermute | solution.py:409
  144.8 11.0 %collective-permute-start.9 = (bf16[512,128]{1,0:T(8,128)(2,1)S(1)}, bf16[512,128]{1,0:T(8,128)(2,1)S(1)}, u32[]{:S(2)}, u32[]{:S(2)}) collective-permute-start(bf16[512,128]{1,0:T(8,128)(2,1)S(1)} %collective-permute-done.4.refs_3_), channel_id=1, source_target_pairs={{0,1},{1,2},{2,3},{3,4},{4,5},{5,6},{6,7},{7,0},{8,9},{9,10},{10,1... | collective-permute-start | bytes 393224 | tf_op jit(solution)/shard_map/ppermute | solution.py:409
  146.7 9.1 %collective-permute-start.10 = (bf16[512,128]{1,0:T(8,128)(2,1)S(1)}, bf16[512,128]{1,0:T(8,128)(2,1)S(1)}, u32[]{:S(2)}, u32[]{:S(2)}) collective-permute-start(bf16[512,128]{1,0:T(8,128)(2,1)S(1)} %collective-permute-done.5.refs_4_), channel_id=1, source_target_pairs={{0,7},{1,0},{2,1},{3,2},{4,3},{5,4},{6,5},{7,6},{8,15},{9,8},{10,9... | collective-permute-start | bytes 393224 | tf_op jit(solution)/shard_map/ppermute | solution.py:409

commit v7 on v6

--- a/solution.py
+++ b/solution.py
@@ -452,13 +452,13 @@
     hidden = hidden_copies(place, parts, weights, groups)
     spread_hidden = swap(hidden, "dom", far_groups)
     own, columns = second_mixture(group, hidden, stale_mixed, tile_values, sources, index)
-    before, after = moved(own, "feat", 1), moved(own, "feat", -1)
+    before = moved(own, "feat", 1)
     blocks = pack_second(spread_hidden, columns, near)
-    blocks, before, after = lax.optimization_barrier((blocks, before, after))
+    blocks, before, own = lax.optimization_barrier((blocks, before, own))
     received = swap(blocks, "dom", near_groups).reshape((-1,) + blocks.shape[2:])
-    parts = {0: own, 1: before, -1: after}
-    parts.update({4: moved(before, "feat", 3), 3: moved(before, "feat", 2), -3: moved(after, "feat", -2)})
-    parts.update({2: moved(before, "feat", 1), -2: moved(after, "feat", -1)})
+    parts = {0: own, 1: before}
+    parts.update({4: moved(before, "feat", 3), -3: moved(own, "feat", -3), 3: moved(before, "feat", 2)})
+    parts.update({-2: moved(own, "feat", -2), 2: moved(before, "feat", 1), -1: moved(own, "feat", -1)})
     layer_out = final_rows(place, weights, parts)
     fresh_halo = compact(received, listed, groups)
     return (layer_out, fresh_halo)

time: 167 us -> 167 us (level)
  starting transfers between devices: 76.4 us -> 78.2 us
  waiting for transfers between devices: 38.3 us -> 36.5 us
    all_to_all x4, waiting for transfers between devices: 33.8 us -> 31.9 us  [swap(): lax.all_to_all(blocks, axis, split_axis=0, concat_axis=0, axis_index_grou...]
    ppermute x10, starting transfers between devices: 42.3 us -> 44.1 us  [moved(): return lax.ppermute(rows, axis, [(i, (i + by) % size) for i in range(size)])]
  transfers between devices with their start and end apart: 15 -> 15, of which waited for: 5 -> 6; matrix products, arithmetic and copies ran while one was open for 2% -> 2% of each run, Pallas kernels for 5% -> 5%
where the time goes in v7:
time: 167 us
  starting transfers between devices  78.2 us (47%)
  waiting for transfers between devices  36.5 us (22%)
  blocking collectives  32.3 us (19%)
  Pallas kernels  14.7 us (9%)
  local copies, waits for them, and re-layouts  3.25 us (2%)
    ppermute x10, starting transfers between devices, moved(): return lax.ppermute(rows, axis, [(i, (i + by) % size) for i in range(size)])  44.1 us
    all_to_all x4, starting transfers between devices, swap(): lax.all_to_all(blocks, axis, split_axis=0, concat_axis=0, axis_index_grou...  32.3 us
    all_to_all x4, waiting for transfers between devices, swap(): lax.all_to_all(blocks, axis, split_axis=0, concat_axis=0, axis_index_grou...  31.9 us
    all_gather x1, blocking collectives, slab_columns(): lax.all_gather(both, 'dom', axis=0, tiled=True, axis_index_groups=slabs)  14.3 us
    all_gather x1, blocking collectives, own_columns(): lax.all_gather(both, 'dom', axis=0, tiled=True, axis_index_groups=strides)  14.1 us
    ppermute x10, waiting for transfers between devices, moved(): return lax.ppermute(rows, axis, [(i, (i + by) % size) for i in range(size)])  4.6 us
    all_gather x1, blocking collectives, own_columns(): lax.all_gather(rows, 'dom', axis=0, tiled=True, axis_index_groups=pairs)  3.79 us
    pallas_call x1, Pallas kernels, pack_first(): pl.pallas_call(pack_first_kernel, in_specs=[vmem] * 3, out_specs=[pl.Bloc...  3.37 us
  transfers between devices with their start and end apart: 15, of which 6 were waited for; matrix products, arithmetic and copies ran while one was open for 2% of the time, Pallas kernels for 5%

profile of v7, /device:TPU:7, one launch (start us, length us, event | category | flops | bytes accessed | tf_op | source)
XLA Modules:
  0.0 166.6 jit_solution(1904521335707309878)
XLA Ops:
  0.6 3.4 %pack_first.1 = (bf16[64,128,128]{2,1,0:T(8,128)(2,1)}, bf16[4,32,128]{2,1,0:T(8,128)(2,1)}) custom-call(bf16[512,128]{1,0:T(8,128)(2,1)} %first_ref.1, s32[64,128]{1,0:T(8,128)} %bitcast.37, s32[1,64]{1,0:T(1,128)} %counts_ref.1), custom_call_target="tpu_custom_call" | custom-call | flops 1073741824 | bytes 3145728 | tf_op jit(solution)/shard_map/pack_first/pallas_call | solution.py:107
  4.1 14.3 %all-to-all-start = ((bf16[64,128,128]{2,1,0:T(8,128)(2,1)}), bf16[64,128,128]{2,1,0:T(8,128)(2,1)S(1)}, u32[]{:S(2)}, u32[]{:S(2)}) async-start(bf16[64,128,128]{2,1,0:T(8,128)(2,1)} %get-tuple-element.23), calls=%async_computation | async-start | bytes 4194304 | tf_op jit(solution)/shard_map/all_to_all | solution.py:404
  19.0 1.9 %collective-permute-start = (bf16[32,128]{1,0:T(8,128)(2,1)}, bf16[32,128]{1,0:T(8,128)(2,1)}, u32[]{:S(2)}, u32[]{:S(2)}) collective-permute-start(bf16[32,128]{1,0:T(8,128)(2,1)} %pad_maximum_fusion), channel_id=1, source_target_pairs={{0,0},{1,64},{2,128},{3,192},{4,256},{5,320},{6,384},{7,448},{8,8}... | collective-permute-start | bytes 24584 | tf_op jit(solution)/shard_map/ppermute | solution.py:389
  22.3 6.3 %collective-permute-start.1 = (bf16[32,128]{1,0:T(8,128)(2,1)}, bf16[32,128]{1,0:T(8,128)(2,1)}, u32[]{:S(2)}, u32[]{:S(2)}) collective-permute-start(bf16[32,128]{1,0:T(8,128)(2,1)} %get-tuple-element.42), channel_id=1, source_target_pairs={{0,128},{8,136},{16,144},{24,152},{32,160},{40,168},{48,176},{56,1... | collective-permute-start | bytes 24584 | tf_op jit(solution)/shard_map/ppermute | solution.py:409
  28.6 8.2 %collective-permute-start.2 = (bf16[32,128]{1,0:T(8,128)(2,1)}, bf16[32,128]{1,0:T(8,128)(2,1)}, u32[]{:S(2)}, u32[]{:S(2)}) collective-permute-start(bf16[32,128]{1,0:T(8,128)(2,1)} %get-tuple-element.41), channel_id=1, source_target_pairs={{0,256},{8,264},{16,272},{24,280},{32,288},{40,296},{48,304},{56,3... | collective-permute-start | bytes 24584 | tf_op jit(solution)/shard_map/ppermute | solution.py:409
  36.8 5.5 %collective-permute-start.3 = (bf16[32,128]{1,0:T(8,128)(2,1)}, bf16[32,128]{1,0:T(8,128)(2,1)}, u32[]{:S(2)}, u32[]{:S(2)}) collective-permute-start(bf16[32,128]{1,0:T(8,128)(2,1)} %get-tuple-element.40), channel_id=1, source_target_pairs={{0,384},{8,392},{16,400},{24,408},{32,416},{40,424},{48,432},{56,4... | collective-permute-start | bytes 24584 | tf_op jit(solution)/shard_map/ppermute | solution.py:409
  45.2 14.3 %all_gather.9 = bf16[256,128]{1,0:T(8,128)(2,1)S(1)} all-gather(bf16[32,128]{1,0:T(8,128)(2,1)} %collective-permute-done), channel_id=1, replica_groups={{0,8,16,24,32,40,48,56},{64,72,80,88,96,104,112,120},{128,136,144,152,1..., dimensions={0}, use_global_device_ids=true | all-gather | bytes 73728 | tf_op jit(solution)/shard_map/all_gather | solution.py:391
  60.2 8.3 %all-to-all-done.halo_ref = bf16[64,128,128]{2,1,0:T(8,128)(2,1)S(1)} async-done(((bf16[64,128,128]{2,1,0:T(8,128)(2,1)}), bf16[64,128,128]{2,1,0:T(8,128)(2,1)S(1)}, u32[]{:S(2)}, u32[]{:S(2)}) %all-to-all-start) | async-done | bytes 2097184 | tf_op jit(solution)/shard_map/all_to_all | solution.py:404
  68.5 2.0 %first_mixture.1 = bf16[8,512,128]{2,1,0:T(8,128)(2,1)} custom-call(bf16[512,128]{1,0:T(8,128)(2,1)S(1)} %copy-done.2, bf16[64,128,128]{2,1,0:T(8,128)(2,1)S(1)} %all-to-all-done.halo_ref, bf16[4,10,128,128]{3,2,1,0:T(8,128)(2,1)S(1)} %copy-done, s32[4,10]{1,0:T(4,128)S(1)} %bitcast.28, s32[32]{0:T(128)S(1)} %bitcast.30), custom_call_target="tpu_custom_call" | custom-call | flops 170000000 | bytes 5242880 | tf_op jit(solution)/shard_map/first_mixture/pallas_call | solution.py:210
  70.5 8.7 %all-to-all-start.1 = ((bf16[8,512,128]{2,1,0:T(8,128)(2,1)}), bf16[8,512,128]{2,1,0:T(8,128)(2,1)S(1)}, u32[]{:S(2)}, u32[]{:S(2)}) async-start(bf16[8,512,128]{2,1,0:T(8,128)(2,1)} %first_mixture.1), calls=%async_computation.1 | async-start | bytes 2097152 | tf_op jit(solution)/shard_map/all_to_all | solution.py:404
  79.2 3.8 %all_gather.10 = bf16[512,128]{1,0:T(8,128)(2,1)S(1)} all-gather(bf16[256,128]{1,0:T(8,128)(2,1)S(1)} %bitcast.33), channel_id=1, replica_groups={{0,64},{8,72},{16,80},{24,88},{32,96},{40,104},{48,112},{56,120},{128,1..., dimensions={0}, use_global_device_ids=true | all-gather | bytes 196608 | tf_op jit(solution)/shard_map/all_gather | solution.py:398
  83.0 14.1 %all_gather.11 = bf16[2048,128]{1,0:T(8,128)(2,1)S(1)} all-gather(bf16[512,128]{1,0:T(8,128)(2,1)S(1)} %all_gather.10), channel_id=1, replica_groups={{0,128,256,384},{8,136,264,392},{16,144,272,400},{24,152,280,408},{32,1..., dimensions={0}, use_global_device_ids=true | all-gather | bytes 655360 | tf_op jit(solution)/shard_map/all_gather | solution.py:399
  97.1 11.3 %all-to-all-done.1.parts_ref = bf16[8,512,128]{2,1,0:T(8,128)(2,1)S(1)} async-done(((bf16[8,512,128]{2,1,0:T(8,128)(2,1)}), bf16[8,512,128]{2,1,0:T(8,128)(2,1)S(1)}, u32[]{:S(2)}, u32[]{:S(2)}) %all-to-all-start.1) | async-done | bytes 1048608 | tf_op jit(solution)/shard_map/all_to_all | solution.py:404
  109.7 3.5 %all-to-all-start.2 = ((bf16[4,512,128]{2,1,0:T(8,128)(2,1)}), bf16[4,512,128]{2,1,0:T(8,128)(2,1)S(1)}, u32[]{:S(2)}, u32[]{:S(2)}) async-start(bf16[4,512,128]{2,1,0:T(8,128)(2,1)} %hidden.1.hidden_ref), calls=%async_computation.2 | async-start | bytes 1048576 | tf_op jit(solution)/shard_map/all_to_all | solution.py:404
  114.5 1.9 %collective-permute-start.4 = (bf16[512,128]{1,0:T(8,128)(2,1)S(1)}, bf16[512,128]{1,0:T(8,128)(2,1)S(1)}, u32[]{:S(2)}, u32[]{:S(2)}) collective-permute-start(bf16[512,128]{1,0:T(8,128)(2,1)S(1)} %get-tuple-element.37.refs_2_), channel_id=1, source_target_pairs={{0,1},{1,2},{2,3},{3,4},{4,5},{5,6},{6,7},{7,0},{8,9},{9,10},{10,1... | collective-permute-start | bytes 393224 | tf_op jit(solution)/shard_map/ppermute | solution.py:409
  116.4 11.0 %all-to-all-done.2.rows_ref = bf16[4,512,128]{2,1,0:T(8,128)(2,1)S(1)} async-done(((bf16[4,512,128]{2,1,0:T(8,128)(2,1)}), bf16[4,512,128]{2,1,0:T(8,128)(2,1)S(1)}, u32[]{:S(2)}, u32[]{:S(2)}) %all-to-all-start.2) | async-done | bytes 524320 | tf_op jit(solution)/shard_map/all_to_all | solution.py:404
  127.5 2.2 %pack_second.1 = bf16[16,4,128,128]{3,2,1,0:T(8,128)(2,1)} custom-call(bf16[4,512,128]{2,1,0:T(8,128)(2,1)S(1)} %all-to-all-done.2.rows_ref, bf16[2,128,128]{2,1,0:T(8,128)(2,1)S(1)} %get-tuple-element.35.columns_ref), custom_call_target="tpu_custom_call" | custom-call | flops 1073741824 | bytes 3145728 | tf_op jit(solution)/shard_map/pack_second/pallas_call | solution.py:144
  129.7 5.8 %all-to-all-start.3 = ((bf16[16,4,128,128]{3,2,1,0:T(8,128)(2,1)}), bf16[16,4,128,128]{3,2,1,0:T(8,128)(2,1)S(1)}, u32[]{:S(2)}, u32[]{:S(2)}) async-start(bf16[16,4,128,128]{3,2,1,0:T(8,128)(2,1)} %pack_second.1), calls=%async_computation.3 | async-start | bytes 4194304 | tf_op jit(solution)/shard_map/all_to_all | solution.py:404
  137.4 2.5 %collective-permute-start.7 = (bf16[512,128]{1,0:T(8,128)(2,1)S(1)}, bf16[512,128]{1,0:T(8,128)(2,1)S(1)}, u32[]{:S(2)}, u32[]{:S(2)}) collective-permute-start(bf16[512,128]{1,0:T(8,128)(2,1)S(1)} %collective-permute-done.4.refs_3_), channel_id=1, source_target_pairs={{0,2},{1,3},{2,4},{3,5},{4,6},{5,7},{6,0},{7,1},{8,10},{9,11},{10,... | collective-permute-start | bytes 393224 | tf_op jit(solution)/shard_map/ppermute | solution.py:409
  139.9 5.8 %collective-permute-start.6 = (bf16[512,128]{1,0:T(8,128)(2,1)S(1)}, bf16[512,128]{1,0:T(8,128)(2,1)S(1)}, u32[]{:S(2)}, u32[]{:S(2)}) collective-permute-start(bf16[512,128]{1,0:T(8,128)(2,1)S(1)} %get-tuple-element.37.refs_2_), channel_id=1, source_target_pairs={{0,5},{1,6},{2,7},{3,0},{4,1},{5,2},{6,3},{7,4},{8,13},{9,14},{10,... | collective-permute-start | bytes 393224 | tf_op jit(solution)/shard_map/ppermute | solution.py:409
  145.7 5.5 %collective-permute-start.8 = (bf16[512,128]{1,0:T(8,128)(2,1)S(1)}, bf16[512,128]{1,0:T(8,128)(2,1)S(1)}, u32[]{:S(2)}, u32[]{:S(2)}) collective-permute-start(bf16[512,128]{1,0:T(8,128)(2,1)S(1)} %get-tuple-element.37.refs_2_), channel_id=1, source_target_pairs={{0,6},{1,7},{2,0},{3,1},{4,2},{5,3},{6,4},{7,5},{8,14},{9,15},{10,... | collective-permute-start | bytes 393224 | tf_op jit(solution)/shard_map/ppermute | solution.py:409
  151.2 1.9 %collective-permute-start.9 = (bf16[512,128]{1,0:T(8,128)(2,1)S(1)}, bf16[512,128]{1,0:T(8,128)(2,1)S(1)}, u32[]{:S(2)}, u32[]{:S(2)}) collective-permute-start(bf16[512,128]{1,0:T(8,128)(2,1)S(1)} %collective-permute-done.4.refs_3_), channel_id=1, source_target_pairs={{0,1},{1,2},{2,3},{3,4},{4,5},{5,6},{6,7},{7,0},{8,9},{9,10},{10,1... | collective-permute-start | bytes 393224 | tf_op jit(solution)/shard_map/ppermute | solution.py:409
  153.1 4.6 %collective-permute-start.10 = (bf16[512,128]{1,0:T(8,128)(2,1)S(1)}, bf16[512,128]{1,0:T(8,128)(2,1)S(1)}, u32[]{:S(2)}, u32[]{:S(2)}) collective-permute-start(bf16[512,128]{1,0:T(8,128)(2,1)S(1)} %get-tuple-element.37.refs_2_), channel_id=1, source_target_pairs={{0,7},{1,0},{2,1},{3,2},{4,3},{5,4},{6,5},{7,6},{8,15},{9,8},{10,9... | collective-permute-start | bytes 393224 | tf_op jit(solution)/shard_map/ppermute | solution.py:409
  157.7 3.8 %collective-permute-done.8.refs_7_ = bf16[512,128]{1,0:T(8,128)(2,1)S(1)} collective-permute-done((bf16[512,128]{1,0:T(8,128)(2,1)S(1)}, bf16[512,128]{1,0:T(8,128)(2,1)S(1)}, u32[]{:S(2)}, u32[]{:S(2)}) %collective-permute-start.8) | collective-permute-done | bytes 131104 | tf_op jit(solution)/shard_map/ppermute | solution.py:409
  (36 shorter events, 15.1 us)
Async XLA Ops:
  4.0 14.4 %copy-start.6 = (bf16[128,16]{0,1:T(8,128)(2,1)S(1)}, bf16[128,16]{0,1:T(8,128)(2,1)}, u32[]{:S(2)}) copy-start(bf16[128,16]{0,1:T(8,128)(2,1)} %param.11) | copy-start | bytes 12292
  4.0 14.3 %copy-start.7 = (bf16[128,16]{0,1:T(8,128)(2,1)S(1)}, bf16[128,16]{0,1:T(8,128)(2,1)}, u32[]{:S(2)}) copy-start(bf16[128,16]{0,1:T(8,128)(2,1)} %param.10) | copy-start | bytes 12292
  4.0 38.2 %copy-start = (bf16[4,10,128,128]{3,2,1,0:T(8,128)(2,1)S(1)}, bf16[4,10,128,128]{3,2,1,0:T(8,128)(2,1)}, u32[]{:S(2)}) copy-start(bf16[4,10,128,128]{3,2,1,0:T(8,128)(2,1)} %tiles_ref.5) | copy-start | bytes 3932164
  4.0 38.2 %copy-start.2 = (bf16[512,128]{1,0:T(8,128)(2,1)S(1)}, bf16[512,128]{1,0:T(8,128)(2,1)}, u32[]{:S(2)}) copy-start(bf16[512,128]{1,0:T(8,128)(2,1)} %first_ref.1) | copy-start | bytes 393220
  4.1 38.2 %copy-start.3 = (s32[1,4,10]{2,1,0:T(4,128)S(1)}, s32[1,4,10]{2,1,0:T(4,128)}, u32[]{:S(2)}) copy-start(s32[1,4,10]{2,1,0:T(4,128)} %param.13) | copy-start | bytes 484
  4.1 64.4 %all-to-all-start = ((bf16[64,128,128]{2,1,0:T(8,128)(2,1)}), bf16[64,128,128]{2,1,0:T(8,128)(2,1)S(1)}, u32[]{:S(2)}, u32[]{:S(2)}) async-start(bf16[64,128,128]{2,1,0:T(8,128)(2,1)} %get-tuple-element.23), calls=%async_computation | async-start | bytes 4194304 | tf_op jit(solution)/shard_map/all_to_all | solution.py:404
  18.3 50.1 %copy-start.4 = (s32[1,32]{1,0:T(1,128)S(1)}, s32[1,32]{1,0:T(1,128)}, u32[]{:S(2)}) copy-start(s32[1,32]{1,0:T(1,128)} %param.14) | copy-start | bytes 388
  19.0 26.2 %collective-permute-start = (bf16[32,128]{1,0:T(8,128)(2,1)}, bf16[32,128]{1,0:T(8,128)(2,1)}, u32[]{:S(2)}, u32[]{:S(2)}) collective-permute-start(bf16[32,128]{1,0:T(8,128)(2,1)} %pad_maximum_fusion), channel_id=1, source_target_pairs={{0,0},{1,64},{2,128},{3,192},{4,256},{5,320},{6,384},{7,448},{8,8}... | collective-permute-start | bytes 24584 | tf_op jit(solution)/shard_map/ppermute | solution.py:389
  22.3 48.2 %collective-permute-start.1 = (bf16[32,128]{1,0:T(8,128)(2,1)}, bf16[32,128]{1,0:T(8,128)(2,1)}, u32[]{:S(2)}, u32[]{:S(2)}) collective-permute-start(bf16[32,128]{1,0:T(8,128)(2,1)} %get-tuple-element.42), channel_id=1, source_target_pairs={{0,128},{8,136},{16,144},{24,152},{32,160},{40,168},{48,176},{56,1... | collective-permute-start | bytes 24584 | tf_op jit(solution)/shard_map/ppermute | solution.py:409
  28.6 41.9 %collective-permute-start.2 = (bf16[32,128]{1,0:T(8,128)(2,1)}, bf16[32,128]{1,0:T(8,128)(2,1)}, u32[]{:S(2)}, u32[]{:S(2)}) collective-permute-start(bf16[32,128]{1,0:T(8,128)(2,1)} %get-tuple-element.41), channel_id=1, source_target_pairs={{0,256},{8,264},{16,272},{24,280},{32,288},{40,296},{48,304},{56,3... | collective-permute-start | bytes 24584 | tf_op jit(solution)/shard_map/ppermute | solution.py:409
  36.8 33.7 %collective-permute-start.3 = (bf16[32,128]{1,0:T(8,128)(2,1)}, bf16[32,128]{1,0:T(8,128)(2,1)}, u32[]{:S(2)}, u32[]{:S(2)}) collective-permute-start(bf16[32,128]{1,0:T(8,128)(2,1)} %get-tuple-element.40), channel_id=1, source_target_pairs={{0,384},{8,392},{16,400},{24,408},{32,416},{40,424},{48,432},{56,4... | collective-permute-start | bytes 24584 | tf_op jit(solution)/shard_map/ppermute | solution.py:409
  42.3 1.2 copy-start.1
  70.5 8.7 %copy-start.5 = (bf16[2,8,16,128]{3,2,1,0:T(8,128)(2,1)S(1)}, bf16[2,8,16,128]{3,2,1,0:T(8,128)(2,1)}, u32[]{:S(2)}) copy-start(bf16[2,8,16,128]{3,2,1,0:T(8,128)(2,1)} %copy.11) | copy-start | bytes 196612
  70.5 37.9 %all-to-all-start.1 = ((bf16[8,512,128]{2,1,0:T(8,128)(2,1)}), bf16[8,512,128]{2,1,0:T(8,128)(2,1)S(1)}, u32[]{:S(2)}, u32[]{:S(2)}) async-start(bf16[8,512,128]{2,1,0:T(8,128)(2,1)} %first_mixture.1), calls=%async_computation.1 | async-start | bytes 2097152 | tf_op jit(solution)/shard_map/all_to_all | solution.py:404
  109.7 17.8 %all-to-all-start.2 = ((bf16[4,512,128]{2,1,0:T(8,128)(2,1)}), bf16[4,512,128]{2,1,0:T(8,128)(2,1)S(1)}, u32[]{:S(2)}, u32[]{:S(2)}) async-start(bf16[4,512,128]{2,1,0:T(8,128)(2,1)} %hidden.1.hidden_ref), calls=%async_computation.2 | async-start | bytes 1048576 | tf_op jit(solution)/shard_map/all_to_all | solution.py:404
  114.5 15.1 %collective-permute-start.4 = (bf16[512,128]{1,0:T(8,128)(2,1)S(1)}, bf16[512,128]{1,0:T(8,128)(2,1)S(1)}, u32[]{:S(2)}, u32[]{:S(2)}) collective-permute-start(bf16[512,128]{1,0:T(8,128)(2,1)S(1)} %get-tuple-element.37.refs_2_), channel_id=1, source_target_pairs={{0,1},{1,2},{2,3},{3,4},{4,5},{5,6},{6,7},{7,0},{8,9},{9,10},{10,1... | collective-permute-start | bytes 393224 | tf_op jit(solution)/shard_map/ppermute | solution.py:409
  129.7 35.1 %all-to-all-start.3 = ((bf16[16,4,128,128]{3,2,1,0:T(8,128)(2,1)}), bf16[16,4,128,128]{3,2,1,0:T(8,128)(2,1)S(1)}, u32[]{:S(2)}, u32[]{:S(2)}) async-start(bf16[16,4,128,128]{3,2,1,0:T(8,128)(2,1)} %pack_second.1), calls=%async_computation.3 | async-start | bytes 4194304 | tf_op jit(solution)/shard_map/all_to_all | solution.py:404
  135.5 17.6 %collective-permute-start.5 = (bf16[512,128]{1,0:T(8,128)(2,1)S(1)}, bf16[512,128]{1,0:T(8,128)(2,1)S(1)}, u32[]{:S(2)}, u32[]{:S(2)}) collective-permute-start(bf16[512,128]{1,0:T(8,128)(2,1)S(1)} %collective-permute-done.4.refs_3_), channel_id=1, source_target_pairs={{0,3},{1,4},{2,5},{3,6},{4,7},{5,0},{6,1},{7,2},{8,11},{9,12},{10,... | collective-permute-start | bytes 393224 | tf_op jit(solution)/shard_map/ppermute | solution.py:409
  137.4 20.3 %collective-permute-start.7 = (bf16[512,128]{1,0:T(8,128)(2,1)S(1)}, bf16[512,128]{1,0:T(8,128)(2,1)S(1)}, u32[]{:S(2)}, u32[]{:S(2)}) collective-permute-start(bf16[512,128]{1,0:T(8,128)(2,1)S(1)} %collective-permute-done.4.refs_3_), channel_id=1, source_target_pairs={{0,2},{1,3},{2,4},{3,5},{4,6},{5,7},{6,0},{7,1},{8,10},{9,11},{10,... | collective-permute-start | bytes 393224 | tf_op jit(solution)/shard_map/ppermute | solution.py:409
  139.9 17.8 %collective-permute-start.6 = (bf16[512,128]{1,0:T(8,128)(2,1)S(1)}, bf16[512,128]{1,0:T(8,128)(2,1)S(1)}, u32[]{:S(2)}, u32[]{:S(2)}) collective-permute-start(bf16[512,128]{1,0:T(8,128)(2,1)S(1)} %get-tuple-element.37.refs_2_), channel_id=1, source_target_pairs={{0,5},{1,6},{2,7},{3,0},{4,1},{5,2},{6,3},{7,4},{8,13},{9,14},{10,... | collective-permute-start | bytes 393224 | tf_op jit(solution)/shard_map/ppermute | solution.py:409
  145.7 15.9 %collective-permute-start.8 = (bf16[512,128]{1,0:T(8,128)(2,1)S(1)}, bf16[512,128]{1,0:T(8,128)(2,1)S(1)}, u32[]{:S(2)}, u32[]{:S(2)}) collective-permute-start(bf16[512,128]{1,0:T(8,128)(2,1)S(1)} %get-tuple-element.37.refs_2_), channel_id=1, source_target_pairs={{0,6},{1,7},{2,0},{3,1},{4,2},{5,3},{6,4},{7,5},{8,14},{9,15},{10,... | collective-permute-start | bytes 393224 | tf_op jit(solution)/shard_map/ppermute | solution.py:409
  151.2 10.4 %collective-permute-start.9 = (bf16[512,128]{1,0:T(8,128)(2,1)S(1)}, bf16[512,128]{1,0:T(8,128)(2,1)S(1)}, u32[]{:S(2)}, u32[]{:S(2)}) collective-permute-start(bf16[512,128]{1,0:T(8,128)(2,1)S(1)} %collective-permute-done.4.refs_3_), channel_id=1, source_target_pairs={{0,1},{1,2},{2,3},{3,4},{4,5},{5,6},{6,7},{7,0},{8,9},{9,10},{10,1... | collective-permute-start | bytes 393224 | tf_op jit(solution)/shard_map/ppermute | solution.py:409
  153.1 9.2 %collective-permute-start.10 = (bf16[512,128]{1,0:T(8,128)(2,1)S(1)}, bf16[512,128]{1,0:T(8,128)(2,1)S(1)}, u32[]{:S(2)}, u32[]{:S(2)}) collective-permute-start(bf16[512,128]{1,0:T(8,128)(2,1)S(1)} %get-tuple-element.37.refs_2_), channel_id=1, source_target_pairs={{0,7},{1,0},{2,1},{3,2},{4,3},{5,4},{6,5},{7,6},{8,15},{9,8},{10,9... | collective-permute-start | bytes 393224 | tf_op jit(solution)/shard_map/ppermute | solution.py:409
